TPU v7x, 256 devices: a whole 4x4x8 slice. The times are simulated.
256 devices in a mesh: dp: 32 (over x, y, core), tensor: 8 (over z).
Axes of the slice: x: 4, y: 4, z: 8, core: 2. Of those that a mesh axis runs over, the one named last changes fastest.
Arguments:
- activations: bfloat16 [32768, 8192], P(('dp', 'tensor')), may hold values from -24 to 24
- out_grads: bfloat16 [32768, 2048], P('dp', 'tensor'), may hold values from -0.059814453 to 0.059814453
- master: float32 [8192, 2048], P('dp', 'tensor'), may hold values from -3 to 3
- first_moment: float32 [8192, 2048], P('dp', 'tensor'), may hold values from -2 to 2
- second_moment: float32 [8192, 2048], P('dp', 'tensor'), may hold values from 0.01 to 1
Outputs:
- new_master: float32 [8192, 2048], P('dp', 'tensor')
- new_first: float32 [8192, 2048], P('dp', 'tensor')
- new_second: float32 [8192, 2048], P('dp', 'tensor')
- weights: bfloat16 [8192, 2048], P(None, 'tensor')
All inputs are finite; a program needn't handle non-finite values.
Results may differ from a plain program's by a relative error of at most 0.013.
Values may be sent and summed in bfloat16 or wider, within the bound.
No kernel may reach another device: no remote copies, remote signals or barrier semaphores. Data moves between devices by JAX's collectives and lax.ppermute only.
A program may use at most 128 MiB of HBM per device.

v0:
```python
import jax
import jax.numpy as jnp
from jax import lax
from jax.sharding import PartitionSpec as P

first_bias = 0.9999734386011124
second_bias = 0.0952078528862911


def contract_tokens(left, right):
    return lax.dot_general(
        left, right, (((0,), (0,)), ((), ())), preferred_element_type=jnp.float32
    )


def per_device(activations, out_grads, master, first_moment, second_moment):
    replica_rows = lax.all_gather(activations, "tensor", axis=0, tiled=True)
    grad = lax.psum_scatter(
        contract_tokens(replica_rows, out_grads).astype(jnp.bfloat16),
        "dp",
        scatter_dimension=0,
        tiled=True,
    ).astype(jnp.float32)
    new_first = 0.9 * first_moment + 0.1 * grad
    new_second = 0.999 * second_moment + 0.001 * grad * grad
    first_fix = new_first / first_bias
    second_fix = new_second / second_bias
    new_master = master * (1.0 - 0.05 * 0.1) - 0.05 * first_fix / (jnp.sqrt(second_fix) + 1e-08)
    weights = lax.all_gather(new_master.astype(jnp.bfloat16), "dp", axis=0, tiled=True)
    return (new_master, new_first, new_second, weights)


def solution(mesh):
    return jax.shard_map(
        per_device,
        mesh=mesh,
        in_specs=(
            P(("dp", "tensor"), None),
            P("dp", "tensor"),
            P("dp", "tensor"),
            P("dp", "tensor"),
            P("dp", "tensor"),
        ),
        out_specs=(P("dp", "tensor"), P("dp", "tensor"), P("dp", "tensor"), P(None, "tensor")),
        check_vma=False,
    )
```

profile of v0, /device:TPU:1, one launch (start us, length us, event | category | flops | bytes accessed | tf_op | source)
XLA Modules:
  0.0 352.7 jit_solution(3168861249399175387)
XLA Ops:
  7.2 0.0 copy-start
  7.2 0.0 all-gather.3.cloned.1.call-start
  7.2 0.7 all-gather.3.cloned.1.call-update
  7.9 0.0 copy-start.1
  7.9 0.0 copy-start.2
  7.9 0.0 copy-start.3
  7.9 0.0 reduce-scatter.2.cloned.1.call-start
  8.0 178.4 %all-gather.3.cloned.1.call-done = bf16[1024,8192]{1,0:T(8,128)(2,1)} async-done(((bf16[128,8192]{1,0:T(8,128)(2,1)}), bf16[1024,8192]{1,0:T(8,128)(2,1)}) %all-gather.3.cloned.1.call-update) | async-done | bytes 16777232 | tf_op jit(solution)/shard_map/all_gather | solution.py:17
  186.4 0.0 copy-done
  186.4 12.6 %convolution_convert_fusion = bf16[8192,256]{1,0:T(8,128)(2,1)} fusion(bf16[1024,8192]{1,0:T(8,128)(2,1)} %all-gather.3.cloned.1.call-done, bf16[1024,256]{1,0:T(8,128)(2,1)S(1)} %copy-done), kind=kOutput, calls=%fused_computation | convolution fusion | flops 4297064448 | bytes 21495808 | tf_op jit(solution)/shard_map/dot_general | solution.py:11
  199.0 0.0 reduce-scatter.2.cloned.1.call-update
  199.0 0.0 all-gather.5.cloned.1.call-start
  199.1 86.6 %reduce-scatter.2.cloned.1.call-done = bf16[256,256]{1,0:T(8,128)(2,1)} async-done(((bf16[8192,256]{1,0:T(8,128)(2,1)}), bf16[256,256]{1,0:T(8,128)(2,1)}) %reduce-scatter.2.cloned.1.call-update) | async-done | bytes 131088 | tf_op jit(solution)/shard_map/reduce_scatter | solution.py:18
  285.7 0.0 copy-done.1
  285.7 0.0 copy-done.2
  285.7 0.0 copy-done.3
  285.7 1.9 fusion.2
  287.6 0.0 all-gather.5.cloned.1.call-update
  287.7 54.1 %all-gather.5.cloned.1.call-done = bf16[8192,256]{1,0:T(8,128)(2,1)} async-done(((bf16[256,256]{1,0:T(8,128)(2,1)}), bf16[8192,256]{1,0:T(8,128)(2,1)}) %all-gather.5.cloned.1.call-update) | async-done | bytes 4194320 | tf_op jit(solution)/shard_map/all_gather | solution.py:29
  341.7 4.5 %copy.10 = bf16[8192,256]{1,0:T(8,128)(2,1)} copy(bf16[8192,256]{1,0:T(8,128)(2,1)} %all-gather.5.cloned.1.call-done) | data formatting | bytes 8388608
Async XLA Ops:
  7.2 179.2 %copy-start = (bf16[1024,256]{1,0:T(8,128)(2,1)S(1)}, bf16[1024,256]{1,0:T(8,128)(2,1)}, u32[]{:S(2)}) copy-start(bf16[1024,256]{1,0:T(8,128)(2,1)} %param.6) | copy-start | bytes 1572868
  7.2 179.2 %all-gather.3.cloned.1.call-start = ((), (), s32[]{:S(2)}) async-start(), calls=%async_computation.1 | async-start | bytes 18874368 | tf_op jit(solution)/shard_map/all_gather | solution.py:17
  7.9 277.8 %copy-start.1 = (f32[256,256]{1,0:T(8,128)S(1)}, f32[256,256]{1,0:T(8,128)}, u32[]{:S(2)}) copy-start(f32[256,256]{1,0:T(8,128)} %param.7) | copy-start | bytes 786436
  7.9 277.8 %copy-start.2 = (f32[256,256]{1,0:T(8,128)S(1)}, f32[256,256]{1,0:T(8,128)}, u32[]{:S(2)}) copy-start(f32[256,256]{1,0:T(8,128)} %param.8) | copy-start | bytes 786436
  7.9 277.8 %copy-start.3 = (f32[256,256]{1,0:T(8,128)S(1)}, f32[256,256]{1,0:T(8,128)}, u32[]{:S(2)}) copy-start(f32[256,256]{1,0:T(8,128)} %param.9) | copy-start | bytes 786436
  7.9 277.8 %reduce-scatter.2.cloned.1.call-start = ((), (), s32[]{:S(2)}) async-start(), calls=%async_computation.2 | async-start | bytes 4325376 | tf_op jit(solution)/shard_map/reduce_scatter | solution.py:18
  199.0 142.7 %all-gather.5.cloned.1.call-start = ((), (), s32[]{:S(2)}) async-start(), calls=%async_computation.3 | async-start | bytes 4325376 | tf_op jit(solution)/shard_map/all_gather | solution.py:29
Sparse Core Ops, SparseCore 0:
  9.8 176.5 all-gather.2
  199.1 86.5 reduce-scatter.1
  289.2 52.5 all-gather.4
where the time goes:
time: 353 us
  waiting for transfers between devices  320 us (91%)
  between operations  13.8 us (4%)
  matrix products  12.6 us (4%)
  local copies, waits for them, and re-layouts  4.49 us (1%)
    all_gather x1, waiting for transfers between devices, per_device(): replica_rows = lax.all_gather(activations, 'tensor', axis=0, tiled=True)  178 us
    reduce_scatter x1, waiting for transfers between devices, per_device(): lax.psum_scatter(contract_tokens(replica_rows, out_grads).astype(jnp.bflo...  86.6 us
    all_gather x1, waiting for transfers between devices, per_device(): lax.all_gather(new_master.astype(jnp.bfloat16), 'dp', axis=0, tiled=True)  54.1 us
    dot_general x1, matrix products, contract_tokens(): lax.dot_general(left, right, (((0,), (0,)), ((), ())), preferred_element_...  12.6 us
  transfers between devices with their start and end apart: 3, of which 3 were waited for; matrix products, arithmetic and copies ran while one was open for 0% of the time, Pallas kernels for 0%

commit v1 on v0

v1 whole, which is shorter than its diff:
```python
import functools

import jax
import jax.numpy as jnp
from jax import lax
from jax.experimental import pallas as pl
from jax.experimental.pallas import tpu as pltpu
from jax.sharding import PartitionSpec as P

first_bias = 0.9999734386011124
second_bias = 0.0952078528862911

SIDE = 4


def device_at(x, y, core):
    return ((x % SIDE) * SIDE + (y % SIDE)) * 2 + core


PLACES = [(x, y, core) for x in range(SIDE) for y in range(SIDE) for core in range(2)]
CORE_SWAP = [(device_at(x, y, core), device_at(x, y, 1 - core)) for x, y, core in PLACES]


def ring(step, along_x_on):
    return [
        (
            device_at(x, y, core),
            device_at(x + step, y, core) if core == along_x_on else device_at(x, y + step, core),
        )
        for x, y, core in PLACES
    ]


def groups(along_x_on):
    lines = []
    for at in range(SIDE):
        lines.append([device_at(i, at, along_x_on) for i in range(SIDE)])
        lines.append([device_at(at, i, 1 - along_x_on) for i in range(SIDE)])
    return lines


def place():
    dp = lax.axis_index("dp")
    return dp // (2 * SIDE), (dp // 2) % SIDE, dp % 2


def block_of(x, y, core, split, reduce):
    first = core == 0
    bx = lax.rem(x + jnp.where(first, split, reduce), SIDE)
    by = lax.rem(y + jnp.where(first, reduce, split), SIDE)
    return (bx * SIDE + by) * 2 + core


def run_copies(copies):
    for copy in copies:
        copy.start()
    for copy in copies:
        copy.wait()


def for_peer_kernel(rows, acts, out, sem):
    x, y, core = place()
    copies = []
    for split in range(SIDE):
        for reduce in range(SIDE):
            block = block_of(x, y, 1 - core, split, reduce)
            copies.append(
                pltpu.make_async_copy(
                    acts.at[:, pl.ds(pl.multiple_of(block * rows, rows), rows)],
                    out.at[split, :, pl.ds(reduce * rows, rows)],
                    sem.at[split * SIDE + reduce],
                )
            )
    run_copies(copies)


def chunks_kernel(rows, acts, peer, *rest):
    outs, sem = rest[:SIDE], rest[SIDE]
    x, y, core = place()
    copies = []
    for split in range(SIDE):
        for reduce in range(SIDE):
            block = block_of(x, y, core, split, reduce)
            copies.append(
                pltpu.make_async_copy(
                    acts.at[:, pl.ds(pl.multiple_of(block * rows, rows), rows)],
                    outs[split].at[0, :, pl.ds(reduce * rows, rows)],
                    sem.at[split * SIDE + reduce],
                )
            )
        copies.append(
            pltpu.make_async_copy(peer.at[split], outs[split].at[1], sem.at[SIDE * SIDE + split])
        )
    run_copies(copies)


def product_kernel(rows, a0, a1, a2, a3, g0, g1, g2, g3, out, turned):
    tokens = a0.shape[1]

    @pl.when(pl.program_id(0) == 0)
    def _():
        for i, piece in enumerate((a0, a1, a2, a3)):
            for core in range(2):
                at = (2 * i + core) * tokens
                turned[:, at : at + tokens] = piece[core].T

    right = jnp.concatenate([piece[core, 0] for piece in (g0, g1, g2, g3) for core in range(2)], axis=0)
    for reduce in range(SIDE):
        out[reduce, 0] = jnp.dot(
            turned[reduce * rows : (reduce + 1) * rows, :], right, preferred_element_type=jnp.float32
        ).astype(out.dtype)


def weights_kernel(rows, own, peer, out, sem):
    _, _, core = place()
    copies = []
    for which, (array, of_core) in enumerate(((own, core), (peer, 1 - core))):
        for i in range(SIDE):
            for j in range(SIDE):
                block = jnp.where(of_core == 0, j * SIDE + i, i * SIDE + j) * 2 + of_core
                copies.append(
                    pltpu.make_async_copy(
                        array.at[i, j],
                        out.at[pl.ds(pl.multiple_of(block * rows, rows), rows), :],
                        sem.at[(which * SIDE + i) * SIDE + j],
                    )
                )
    run_copies(copies)


ANY = pl.BlockSpec(memory_space=pl.ANY)


def mover(kernel, out_shape, count, inputs):
    return pl.pallas_call(
        kernel,
        out_shape=out_shape,
        in_specs=[ANY] * inputs,
        out_specs=jax.tree.map(lambda _: ANY, out_shape),
        scratch_shapes=[pltpu.SemaphoreType.DMA((count,))],
    )


def per_device(activations, out_grads, master, first_moment, second_moment):
    tokens, width = activations.shape
    rows, cols = master.shape
    panels = out_grads.shape[0] // tokens
    kept = jax.ShapeDtypeStruct
    wide = SIDE * rows

    for_peer = mover(
        functools.partial(for_peer_kernel, rows), kept((SIDE, tokens, wide), jnp.bfloat16), SIDE * SIDE, 1
    )(activations)
    from_peer = lax.ppermute(for_peer, "dp", CORE_SWAP)
    chunk = kept((2, tokens, wide), jnp.bfloat16)
    chunks = mover(
        functools.partial(chunks_kernel, rows), [chunk] * SIDE, SIDE * SIDE + SIDE, 2
    )(activations, from_peer)
    acts = [chunks[0]] + [lax.ppermute(chunks[i], "dp", ring(i, 0)) for i in range(1, SIDE)]

    mine = lax.all_to_all(out_grads.reshape(panels, tokens, cols), "tensor", 0, 0)
    both = jnp.stack([mine, lax.ppermute(mine, "dp", CORE_SWAP)])
    grads = [both] + [lax.ppermute(both, "dp", ring(i, 0)) for i in range(1, SIDE)]

    parts = pl.pallas_call(
        functools.partial(product_kernel, rows),
        grid=(panels,),
        out_shape=kept((SIDE, panels, rows, cols), jnp.bfloat16),
        in_specs=[pl.BlockSpec((2, tokens, wide), lambda i: (0, 0, 0))] * SIDE
        + [pl.BlockSpec((2, 1, tokens, cols), lambda i: (0, i, 0, 0))] * SIDE,
        out_specs=pl.BlockSpec((SIDE, 1, rows, cols), lambda i: (0, i, 0, 0)),
        scratch_shapes=[pltpu.VMEM((wide, 2 * SIDE * tokens), jnp.bfloat16)],
        compiler_params=pltpu.CompilerParams(vmem_limit_bytes=40 * 1024 * 1024),
    )(*acts, *grads)

    half = panels // 2
    f32 = jnp.float32
    up = lax.ppermute(parts[2, :half], "dp", ring(1, 1))
    down = lax.ppermute(parts[2, half:], "dp", ring(3, 1))
    up_sum = (parts[1, :half].astype(f32) + up.astype(f32)).astype(jnp.bfloat16)
    down_sum = (parts[3, half:].astype(f32) + down.astype(f32)).astype(jnp.bfloat16)
    up = lax.ppermute(jnp.concatenate([up_sum, parts[1, half:]]), "dp", ring(1, 1))
    down = lax.ppermute(jnp.concatenate([parts[3, :half], down_sum]), "dp", ring(3, 1))
    line = (parts[0].astype(f32) + up.astype(f32) + down.astype(f32)).astype(jnp.bfloat16)

    grad = jnp.sum(lax.all_to_all(line, "tensor", 0, 0).astype(f32), axis=0)

    new_first = 0.9 * first_moment + 0.1 * grad
    new_second = 0.999 * second_moment + 0.001 * grad * grad
    first_fix = new_first / first_bias
    second_fix = new_second / second_bias
    new_master = master * (1.0 - 0.05 * 0.1) - 0.05 * first_fix / (jnp.sqrt(second_fix) + 1e-08)

    own = new_master.astype(jnp.bfloat16)
    own = lax.all_to_all(
        jnp.broadcast_to(own, (SIDE, rows, cols)), "dp", 0, 0, axis_index_groups=groups(0)
    )
    own = lax.all_to_all(
        jnp.broadcast_to(own, (SIDE, SIDE, rows, cols)), "dp", 0, 0, axis_index_groups=groups(1)
    )
    peer = lax.ppermute(own, "dp", CORE_SWAP)
    weights = mover(
        functools.partial(weights_kernel, rows), kept((width, cols), jnp.bfloat16), 2 * SIDE * SIDE, 2
    )(own, peer)
    return (new_master, new_first, new_second, weights)


def solution(mesh):
    return jax.shard_map(
        per_device,
        mesh=mesh,
        in_specs=(
            P(("dp", "tensor"), None),
            P("dp", "tensor"),
            P("dp", "tensor"),
            P("dp", "tensor"),
            P("dp", "tensor"),
        ),
        out_specs=(P("dp", "tensor"), P("dp", "tensor"), P("dp", "tensor"), P(None, "tensor")),
        check_vma=False,
    )
```

time: 353 us -> 388 us (1.099)
  waiting for transfers between devices: 320 us -> 59.8 us
  Pallas kernels: 0 us -> 233 us
  blocking collectives: 0 us -> 60.8 us
  starting transfers between devices: 0.12 us -> 29.3 us
  between operations: 13.8 us -> 0.81 us
  matrix products: 12.6 us -> 0 us
    pallas_call x0 -> x4, Pallas kernels: none -> 233 us  [the longest x1 128 us: per_device(): mover(functools.partial(weights_kernel, rows), kept((width, cols), jnp.bf...]
    all_gather x2 -> x0, waiting for transfers between devices: 232 us -> none  [the longest x1 178 us: per_device(): replica_rows = lax.all_gather(activations, 'tensor', axis=0, tiled=True)]
    reduce_scatter x1 -> x0, waiting for transfers between devices: 86.6 us -> none  [per_device(): lax.psum_scatter(contract_tokens(replica_rows, out_grads).astype(jnp.bflo...]
    all_to_all x0 -> x3, blocking collectives: none -> 60.8 us  [the longest x1 31.1 us: per_device(): grad = jnp.sum(lax.all_to_all(line, 'tensor', 0, 0).astype(f32), axis=0)]
    ppermute x0 -> x13, waiting for transfers between devices: none -> 59.8 us  [the longest x3 31.1 us: per_device(): lax.ppermute(chunks[i], 'dp', ring(i, 0))]
    ppermute x0 -> x13, starting transfers between devices: none -> 20.2 us  [the longest x1 5.55 us: per_device(): peer = lax.ppermute(own, 'dp', CORE_SWAP)]
    dot_general x1 -> x0, matrix products: 12.6 us -> none  [contract_tokens(): lax.dot_general(left, right, (((0,), (0,)), ((), ())), preferred_element_...]
    all_to_all x0 -> x1, starting transfers between devices: none -> 9.03 us  [per_device(): lax.all_to_all(out_grads.reshape(panels, tokens, cols), 'tensor', 0, 0)]
  transfers between devices with their start and end apart: 3 -> 14, of which waited for: 3 -> 7; matrix products, arithmetic and copies ran while one was open for 0% -> 0% of each run, Pallas kernels for 0% -> 25%
where the time goes in v1:
time: 388 us; the launch traced here: 387 us
  Pallas kernels  233 us (60%)
  blocking collectives  60.8 us (16%)
  waiting for transfers between devices  59.8 us (15%)
  starting transfers between devices  29.3 us (8%)
    pallas_call x1, Pallas kernels, per_device(): mover(functools.partial(weights_kernel, rows), kept((width, cols), jnp.bf...  128 us
    pallas_call x1, Pallas kernels, per_device(): mover(functools.partial(chunks_kernel, rows), [chunk] * SIDE, SIDE * SIDE...  64.8 us
    pallas_call x1, Pallas kernels, per_device(): mover(functools.partial(for_peer_kernel, rows), kept((SIDE, tokens, wide)...  33 us
    ppermute x3, waiting for transfers between devices, per_device(): lax.ppermute(chunks[i], 'dp', ring(i, 0))  31.1 us
    all_to_all x1, blocking collectives, per_device(): grad = jnp.sum(lax.all_to_all(line, 'tensor', 0, 0).astype(f32), axis=0)  31.1 us
    all_to_all x1, blocking collectives, per_device(): lax.all_to_all(jnp.broadcast_to(own, (SIDE, SIDE, rows, cols)), 'dp', 0,...  18.1 us
    ppermute x1, waiting for transfers between devices, per_device(): lax.ppermute(jnp.concatenate([parts[3, :half], down_sum]), 'dp', ring(3, 1))  11.6 us
    all_to_all x1, blocking collectives, per_device(): lax.all_to_all(jnp.broadcast_to(own, (SIDE, rows, cols)), 'dp', 0, 0, axi...  11.5 us
  transfers between devices with their start and end apart: 14, of which 7 were waited for; matrix products, arithmetic and copies ran while one was open for 0% of the time, Pallas kernels for 25%

profile of v1, /device:TPU:1, one launch (start us, length us, event | category | flops | bytes accessed | tf_op | source)
XLA Modules:
  0.0 387.5 jit_solution(1552681582316421306)
XLA Ops:
  0.6 9.0 %all-to-all-start = ((bf16[8,128,256]{2,1,0:T(8,128)(2,1)}), bf16[8,128,256]{2,1,0:T(8,128)(2,1)S(1)}, u32[]{:S(2)}, u32[]{:S(2)}) async-start(bf16[8,128,256]{2,1,0:T(8,128)(2,1)} %bitcast.27), calls=%async_computation | async-start | bytes 1048576 | tf_op jit(solution)/shard_map/all_to_all | solution.py:161
  9.7 33.0 %shard_map.84 = bf16[4,128,1024]{2,1,0:T(8,128)(2,1)} custom-call(bf16[128,8192]{1,0:T(8,128)(2,1)} %acts.3), custom_call_target="tpu_custom_call" | custom-call | tf_op jit(solution)/shard_map/pallas_call | solution.py:151
  42.7 1.0 collective-permute-start
  43.7 0.0 all-to-all-done
  43.7 0.1 collective-permute-start.4
  43.8 2.8 collective-permute-done.peer
  46.6 0.0 copy-start.2
  46.6 1.0 copy-done.2
  47.6 64.8 %shard_map.85 = (bf16[2,128,1024]{2,1,0:T(8,128)(2,1)}, bf16[2,128,1024]{2,1,0:T(8,128)(2,1)}, bf16[2,128,1024]{2,1,0:T(8,128)(2,1)}, bf16[2,128,1024]{2,1,0:T(8,128)(2,1)}) custom-call(bf16[128,8192]{1,0:T(8,128)(2,1)} %acts.3, bf16[4,128,1024]{2,1,0:T(8,128)(2,1)} %copy-done.2), custom_call_target="tpu_custom_call" | custom-call | tf_op jit(solution)/shard_map/pallas_call | solution.py:156
  112.4 0.0 copy-start.7
  112.4 0.0 copy-start.6
  112.4 0.0 copy-start
  112.4 1.4 collective-permute-start.1
  113.8 0.0 collective-permute-done.4
  113.8 0.1 pad_maximum_fusion.g0
  113.9 1.5 collective-permute-start.7
  115.4 1.6 collective-permute-start.6
  117.1 0.4 collective-permute-start.5
  117.5 0.0 copy-done.7
  117.5 1.6 collective-permute-start.2
  119.0 3.3 collective-permute-done.1.a1
  122.3 0.0 copy-done.6
  122.3 1.5 collective-permute-start.3
  123.8 27.8 %collective-permute-done.2.a2 = bf16[2,128,1024]{2,1,0:T(8,128)(2,1)S(1)} collective-permute-done((bf16[2,128,1024]{2,1,0:T(8,128)(2,1)S(1)}, bf16[2,128,1024]{2,1,0:T(8,128)(2,1)S(1)}, u32[]{:S(2)}, u32[]{:S(2)}) %collective-permute-start.2) | collective-permute-done | bytes 524320 | tf_op jit(solution)/shard_map/ppermute | solution.py:159
  151.6 0.0 collective-permute-done.3.a3
  151.6 0.0 collective-permute-done.7.g3
  151.6 0.0 collective-permute-done.6.g2
  151.6 0.0 collective-permute-done.5.g1
  151.6 0.0 copy-done
  151.7 7.0 %shard_map.86 = bf16[4,8,256,256]{3,2,1,0:T(8,128)(2,1)S(1)} custom-call(bf16[2,128,1024]{2,1,0:T(8,128)(2,1)S(1)} %copy-done, bf16[2,128,1024]{2,1,0:T(8,128)(2,1)S(1)} %collective-permute-done.1.a1, bf16[2,128,1024]{2,1,0:T(8,128)(2,1)S(1)} %collective-permute-done.2.a2, bf16[2,128,1024]{2,1,0:T(8,128)(2,1)S(1)} %collective-permute-done.3.a3, ...), custom_call_target="tpu_custom_call" | custom-call | tf_op jit(solution)/shard_map/pallas_call | solution.py:165
  158.7 0.1 slice_bitcast_fusion.5
  158.8 1.0 collective-permute-start.8
  159.8 1.8 collective-permute-start.10
  161.6 6.9 %collective-permute-done.8 = bf16[4,256,256]{2,1,0:T(8,128)(2,1)S(1)} collective-permute-done((bf16[4,256,256]{2,1,0:T(8,128)(2,1)S(1)}, bf16[4,256,256]{2,1,0:T(8,128)(2,1)S(1)}, u32[]{:S(2)}, u32[]{:S(2)}) %collective-permute-start.8) | collective-permute-done | bytes 524320 | tf_op jit(solution)/shard_map/ppermute | solution.py:178
  168.4 0.0 collective-permute-done.10
  168.4 0.3 fusion.3
  168.7 0.1 pad_maximum_fusion.2
  168.8 2.8 collective-permute-start.11
  171.6 0.1 pad_maximum_fusion.1
  171.7 0.1 collective-permute-start.9
  171.8 11.6 %collective-permute-done.11 = bf16[8,256,256]{2,1,0:T(8,128)(2,1)S(1)} collective-permute-done((bf16[8,256,256]{2,1,0:T(8,128)(2,1)S(1)}, bf16[8,256,256]{2,1,0:T(8,128)(2,1)S(1)}, u32[]{:S(2)}, u32[]{:S(2)}) %collective-permute-start.11) | collective-permute-done | bytes 1048608 | tf_op jit(solution)/shard_map/ppermute | solution.py:183
  183.3 3.6 collective-permute-done.9
  186.9 0.5 fusion.1
  187.4 0.0 copy-start.3
  187.4 0.0 copy-start.4
  187.4 0.0 copy-start.5
  187.4 31.1 %all_to_all.20 = bf16[8,256,256]{2,1,0:T(8,128)(2,1)S(1)} all-to-all(bf16[8,256,256]{2,1,0:T(8,128)(2,1)S(1)} %fusion.1), channel_id=1, replica_groups=mesh['dp'=32,'tensor'=8] {'tensor'}, dimensions={0} | all-to-all | bytes 2097152 | tf_op jit(solution)/shard_map/all_to_all | solution.py:186
  218.5 0.1 convert_reduce_fusion
  218.6 0.0 copy-done.3
  218.6 0.0 copy-done.4
  218.7 0.0 copy-done.5
  218.7 1.0 fusion.5
  219.7 11.5 %all_to_all.21 = bf16[4,256,256]{2,1,0:T(8,128)(2,1)S(1)} all-to-all(bf16[4,256,256]{2,1,0:T(8,128)(2,1)S(1)} %broadcast_in_dim.6), channel_id=1, replica_groups={{0,64,128,192},{8,24,40,56},{16,80,144,208},{72,88,104,120},{32,96,160,..., dimensions={0} | all-to-all | bytes 1048576 | tf_op jit(solution)/shard_map/all_to_all | solution.py:195
  231.2 0.2 broadcast_in_dim.7
  231.4 18.1 %all_to_all.22.own = bf16[4,4,256,256]{3,2,1,0:T(8,128)(2,1)S(1)} all-to-all(bf16[4,4,256,256]{3,2,1,0:T(8,128)(2,1)S(1)} %broadcast_in_dim.7), channel_id=1, replica_groups={{8,72,136,200},{0,16,32,48},{24,88,152,216},{64,80,96,112},{40,104,168,..., dimensions={0} | all-to-all | bytes 4194304 | tf_op jit(solution)/shard_map/all_to_all | solution.py:198
  249.6 0.0 copy-start.1
  249.6 5.6 %collective-permute-start.12 = (bf16[4,4,256,256]{3,2,1,0:T(8,128)(2,1)S(1)}, bf16[4,4,256,256]{3,2,1,0:T(8,128)(2,1)}, u32[]{:S(2)}, u32[]{:S(2)}) collective-permute-start(bf16[4,4,256,256]{3,2,1,0:T(8,128)(2,1)S(1)} %all_to_all.22.own), channel_id=1, source_target_pairs={{0,8},{8,0},{16,24},{24,16},{32,40},{40,32},{48,56},{56,48},{64,72... | collective-permute-start | bytes 6291464 | tf_op jit(solution)/shard_map/ppermute | solution.py:201
  255.1 3.9 %collective-permute-done.12.peer = bf16[4,4,256,256]{3,2,1,0:T(8,128)(2,1)} collective-permute-done((bf16[4,4,256,256]{3,2,1,0:T(8,128)(2,1)S(1)}, bf16[4,4,256,256]{3,2,1,0:T(8,128)(2,1)}, u32[]{:S(2)}, u32[]{:S(2)}) %collective-permute-start.12) | collective-permute-done | bytes 2097184 | tf_op jit(solution)/shard_map/ppermute | solution.py:201
  259.0 0.0 copy-done.1
  259.0 128.4 %shard_map.87 = bf16[8192,256]{1,0:T(8,128)(2,1)} custom-call(bf16[4,4,256,256]{3,2,1,0:T(8,128)(2,1)} %copy-done.1, bf16[4,4,256,256]{3,2,1,0:T(8,128)(2,1)} %collective-permute-done.12.peer), custom_call_target="tpu_custom_call" | custom-call | tf_op jit(solution)/shard_map/pallas_call | solution.py:202
  (1 shorter events, 0.0 us)
Async XLA Ops:
  0.6 43.1 %all-to-all-start = ((bf16[8,128,256]{2,1,0:T(8,128)(2,1)}), bf16[8,128,256]{2,1,0:T(8,128)(2,1)S(1)}, u32[]{:S(2)}, u32[]{:S(2)}) async-start(bf16[8,128,256]{2,1,0:T(8,128)(2,1)} %bitcast.27), calls=%async_computation | async-start | bytes 1048576 | tf_op jit(solution)/shard_map/all_to_all | solution.py:161
  42.7 3.9 %collective-permute-start = (bf16[4,128,1024]{2,1,0:T(8,128)(2,1)}, bf16[4,128,1024]{2,1,0:T(8,128)(2,1)S(1)}, u32[]{:S(2)}, u32[]{:S(2)}) collective-permute-start(bf16[4,128,1024]{2,1,0:T(8,128)(2,1)} %shard_map.84), channel_id=1, source_target_pairs={{0,8},{8,0},{16,24},{24,16},{32,40},{40,32},{48,56},{56,48},{64,72... | collective-permute-start | bytes 3145736 | tf_op jit(solution)/shard_map/ppermute | solution.py:154
  43.7 70.1 %collective-permute-start.4 = (bf16[8,128,256]{2,1,0:T(8,128)(2,1)S(1)}, bf16[8,128,256]{2,1,0:T(8,128)(2,1)S(1)}, u32[]{:S(2)}, u32[]{:S(2)}) collective-permute-start(bf16[8,128,256]{2,1,0:T(8,128)(2,1)S(1)} %all-to-all-done), channel_id=1, source_target_pairs={{0,8},{8,0},{16,24},{24,16},{32,40},{40,32},{48,56},{56,48},{64,72... | collective-permute-start | bytes 1572872 | tf_op jit(solution)/shard_map/ppermute | solution.py:162
  46.6 1.0 copy-start.2
  112.4 5.1 %copy-start.7 = (bf16[2,128,1024]{2,1,0:T(8,128)(2,1)S(1)}, bf16[2,128,1024]{2,1,0:T(8,128)(2,1)}, u32[]{:S(2)}) copy-start(bf16[2,128,1024]{2,1,0:T(8,128)(2,1)} %get-tuple-element.10) | copy-start | bytes 1572868
  112.4 9.9 %copy-start.6 = (bf16[2,128,1024]{2,1,0:T(8,128)(2,1)S(1)}, bf16[2,128,1024]{2,1,0:T(8,128)(2,1)}, u32[]{:S(2)}) copy-start(bf16[2,128,1024]{2,1,0:T(8,128)(2,1)} %get-tuple-element.11) | copy-start | bytes 1572868
  112.4 39.2 %copy-start = (bf16[2,128,1024]{2,1,0:T(8,128)(2,1)S(1)}, bf16[2,128,1024]{2,1,0:T(8,128)(2,1)}, u32[]{:S(2)}) copy-start(bf16[2,128,1024]{2,1,0:T(8,128)(2,1)} %get-tuple-element.8.a0) | copy-start | bytes 1572868
  112.4 9.9 %collective-permute-start.1 = (bf16[2,128,1024]{2,1,0:T(8,128)(2,1)}, bf16[2,128,1024]{2,1,0:T(8,128)(2,1)S(1)}, u32[]{:S(2)}, u32[]{:S(2)}) collective-permute-start(bf16[2,128,1024]{2,1,0:T(8,128)(2,1)} %get-tuple-element.9), channel_id=1, source_target_pairs={{0,64},{8,24},{16,80},{24,40},{32,96},{40,56},{48,112},{56,8},{64,... | collective-permute-start | bytes 1572872 | tf_op jit(solution)/shard_map/ppermute | solution.py:159
  113.9 37.7 %collective-permute-start.7 = (bf16[2,8,128,256]{3,2,1,0:T(8,128)(2,1)S(1)}, bf16[2,8,128,256]{3,2,1,0:T(8,128)(2,1)S(1)}, u32[]{:S(2)}, u32[]{:S(2)}) collective-permute-start(bf16[2,8,128,256]{3,2,1,0:T(8,128)(2,1)S(1)} %pad_maximum_fusion.g0), channel_id=1, source_target_pairs={{0,192},{8,56},{16,208},{24,8},{32,224},{40,24},{48,240},{56,40},{... | collective-permute-start | bytes 3145736 | tf_op jit(solution)/shard_map/ppermute | solution.py:163
  115.4 36.2 %collective-permute-start.6 = (bf16[2,8,128,256]{3,2,1,0:T(8,128)(2,1)S(1)}, bf16[2,8,128,256]{3,2,1,0:T(8,128)(2,1)S(1)}, u32[]{:S(2)}, u32[]{:S(2)}) collective-permute-start(bf16[2,8,128,256]{3,2,1,0:T(8,128)(2,1)S(1)} %pad_maximum_fusion.g0), channel_id=1, source_target_pairs={{0,128},{8,40},{16,144},{24,56},{32,160},{40,8},{48,176},{56,24},{... | collective-permute-start | bytes 3145736 | tf_op jit(solution)/shard_map/ppermute | solution.py:163
  117.1 34.6 %collective-permute-start.5 = (bf16[2,8,128,256]{3,2,1,0:T(8,128)(2,1)S(1)}, bf16[2,8,128,256]{3,2,1,0:T(8,128)(2,1)S(1)}, u32[]{:S(2)}, u32[]{:S(2)}) collective-permute-start(bf16[2,8,128,256]{3,2,1,0:T(8,128)(2,1)S(1)} %pad_maximum_fusion.g0), channel_id=1, source_target_pairs={{0,64},{8,24},{16,80},{24,40},{32,96},{40,56},{48,112},{56,8},{64,... | collective-permute-start | bytes 3145736 | tf_op jit(solution)/shard_map/ppermute | solution.py:163
  117.5 34.2 %collective-permute-start.2 = (bf16[2,128,1024]{2,1,0:T(8,128)(2,1)S(1)}, bf16[2,128,1024]{2,1,0:T(8,128)(2,1)S(1)}, u32[]{:S(2)}, u32[]{:S(2)}) collective-permute-start(bf16[2,128,1024]{2,1,0:T(8,128)(2,1)S(1)} %copy-done.7), channel_id=1, source_target_pairs={{0,128},{8,40},{16,144},{24,56},{32,160},{40,8},{48,176},{56,24},{... | collective-permute-start | bytes 1572872 | tf_op jit(solution)/shard_map/ppermute | solution.py:159
  122.3 29.3 %collective-permute-start.3 = (bf16[2,128,1024]{2,1,0:T(8,128)(2,1)S(1)}, bf16[2,128,1024]{2,1,0:T(8,128)(2,1)S(1)}, u32[]{:S(2)}, u32[]{:S(2)}) collective-permute-start(bf16[2,128,1024]{2,1,0:T(8,128)(2,1)S(1)} %copy-done.6), channel_id=1, source_target_pairs={{0,192},{8,56},{16,208},{24,8},{32,224},{40,24},{48,240},{56,40},{... | collective-permute-start | bytes 1572872 | tf_op jit(solution)/shard_map/ppermute | solution.py:159
  158.8 9.6 %collective-permute-start.8 = (bf16[4,256,256]{2,1,0:T(8,128)(2,1)S(1)}, bf16[4,256,256]{2,1,0:T(8,128)(2,1)S(1)}, u32[]{:S(2)}, u32[]{:S(2)}) collective-permute-start(bf16[4,256,256]{2,1,0:T(8,128)(2,1)S(1)} %get-tuple-element.18), channel_id=1, source_target_pairs={{0,16},{8,72},{16,32},{24,88},{32,48},{40,104},{48,0},{56,120},{64... | collective-permute-start | bytes 1572872 | tf_op jit(solution)/shard_map/ppermute | solution.py:178
  159.8 8.6 %collective-permute-start.10 = (bf16[4,256,256]{2,1,0:T(8,128)(2,1)S(1)}, bf16[4,256,256]{2,1,0:T(8,128)(2,1)S(1)}, u32[]{:S(2)}, u32[]{:S(2)}) collective-permute-start(bf16[4,256,256]{2,1,0:T(8,128)(2,1)S(1)} %get-tuple-element.19), channel_id=1, source_target_pairs={{0,48},{8,200},{16,0},{24,216},{32,16},{40,232},{48,32},{56,248},{... | collective-permute-start | bytes 1572872 | tf_op jit(solution)/shard_map/ppermute | solution.py:179
  168.8 14.5 %collective-permute-start.11 = (bf16[8,256,256]{2,1,0:T(8,128)(2,1)S(1)}, bf16[8,256,256]{2,1,0:T(8,128)(2,1)S(1)}, u32[]{:S(2)}, u32[]{:S(2)}) collective-permute-start(bf16[8,256,256]{2,1,0:T(8,128)(2,1)S(1)} %pad_maximum_fusion.2), channel_id=1, source_target_pairs={{0,48},{8,200},{16,0},{24,216},{32,16},{40,232},{48,32},{56,248},{... | collective-permute-start | bytes 3145736 | tf_op jit(solution)/shard_map/ppermute | solution.py:183
  171.7 15.2 %collective-permute-start.9 = (bf16[8,256,256]{2,1,0:T(8,128)(2,1)S(1)}, bf16[8,256,256]{2,1,0:T(8,128)(2,1)S(1)}, u32[]{:S(2)}, u32[]{:S(2)}) collective-permute-start(bf16[8,256,256]{2,1,0:T(8,128)(2,1)S(1)} %pad_maximum_fusion.1), channel_id=1, source_target_pairs={{0,16},{8,72},{16,32},{24,88},{32,48},{40,104},{48,0},{56,120},{64... | collective-permute-start | bytes 3145736 | tf_op jit(solution)/shard_map/ppermute | solution.py:182
  187.4 31.3 %copy-start.3 = (f32[256,256]{1,0:T(8,128)S(1)}, f32[256,256]{1,0:T(8,128)}, u32[]{:S(2)}) copy-start(f32[256,256]{1,0:T(8,128)} %param.7) | copy-start | bytes 786436
  187.4 31.3 %copy-start.4 = (f32[256,256]{1,0:T(8,128)S(1)}, f32[256,256]{1,0:T(8,128)}, u32[]{:S(2)}) copy-start(f32[256,256]{1,0:T(8,128)} %param.8) | copy-start | bytes 786436
  187.4 31.3 %copy-start.5 = (f32[256,256]{1,0:T(8,128)S(1)}, f32[256,256]{1,0:T(8,128)}, u32[]{:S(2)}) copy-start(f32[256,256]{1,0:T(8,128)} %param.9) | copy-start | bytes 786436
  249.6 9.5 %copy-start.1 = (bf16[4,4,256,256]{3,2,1,0:T(8,128)(2,1)}, bf16[4,4,256,256]{3,2,1,0:T(8,128)(2,1)S(1)}, u32[]{:S(2)}) copy-start(bf16[4,4,256,256]{3,2,1,0:T(8,128)(2,1)S(1)} %all_to_all.22.own) | copy-start | bytes 6291460
  249.6 9.5 %collective-permute-start.12 = (bf16[4,4,256,256]{3,2,1,0:T(8,128)(2,1)S(1)}, bf16[4,4,256,256]{3,2,1,0:T(8,128)(2,1)}, u32[]{:S(2)}, u32[]{:S(2)}) collective-permute-start(bf16[4,4,256,256]{3,2,1,0:T(8,128)(2,1)S(1)} %all_to_all.22.own), channel_id=1, source_target_pairs={{0,8},{8,0},{16,24},{24,16},{32,40},{40,32},{48,56},{56,48},{64,72... | collective-permute-start | bytes 6291464 | tf_op jit(solution)/shard_map/ppermute | solution.py:201

commit v2 on v1

--- a/solution.py
+++ b/solution.py
@@ -51,47 +51,25 @@
     return (bx * SIDE + by) * 2 + core
 
 
-def run_copies(copies):
-    for copy in copies:
-        copy.start()
-    for copy in copies:
-        copy.wait()
+def block_at(array, block, rows):
+    return array[:, pl.ds(pl.multiple_of(block * rows, rows), rows)]
 
 
-def for_peer_kernel(rows, acts, out, sem):
+def for_peer_kernel(rows, acts, out):
     x, y, core = place()
-    copies = []
     for split in range(SIDE):
         for reduce in range(SIDE):
             block = block_of(x, y, 1 - core, split, reduce)
-            copies.append(
-                pltpu.make_async_copy(
-                    acts.at[:, pl.ds(pl.multiple_of(block * rows, rows), rows)],
-                    out.at[split, :, pl.ds(reduce * rows, rows)],
-                    sem.at[split * SIDE + reduce],
-                )
-            )
-    run_copies(copies)
+            out[split, :, reduce * rows : (reduce + 1) * rows] = block_at(acts, block, rows)
 
 
-def chunks_kernel(rows, acts, peer, *rest):
-    outs, sem = rest[:SIDE], rest[SIDE]
+def chunks_kernel(rows, acts, peer, *outs):
     x, y, core = place()
-    copies = []
     for split in range(SIDE):
         for reduce in range(SIDE):
             block = block_of(x, y, core, split, reduce)
-            copies.append(
-                pltpu.make_async_copy(
-                    acts.at[:, pl.ds(pl.multiple_of(block * rows, rows), rows)],
-                    outs[split].at[0, :, pl.ds(reduce * rows, rows)],
-                    sem.at[split * SIDE + reduce],
-                )
-            )
-        copies.append(
-            pltpu.make_async_copy(peer.at[split], outs[split].at[1], sem.at[SIDE * SIDE + split])
-        )
-    run_copies(copies)
+            outs[split][0, :, reduce * rows : (reduce + 1) * rows] = block_at(acts, block, rows)
+        outs[split][1] = peer[split]
 
 
 def product_kernel(rows, a0, a1, a2, a3, g0, g1, g2, g3, out, turned):
@@ -111,33 +89,28 @@
         ).astype(out.dtype)
 
 
-def weights_kernel(rows, own, peer, out, sem):
+def weights_kernel(own, peer, out):
     _, _, core = place()
-    copies = []
-    for which, (array, of_core) in enumerate(((own, core), (peer, 1 - core))):
-        for i in range(SIDE):
-            for j in range(SIDE):
-                block = jnp.where(of_core == 0, j * SIDE + i, i * SIDE + j) * 2 + of_core
-                copies.append(
-                    pltpu.make_async_copy(
-                        array.at[i, j],
-                        out.at[pl.ds(pl.multiple_of(block * rows, rows), rows), :],
-                        sem.at[(which * SIDE + i) * SIDE + j],
-                    )
-                )
-    run_copies(copies)
+    x = pl.program_id(0)
+    for of_core, (first, second) in enumerate(((own, peer), (peer, own))):
+
+        @pl.when(core == of_core)
+        def _():
+            for y in range(SIDE):
+                out[0, y, 0] = first[y, x]
+                out[0, y, 1] = second[x, y]
 
 
-ANY = pl.BlockSpec(memory_space=pl.ANY)
+VMEM = pl.BlockSpec(memory_space=pltpu.VMEM)
 
 
-def mover(kernel, out_shape, count, inputs):
+def mover(kernel, out_shape, inputs):
     return pl.pallas_call(
         kernel,
         out_shape=out_shape,
-        in_specs=[ANY] * inputs,
-        out_specs=jax.tree.map(lambda _: ANY, out_shape),
-        scratch_shapes=[pltpu.SemaphoreType.DMA((count,))],
+        in_specs=[VMEM] * inputs,
+        out_specs=jax.tree.map(lambda _: VMEM, out_shape),
+        compiler_params=pltpu.CompilerParams(vmem_limit_bytes=32 * 1024 * 1024),
     )
 
 
@@ -149,12 +122,12 @@
     wide = SIDE * rows
 
     for_peer = mover(
-        functools.partial(for_peer_kernel, rows), kept((SIDE, tokens, wide), jnp.bfloat16), SIDE * SIDE, 1
+        functools.partial(for_peer_kernel, rows), kept((SIDE, tokens, wide), jnp.bfloat16), 1
     )(activations)
     from_peer = lax.ppermute(for_peer, "dp", CORE_SWAP)
     chunk = kept((2, tokens, wide), jnp.bfloat16)
     chunks = mover(
-        functools.partial(chunks_kernel, rows), [chunk] * SIDE, SIDE * SIDE + SIDE, 2
+        functools.partial(chunks_kernel, rows), [chunk] * SIDE, 2
     )(activations, from_peer)
     acts = [chunks[0]] + [lax.ppermute(chunks[i], "dp", ring(i, 0)) for i in range(1, SIDE)]
 
@@ -199,9 +172,14 @@
         jnp.broadcast_to(own, (SIDE, SIDE, rows, cols)), "dp", 0, 0, axis_index_groups=groups(1)
     )
     peer = lax.ppermute(own, "dp", CORE_SWAP)
-    weights = mover(
-        functools.partial(weights_kernel, rows), kept((width, cols), jnp.bfloat16), 2 * SIDE * SIDE, 2
-    )(own, peer)
+    weights = pl.pallas_call(
+        weights_kernel,
+        grid=(SIDE,),
+        out_shape=kept((SIDE, SIDE, 2, rows, cols), jnp.bfloat16),
+        in_specs=[VMEM] * 2,
+        out_specs=pl.BlockSpec((1, SIDE, 2, rows, cols), lambda i: (i, 0, 0, 0, 0)),
+        compiler_params=pltpu.CompilerParams(vmem_limit_bytes=32 * 1024 * 1024),
+    )(own, peer).reshape(width, cols)
     return (new_master, new_first, new_second, weights)
 
 

time: 388 us -> 175 us (0.45)
  Pallas kernels: 233 us -> 10.8 us
  waiting for transfers between devices: 59.8 us -> 70.1 us
    pallas_call x2, Pallas kernels: 193 us -> 2.63 us  [the longest x1 2.42 us: per_device(): pl.pallas_call(weights_kernel, grid=(SIDE,), out_shape=kept((SIDE, SIDE,...]
    pallas_call x1, Pallas kernels: 33 us -> 1.11 us  [per_device(): mover(functools.partial(for_peer_kernel, rows), kept((SIDE, tokens, wide)...]
    all_to_all x1, waiting for transfers between devices: 0.01 us -> 14.4 us  [per_device(): lax.all_to_all(out_grads.reshape(panels, tokens, cols), 'tensor', 0, 0)]
    all_to_all x1, blocking collectives: 11.5 us -> 15.7 us  [per_device(): lax.all_to_all(jnp.broadcast_to(own, (SIDE, rows, cols)), 'dp', 0, 0, axi...]
    all_to_all x1, blocking collectives: 31.1 us -> 27.2 us  [per_device(): grad = jnp.sum(lax.all_to_all(line, 'tensor', 0, 0).astype(f32), axis=0)]
  transfers between devices with their start and end apart: 14 -> 14, of which waited for: 7 -> 9; matrix products, arithmetic and copies ran while one was open for 0% -> 1% of each run, Pallas kernels for 25% -> 1%
where the time goes in v2:
time: 175 us
  waiting for transfers between devices  70.1 us (40%)
  blocking collectives  61 us (35%)
  starting transfers between devices  27.3 us (16%)
  Pallas kernels  10.8 us (6%)
  other arithmetic  3.19 us (2%)
  local copies, waits for them, and re-layouts  1.99 us (1%)
    ppermute x3, waiting for transfers between devices, per_device(): lax.ppermute(chunks[i], 'dp', ring(i, 0))  29.8 us
    all_to_all x1, blocking collectives, per_device(): grad = jnp.sum(lax.all_to_all(line, 'tensor', 0, 0).astype(f32), axis=0)  27.2 us
    all_to_all x1, blocking collectives, per_device(): lax.all_to_all(jnp.broadcast_to(own, (SIDE, SIDE, rows, cols)), 'dp', 0,...  18.1 us
    all_to_all x1, blocking collectives, per_device(): lax.all_to_all(jnp.broadcast_to(own, (SIDE, rows, cols)), 'dp', 0, 0, axi...  15.7 us
    all_to_all x1, waiting for transfers between devices, per_device(): lax.all_to_all(out_grads.reshape(panels, tokens, cols), 'tensor', 0, 0)  14.4 us
    ppermute x1, waiting for transfers between devices, per_device(): lax.ppermute(jnp.concatenate([parts[3, :half], down_sum]), 'dp', ring(3, 1))  11.6 us
    all_to_all x1, starting transfers between devices, per_device(): lax.all_to_all(out_grads.reshape(panels, tokens, cols), 'tensor', 0, 0)  9.03 us
    pallas_call x1, Pallas kernels, per_device(): pl.pallas_call(functools.partial(product_kernel, rows), grid=(panels,), o...  7 us
  transfers between devices with their start and end apart: 14, of which 9 were waited for; matrix products, arithmetic and copies ran while one was open for 1% of the time, Pallas kernels for 1%

profile of v2, /device:TPU:1, one launch (start us, length us, event | category | flops | bytes accessed | tf_op | source)
XLA Modules:
  0.0 175.1 jit_solution(5609080376694211506)
XLA Ops:
  0.6 9.0 %all-to-all-start = ((bf16[8,128,256]{2,1,0:T(8,128)(2,1)}), bf16[8,128,256]{2,1,0:T(8,128)(2,1)}, u32[]{:S(2)}, u32[]{:S(2)}) async-start(bf16[8,128,256]{2,1,0:T(8,128)(2,1)} %bitcast.28), calls=%async_computation | async-start | bytes 1048576 | tf_op jit(solution)/shard_map/all_to_all | solution.py:134
  9.7 0.0 copy-start
  9.7 1.6 copy-done
  11.2 0.0 copy-start.1
  11.3 1.1 shard_map.84
  12.4 1.0 collective-permute-start
  13.3 14.4 %all-to-all-done = bf16[8,128,256]{2,1,0:T(8,128)(2,1)} async-done(((bf16[8,128,256]{2,1,0:T(8,128)(2,1)}), bf16[8,128,256]{2,1,0:T(8,128)(2,1)}, u32[]{:S(2)}, u32[]{:S(2)}) %all-to-all-start) | async-done | bytes 524320 | tf_op jit(solution)/shard_map/all_to_all | solution.py:134
  27.7 0.5 collective-permute-start.4
  28.2 0.0 collective-permute-done.peer
  28.2 0.0 copy-done.1
  28.2 0.2 shard_map.85
  28.4 1.4 collective-permute-start.1
  29.8 0.1 collective-permute-done.4
  30.0 1.1 pad_maximum_fusion.g0
  31.1 2.8 %collective-permute-start.7 = (bf16[2,8,128,256]{3,2,1,0:T(8,128)(2,1)S(1)}, bf16[2,8,128,256]{3,2,1,0:T(8,128)(2,1)S(1)}, u32[]{:S(2)}, u32[]{:S(2)}) collective-permute-start(bf16[2,8,128,256]{3,2,1,0:T(8,128)(2,1)S(1)} %pad_maximum_fusion.g0), channel_id=1, source_target_pairs={{0,192},{8,56},{16,208},{24,8},{32,224},{40,24},{48,240},{56,40},{... | collective-permute-start | bytes 3145736 | tf_op jit(solution)/shard_map/ppermute | solution.py:136
  33.9 0.3 collective-permute-start.6
  34.3 0.7 collective-permute-start.5
  35.0 1.9 %collective-permute-start.2 = (bf16[2,128,1024]{2,1,0:T(8,128)(2,1)S(1)}, bf16[2,128,1024]{2,1,0:T(8,128)(2,1)S(1)}, u32[]{:S(2)}, u32[]{:S(2)}) collective-permute-start(bf16[2,128,1024]{2,1,0:T(8,128)(2,1)S(1)} %get-tuple-element.10), channel_id=1, source_target_pairs={{0,128},{8,40},{16,144},{24,56},{32,160},{40,8},{48,176},{56,24},{... | collective-permute-start | bytes 1572872 | tf_op jit(solution)/shard_map/ppermute | solution.py:132
  36.9 1.2 collective-permute-done.1.a1
  38.1 1.5 collective-permute-start.3
  39.6 27.9 %collective-permute-done.2.a2 = bf16[2,128,1024]{2,1,0:T(8,128)(2,1)S(1)} collective-permute-done((bf16[2,128,1024]{2,1,0:T(8,128)(2,1)S(1)}, bf16[2,128,1024]{2,1,0:T(8,128)(2,1)S(1)}, u32[]{:S(2)}, u32[]{:S(2)}) %collective-permute-start.2) | collective-permute-done | bytes 524320 | tf_op jit(solution)/shard_map/ppermute | solution.py:132
  67.4 0.7 collective-permute-done.3.a3
  68.1 0.0 collective-permute-done.7.g3
  68.1 0.0 collective-permute-done.6.g2
  68.1 0.0 collective-permute-done.5.g1
  68.1 7.0 %shard_map.86 = bf16[4,8,256,256]{3,2,1,0:T(8,128)(2,1)S(1)} custom-call(bf16[2,128,1024]{2,1,0:T(8,128)(2,1)S(1)} %get-tuple-element.8.a0, bf16[2,128,1024]{2,1,0:T(8,128)(2,1)S(1)} %collective-permute-done.1.a1, bf16[2,128,1024]{2,1,0:T(8,128)(2,1)S(1)} %collective-permute-done.2.a2, bf16[2,128,1024]{2,1,0:T(8,128)(2,1)S(1)} %collective-permute-done.3.a3, ...), custom_call_target="tpu_custom_call" | custom-call | tf_op jit(solution)/shard_map/pallas_call | solution.py:138
  75.2 0.1 slice_bitcast_fusion.5
  75.3 1.3 collective-permute-start.8
  76.6 1.5 collective-permute-start.10
  78.1 6.9 %collective-permute-done.8 = bf16[4,256,256]{2,1,0:T(8,128)(2,1)S(1)} collective-permute-done((bf16[4,256,256]{2,1,0:T(8,128)(2,1)S(1)}, bf16[4,256,256]{2,1,0:T(8,128)(2,1)S(1)}, u32[]{:S(2)}, u32[]{:S(2)}) %collective-permute-start.8) | collective-permute-done | bytes 524320 | tf_op jit(solution)/shard_map/ppermute | solution.py:151
  84.9 0.0 collective-permute-done.10
  84.9 0.3 fusion.3
  85.2 0.1 pad_maximum_fusion.2
  85.3 2.8 %collective-permute-start.11 = (bf16[8,256,256]{2,1,0:T(8,128)(2,1)S(1)}, bf16[8,256,256]{2,1,0:T(8,128)(2,1)S(1)}, u32[]{:S(2)}, u32[]{:S(2)}) collective-permute-start(bf16[8,256,256]{2,1,0:T(8,128)(2,1)S(1)} %pad_maximum_fusion.2), channel_id=1, source_target_pairs={{0,48},{8,200},{16,0},{24,216},{32,16},{40,232},{48,32},{56,248},{... | collective-permute-start | bytes 3145736 | tf_op jit(solution)/shard_map/ppermute | solution.py:156
  88.1 0.1 pad_maximum_fusion.1
  88.2 0.1 collective-permute-start.9
  88.2 11.6 %collective-permute-done.11 = bf16[8,256,256]{2,1,0:T(8,128)(2,1)S(1)} collective-permute-done((bf16[8,256,256]{2,1,0:T(8,128)(2,1)S(1)}, bf16[8,256,256]{2,1,0:T(8,128)(2,1)S(1)}, u32[]{:S(2)}, u32[]{:S(2)}) %collective-permute-start.11) | collective-permute-done | bytes 1048608 | tf_op jit(solution)/shard_map/ppermute | solution.py:156
  99.8 3.6 %collective-permute-done.9 = bf16[8,256,256]{2,1,0:T(8,128)(2,1)S(1)} collective-permute-done((bf16[8,256,256]{2,1,0:T(8,128)(2,1)S(1)}, bf16[8,256,256]{2,1,0:T(8,128)(2,1)S(1)}, u32[]{:S(2)}, u32[]{:S(2)}) %collective-permute-start.9) | collective-permute-done | bytes 1048608 | tf_op jit(solution)/shard_map/ppermute | solution.py:155
  103.4 0.5 fusion.1
  103.8 0.0 copy-start.2
  103.9 0.0 copy-start.3
  103.9 0.0 copy-start.4
  103.9 27.2 %all_to_all.20 = bf16[8,256,256]{2,1,0:T(8,128)(2,1)S(1)} all-to-all(bf16[8,256,256]{2,1,0:T(8,128)(2,1)S(1)} %fusion.1), channel_id=1, replica_groups=mesh['dp'=32,'tensor'=8] {'tensor'}, dimensions={0} | all-to-all | bytes 2097152 | tf_op jit(solution)/shard_map/all_to_all | solution.py:159
  131.0 0.1 convert_reduce_fusion
  131.2 0.0 copy-done.2
  131.2 0.0 copy-done.3
  131.2 0.0 copy-done.4
  131.2 1.0 fusion.5
  132.2 15.7 %all_to_all.21 = bf16[4,256,256]{2,1,0:T(8,128)(2,1)S(1)} all-to-all(bf16[4,256,256]{2,1,0:T(8,128)(2,1)S(1)} %broadcast_in_dim.6), channel_id=1, replica_groups={{0,64,128,192},{8,24,40,56},{16,80,144,208},{72,88,104,120},{32,96,160,..., dimensions={0} | all-to-all | bytes 1048576 | tf_op jit(solution)/shard_map/all_to_all | solution.py:168
  147.9 0.2 broadcast_in_dim.7
  148.1 18.1 %all_to_all.22.own = bf16[4,4,256,256]{3,2,1,0:T(8,128)(2,1)S(1)} all-to-all(bf16[4,4,256,256]{3,2,1,0:T(8,128)(2,1)S(1)} %broadcast_in_dim.7), channel_id=1, replica_groups={{8,72,136,200},{0,16,32,48},{24,88,152,216},{64,80,96,112},{40,104,168,..., dimensions={0} | all-to-all | bytes 4194304 | tf_op jit(solution)/shard_map/all_to_all | solution.py:171
  166.2 2.6 %collective-permute-start.12 = (bf16[4,4,256,256]{3,2,1,0:T(8,128)(2,1)S(1)}, bf16[4,4,256,256]{3,2,1,0:T(8,128)(2,1)S(1)}, u32[]{:S(2)}, u32[]{:S(2)}) collective-permute-start(bf16[4,4,256,256]{3,2,1,0:T(8,128)(2,1)S(1)} %all_to_all.22.own), channel_id=1, source_target_pairs={{0,8},{8,0},{16,24},{24,16},{32,40},{40,32},{48,56},{56,48},{64,72... | collective-permute-start | bytes 6291464 | tf_op jit(solution)/shard_map/ppermute | solution.py:174
  168.9 3.8 %collective-permute-done.12.peer = bf16[4,4,256,256]{3,2,1,0:T(8,128)(2,1)S(1)} collective-permute-done((bf16[4,4,256,256]{3,2,1,0:T(8,128)(2,1)S(1)}, bf16[4,4,256,256]{3,2,1,0:T(8,128)(2,1)S(1)}, u32[]{:S(2)}, u32[]{:S(2)}) %collective-permute-start.12) | collective-permute-done | bytes 2097184 | tf_op jit(solution)/shard_map/ppermute | solution.py:174
  172.7 2.4 %shard_map.87 = bf16[4,4,2,256,256]{4,3,2,1,0:T(8,128)(2,1)} custom-call(bf16[4,4,256,256]{3,2,1,0:T(8,128)(2,1)S(1)} %all_to_all.22.own, bf16[4,4,256,256]{3,2,1,0:T(8,128)(2,1)S(1)} %collective-permute-done.12.peer), custom_call_target="tpu_custom_call" | custom-call | tf_op jit(solution)/shard_map/pallas_call | solution.py:175
  (1 shorter events, 0.0 us)
Async XLA Ops:
  0.6 27.1 %all-to-all-start = ((bf16[8,128,256]{2,1,0:T(8,128)(2,1)}), bf16[8,128,256]{2,1,0:T(8,128)(2,1)}, u32[]{:S(2)}, u32[]{:S(2)}) async-start(bf16[8,128,256]{2,1,0:T(8,128)(2,1)} %bitcast.28), calls=%async_computation | async-start | bytes 1048576 | tf_op jit(solution)/shard_map/all_to_all | solution.py:134
  9.7 1.6 copy-start
  11.2 17.0 %copy-start.1 = (bf16[128,8192]{1,0:T(8,128)(2,1)S(1)}, bf16[128,8192]{1,0:T(8,128)(2,1)}, u32[]{:S(2)}) copy-start(bf16[128,8192]{1,0:T(8,128)(2,1)} %acts.3) | copy-start | bytes 6291460
  12.4 15.9 %collective-permute-start = (bf16[4,128,1024]{2,1,0:T(8,128)(2,1)}, bf16[4,128,1024]{2,1,0:T(8,128)(2,1)S(1)}, u32[]{:S(2)}, u32[]{:S(2)}) collective-permute-start(bf16[4,128,1024]{2,1,0:T(8,128)(2,1)} %shard_map.84), channel_id=1, source_target_pairs={{0,8},{8,0},{16,24},{24,16},{32,40},{40,32},{48,56},{56,48},{64,72... | collective-permute-start | bytes 3145736 | tf_op jit(solution)/shard_map/ppermute | solution.py:127
  27.7 2.2 %collective-permute-start.4 = (bf16[8,128,256]{2,1,0:T(8,128)(2,1)}, bf16[8,128,256]{2,1,0:T(8,128)(2,1)S(1)}, u32[]{:S(2)}, u32[]{:S(2)}) collective-permute-start(bf16[8,128,256]{2,1,0:T(8,128)(2,1)} %all-to-all-done), channel_id=1, source_target_pairs={{0,8},{8,0},{16,24},{24,16},{32,40},{40,32},{48,56},{56,48},{64,72... | collective-permute-start | bytes 1572872 | tf_op jit(solution)/shard_map/ppermute | solution.py:135
  28.4 9.7 %collective-permute-start.1 = (bf16[2,128,1024]{2,1,0:T(8,128)(2,1)S(1)}, bf16[2,128,1024]{2,1,0:T(8,128)(2,1)S(1)}, u32[]{:S(2)}, u32[]{:S(2)}) collective-permute-start(bf16[2,128,1024]{2,1,0:T(8,128)(2,1)S(1)} %get-tuple-element.9), channel_id=1, source_target_pairs={{0,64},{8,24},{16,80},{24,40},{32,96},{40,56},{48,112},{56,8},{64,... | collective-permute-start | bytes 1572872 | tf_op jit(solution)/shard_map/ppermute | solution.py:132
  31.1 37.0 %collective-permute-start.7 = (bf16[2,8,128,256]{3,2,1,0:T(8,128)(2,1)S(1)}, bf16[2,8,128,256]{3,2,1,0:T(8,128)(2,1)S(1)}, u32[]{:S(2)}, u32[]{:S(2)}) collective-permute-start(bf16[2,8,128,256]{3,2,1,0:T(8,128)(2,1)S(1)} %pad_maximum_fusion.g0), channel_id=1, source_target_pairs={{0,192},{8,56},{16,208},{24,8},{32,224},{40,24},{48,240},{56,40},{... | collective-permute-start | bytes 3145736 | tf_op jit(solution)/shard_map/ppermute | solution.py:136
  33.9 34.2 %collective-permute-start.6 = (bf16[2,8,128,256]{3,2,1,0:T(8,128)(2,1)S(1)}, bf16[2,8,128,256]{3,2,1,0:T(8,128)(2,1)S(1)}, u32[]{:S(2)}, u32[]{:S(2)}) collective-permute-start(bf16[2,8,128,256]{3,2,1,0:T(8,128)(2,1)S(1)} %pad_maximum_fusion.g0), channel_id=1, source_target_pairs={{0,128},{8,40},{16,144},{24,56},{32,160},{40,8},{48,176},{56,24},{... | collective-permute-start | bytes 3145736 | tf_op jit(solution)/shard_map/ppermute | solution.py:136
  34.3 33.9 %collective-permute-start.5 = (bf16[2,8,128,256]{3,2,1,0:T(8,128)(2,1)S(1)}, bf16[2,8,128,256]{3,2,1,0:T(8,128)(2,1)S(1)}, u32[]{:S(2)}, u32[]{:S(2)}) collective-permute-start(bf16[2,8,128,256]{3,2,1,0:T(8,128)(2,1)S(1)} %pad_maximum_fusion.g0), channel_id=1, source_target_pairs={{0,64},{8,24},{16,80},{24,40},{32,96},{40,56},{48,112},{56,8},{64,... | collective-permute-start | bytes 3145736 | tf_op jit(solution)/shard_map/ppermute | solution.py:136
  35.0 32.5 %collective-permute-start.2 = (bf16[2,128,1024]{2,1,0:T(8,128)(2,1)S(1)}, bf16[2,128,1024]{2,1,0:T(8,128)(2,1)S(1)}, u32[]{:S(2)}, u32[]{:S(2)}) collective-permute-start(bf16[2,128,1024]{2,1,0:T(8,128)(2,1)S(1)} %get-tuple-element.10), channel_id=1, source_target_pairs={{0,128},{8,40},{16,144},{24,56},{32,160},{40,8},{48,176},{56,24},{... | collective-permute-start | bytes 1572872 | tf_op jit(solution)/shard_map/ppermute | solution.py:132
  38.1 30.0 %collective-permute-start.3 = (bf16[2,128,1024]{2,1,0:T(8,128)(2,1)S(1)}, bf16[2,128,1024]{2,1,0:T(8,128)(2,1)S(1)}, u32[]{:S(2)}, u32[]{:S(2)}) collective-permute-start(bf16[2,128,1024]{2,1,0:T(8,128)(2,1)S(1)} %get-tuple-element.11), channel_id=1, source_target_pairs={{0,192},{8,56},{16,208},{24,8},{32,224},{40,24},{48,240},{56,40},{... | collective-permute-start | bytes 1572872 | tf_op jit(solution)/shard_map/ppermute | solution.py:132
  75.3 9.6 %collective-permute-start.8 = (bf16[4,256,256]{2,1,0:T(8,128)(2,1)S(1)}, bf16[4,256,256]{2,1,0:T(8,128)(2,1)S(1)}, u32[]{:S(2)}, u32[]{:S(2)}) collective-permute-start(bf16[4,256,256]{2,1,0:T(8,128)(2,1)S(1)} %get-tuple-element.18), channel_id=1, source_target_pairs={{0,16},{8,72},{16,32},{24,88},{32,48},{40,104},{48,0},{56,120},{64... | collective-permute-start | bytes 1572872 | tf_op jit(solution)/shard_map/ppermute | solution.py:151
  76.6 8.3 %collective-permute-start.10 = (bf16[4,256,256]{2,1,0:T(8,128)(2,1)S(1)}, bf16[4,256,256]{2,1,0:T(8,128)(2,1)S(1)}, u32[]{:S(2)}, u32[]{:S(2)}) collective-permute-start(bf16[4,256,256]{2,1,0:T(8,128)(2,1)S(1)} %get-tuple-element.19), channel_id=1, source_target_pairs={{0,48},{8,200},{16,0},{24,216},{32,16},{40,232},{48,32},{56,248},{... | collective-permute-start | bytes 1572872 | tf_op jit(solution)/shard_map/ppermute | solution.py:152
  85.3 14.5 %collective-permute-start.11 = (bf16[8,256,256]{2,1,0:T(8,128)(2,1)S(1)}, bf16[8,256,256]{2,1,0:T(8,128)(2,1)S(1)}, u32[]{:S(2)}, u32[]{:S(2)}) collective-permute-start(bf16[8,256,256]{2,1,0:T(8,128)(2,1)S(1)} %pad_maximum_fusion.2), channel_id=1, source_target_pairs={{0,48},{8,200},{16,0},{24,216},{32,16},{40,232},{48,32},{56,248},{... | collective-permute-start | bytes 3145736 | tf_op jit(solution)/shard_map/ppermute | solution.py:156
  88.2 15.2 %collective-permute-start.9 = (bf16[8,256,256]{2,1,0:T(8,128)(2,1)S(1)}, bf16[8,256,256]{2,1,0:T(8,128)(2,1)S(1)}, u32[]{:S(2)}, u32[]{:S(2)}) collective-permute-start(bf16[8,256,256]{2,1,0:T(8,128)(2,1)S(1)} %pad_maximum_fusion.1), channel_id=1, source_target_pairs={{0,16},{8,72},{16,32},{24,88},{32,48},{40,104},{48,0},{56,120},{64... | collective-permute-start | bytes 3145736 | tf_op jit(solution)/shard_map/ppermute | solution.py:155
  103.8 27.3 %copy-start.2 = (f32[256,256]{1,0:T(8,128)S(1)}, f32[256,256]{1,0:T(8,128)}, u32[]{:S(2)}) copy-start(f32[256,256]{1,0:T(8,128)} %param.7) | copy-start | bytes 786436
  103.9 27.3 %copy-start.3 = (f32[256,256]{1,0:T(8,128)S(1)}, f32[256,256]{1,0:T(8,128)}, u32[]{:S(2)}) copy-start(f32[256,256]{1,0:T(8,128)} %param.8) | copy-start | bytes 786436
  103.9 27.3 %copy-start.4 = (f32[256,256]{1,0:T(8,128)S(1)}, f32[256,256]{1,0:T(8,128)}, u32[]{:S(2)}) copy-start(f32[256,256]{1,0:T(8,128)} %param.9) | copy-start | bytes 786436
  166.2 6.4 %collective-permute-start.12 = (bf16[4,4,256,256]{3,2,1,0:T(8,128)(2,1)S(1)}, bf16[4,4,256,256]{3,2,1,0:T(8,128)(2,1)S(1)}, u32[]{:S(2)}, u32[]{:S(2)}) collective-permute-start(bf16[4,4,256,256]{3,2,1,0:T(8,128)(2,1)S(1)} %all_to_all.22.own), channel_id=1, source_target_pairs={{0,8},{8,0},{16,24},{24,16},{32,40},{40,32},{48,56},{56,48},{64,72... | collective-permute-start | bytes 6291464 | tf_op jit(solution)/shard_map/ppermute | solution.py:174

commit v3 on v2

--- a/solution.py
+++ b/solution.py
@@ -72,33 +72,42 @@
         outs[split][1] = peer[split]
 
 
-def product_kernel(rows, a0, a1, a2, a3, g0, g1, g2, g3, out, turned):
-    tokens = a0.shape[1]
-
-    @pl.when(pl.program_id(0) == 0)
-    def _():
-        for i, piece in enumerate((a0, a1, a2, a3)):
-            for core in range(2):
-                at = (2 * i + core) * tokens
-                turned[:, at : at + tokens] = piece[core].T
-
-    right = jnp.concatenate([piece[core, 0] for piece in (g0, g1, g2, g3) for core in range(2)], axis=0)
-    for reduce in range(SIDE):
-        out[reduce, 0] = jnp.dot(
-            turned[reduce * rows : (reduce + 1) * rows, :], right, preferred_element_type=jnp.float32
-        ).astype(out.dtype)
-
-
-def weights_kernel(own, peer, out):
-    _, _, core = place()
-    x = pl.program_id(0)
-    for of_core, (first, second) in enumerate(((own, peer), (peer, own))):
-
-        @pl.when(core == of_core)
-        def _():
-            for y in range(SIDE):
-                out[0, y, 0] = first[y, x]
-                out[0, y, 1] = second[x, y]
+def product_kernel(which, rows, a0, a1, a2, a3, g0, g1, g2, g3, *outs):
+    acts, grads = (a0, a1, a2, a3), (g0, g1, g2, g3)
+    panels = g0.shape[1]
+    here = lax.axis_index("tensor")
+    left = {
+        reduce: jnp.concatenate(
+            [piece[core, :, reduce * rows : (reduce + 1) * rows].T for piece in acts for core in range(2)], axis=1
+        )
+        for reduce in sorted({reduce for reduce, _ in which})
+    }
+    for (reduce, away), out in zip(which, outs):
+        for i, step in enumerate(away):
+            panel = lax.rem(here + step, panels)
+            right = jnp.concatenate([piece[core, panel] for piece in grads for core in range(2)], axis=0)
+            out[i] = jnp.dot(left[reduce], right, preferred_element_type=jnp.float32).astype(out.dtype)
+
+
+def weights_kernel(*refs):
+    *parts, out = refs
+    x, y, core = place()
+    panel_x = pl.program_id(0)
+    off_x = lax.rem(x + SIDE - panel_x, SIDE)
+    for of_core in range(2):
+        first, second = parts[SIDE * of_core :][:SIDE], parts[SIDE * (1 - of_core) :][:SIDE]
+
+        for case in range(SIDE):
+
+            @pl.when((core == of_core) & (y == case))
+            def _():
+                for at in range(SIDE):
+                    out[0, at, 0] = first[(case - at) % SIDE][off_x]
+
+            @pl.when((core == of_core) & (off_x == case))
+            def _():
+                for at in range(SIDE):
+                    out[0, at, 1] = second[case][lax.rem(y + SIDE - at, SIDE)]
 
 
 VMEM = pl.BlockSpec(memory_space=pltpu.VMEM)
@@ -110,7 +119,7 @@
         out_shape=out_shape,
         in_specs=[VMEM] * inputs,
         out_specs=jax.tree.map(lambda _: VMEM, out_shape),
-        compiler_params=pltpu.CompilerParams(vmem_limit_bytes=32 * 1024 * 1024),
+        compiler_params=pltpu.CompilerParams(vmem_limit_bytes=20 * 1024 * 1024),
     )
 
 
@@ -135,28 +144,33 @@
     both = jnp.stack([mine, lax.ppermute(mine, "dp", CORE_SWAP)])
     grads = [both] + [lax.ppermute(both, "dp", ring(i, 0)) for i in range(1, SIDE)]
 
-    parts = pl.pallas_call(
-        functools.partial(product_kernel, rows),
-        grid=(panels,),
-        out_shape=kept((SIDE, panels, rows, cols), jnp.bfloat16),
-        in_specs=[pl.BlockSpec((2, tokens, wide), lambda i: (0, 0, 0))] * SIDE
-        + [pl.BlockSpec((2, 1, tokens, cols), lambda i: (0, i, 0, 0))] * SIDE,
-        out_specs=pl.BlockSpec((SIDE, 1, rows, cols), lambda i: (0, i, 0, 0)),
-        scratch_shapes=[pltpu.VMEM((wide, 2 * SIDE * tokens), jnp.bfloat16)],
-        compiler_params=pltpu.CompilerParams(vmem_limit_bytes=40 * 1024 * 1024),
-    )(*acts, *grads)
-
-    half = panels // 2
+    def product(*which):
+        return mover(
+            functools.partial(product_kernel, which, rows),
+            [kept((len(away), rows, cols), jnp.bfloat16) for _, away in which],
+            2 * SIDE,
+        )(*acts, *grads)
+
+    far = tuple(range(panels // 2 - 1, panels // 2 + 2))
+    near = tuple(step for step in range(panels) if step not in far)
     f32 = jnp.float32
-    up = lax.ppermute(parts[2, :half], "dp", ring(1, 1))
-    down = lax.ppermute(parts[2, half:], "dp", ring(3, 1))
-    up_sum = (parts[1, :half].astype(f32) + up.astype(f32)).astype(jnp.bfloat16)
-    down_sum = (parts[3, half:].astype(f32) + down.astype(f32)).astype(jnp.bfloat16)
-    up = lax.ppermute(jnp.concatenate([up_sum, parts[1, half:]]), "dp", ring(1, 1))
-    down = lax.ppermute(jnp.concatenate([parts[3, :half], down_sum]), "dp", ring(3, 1))
-    line = (parts[0].astype(f32) + up.astype(f32) + down.astype(f32)).astype(jnp.bfloat16)
-
-    grad = jnp.sum(lax.all_to_all(line, "tensor", 0, 0).astype(f32), axis=0)
+    moved = [
+        [lax.ppermute(part, "dp", ring(i, 1)) for i, part in zip((2, 1, 3), product((2, away), (1, away), (3, away)))]
+        for away in (far, near)
+    ]
+    kept_parts = product((0, far), (0, near))
+
+    def line(at):
+        return sum((part.astype(f32) for part in moved[at]), kept_parts[at].astype(f32)).astype(jnp.bfloat16)
+
+    def along_tensor(part, step):
+        return lax.ppermute(part, "tensor", [(i, (i + step) % panels) for i in range(panels)])
+
+    line_far = line(0)
+    terms = [along_tensor(line_far[i], step) for i, step in enumerate(far)]
+    line_near = line(1)
+    terms += [along_tensor(line_near[i], step) for i, step in enumerate(near) if step]
+    grad = sum((term.astype(f32) for term in terms), line_near[0].astype(f32))
 
     new_first = 0.9 * first_moment + 0.1 * grad
     new_second = 0.999 * second_moment + 0.001 * grad * grad
@@ -165,21 +179,17 @@
     new_master = master * (1.0 - 0.05 * 0.1) - 0.05 * first_fix / (jnp.sqrt(second_fix) + 1e-08)
 
     own = new_master.astype(jnp.bfloat16)
-    own = lax.all_to_all(
-        jnp.broadcast_to(own, (SIDE, rows, cols)), "dp", 0, 0, axis_index_groups=groups(0)
-    )
-    own = lax.all_to_all(
-        jnp.broadcast_to(own, (SIDE, SIDE, rows, cols)), "dp", 0, 0, axis_index_groups=groups(1)
-    )
-    peer = lax.ppermute(own, "dp", CORE_SWAP)
+    line = jnp.stack([own] + [lax.ppermute(own, "dp", ring(i, 0)) for i in range(1, SIDE)])
+    own = [line] + [lax.ppermute(line, "dp", ring(i, 1)) for i in range(1, SIDE)]
+    peer = [lax.ppermute(part, "dp", CORE_SWAP) for part in own]
     weights = pl.pallas_call(
         weights_kernel,
         grid=(SIDE,),
         out_shape=kept((SIDE, SIDE, 2, rows, cols), jnp.bfloat16),
-        in_specs=[VMEM] * 2,
+        in_specs=[VMEM] * (2 * SIDE),
         out_specs=pl.BlockSpec((1, SIDE, 2, rows, cols), lambda i: (i, 0, 0, 0, 0)),
-        compiler_params=pltpu.CompilerParams(vmem_limit_bytes=32 * 1024 * 1024),
-    )(own, peer).reshape(width, cols)
+        compiler_params=pltpu.CompilerParams(vmem_limit_bytes=20 * 1024 * 1024),
+    )(*own, *peer).reshape(width, cols)
     return (new_master, new_first, new_second, weights)
 
 

time: 175 us -> 145 us (0.83)
  blocking collectives: 61 us -> 0 us
  starting transfers between devices: 27.3 us -> 55.7 us
  waiting for transfers between devices: 70.1 us -> 75.1 us
  Pallas kernels: 10.8 us -> 8.82 us
    all_to_all x3 -> x0, blocking collectives: 60.9 us -> none  [the longest x1 27.2 us: per_device(): grad = jnp.sum(lax.all_to_all(line, 'tensor', 0, 0).astype(f32), axis=0)]
    ppermute x5 -> x23, starting transfers between devices: 8.22 us -> 37.1 us  [the longest x4 14.6 us: per_device(): peer = [lax.ppermute(part, 'dp', CORE_SWAP) for part in own]]
    ppermute x5 -> x23, waiting for transfers between devices: 25.8 us -> 28.8 us  [the longest x6 13.6 us: per_device(): lax.ppermute(part, 'dp', ring(i, 1))]
    ppermute x3, waiting for transfers between devices: 29.8 us -> 31.8 us  [per_device(): lax.ppermute(chunks[i], 'dp', ring(i, 0))]
    pallas_call x1 -> x3, Pallas kernels: 7 us -> 5.01 us  [product(): mover(functools.partial(product_kernel, which, rows), [kept((len(away), r...]
  transfers between devices with their start and end apart: 14 -> 32, of which waited for: 9 -> 20; matrix products, arithmetic and copies ran while one was open for 1% -> 1% of each run, Pallas kernels for 1% -> 3%
where the time goes in v3:
time: 145 us
  waiting for transfers between devices  75.1 us (52%)
  starting transfers between devices  55.7 us (38%)
  Pallas kernels  8.82 us (6%)
  other arithmetic  2.87 us (2%)
  local copies, waits for them, and re-layouts  1.67 us (1%)
    ppermute x3, waiting for transfers between devices, per_device(): lax.ppermute(chunks[i], 'dp', ring(i, 0))  31.8 us
    ppermute x4, starting transfers between devices, per_device(): peer = [lax.ppermute(part, 'dp', CORE_SWAP) for part in own]  14.6 us
    all_to_all x1, waiting for transfers between devices, per_device(): lax.all_to_all(out_grads.reshape(panels, tokens, cols), 'tensor', 0, 0)  14.4 us
    ppermute x6, waiting for transfers between devices, per_device(): lax.ppermute(part, 'dp', ring(i, 1))  13.6 us
    all_to_all x1, starting transfers between devices, per_device(): lax.all_to_all(out_grads.reshape(panels, tokens, cols), 'tensor', 0, 0)  9.03 us
    ppermute x6, starting transfers between devices, per_device(): lax.ppermute(part, 'dp', ring(i, 1))  7.48 us
    ppermute x7, waiting for transfers between devices, along_tensor(): lax.ppermute(part, 'tensor', [(i, (i + step) % panels) for i in range(pan...  7.4 us
    ppermute x7, starting transfers between devices, along_tensor(): lax.ppermute(part, 'tensor', [(i, (i + step) % panels) for i in range(pan...  7.06 us
  transfers between devices with their start and end apart: 32, of which 20 were waited for; matrix products, arithmetic and copies ran while one was open for 1% of the time, Pallas kernels for 3%

profile of v3, /device:TPU:1, one launch (start us, length us, event | category | flops | bytes accessed | tf_op | source)
XLA Modules:
  0.0 145.0 jit_solution(10161165580351325316)
XLA Ops:
  0.6 9.0 %all-to-all-start = ((bf16[8,128,256]{2,1,0:T(8,128)(2,1)}), bf16[8,128,256]{2,1,0:T(8,128)(2,1)}, u32[]{:S(2)}, u32[]{:S(2)}) async-start(bf16[8,128,256]{2,1,0:T(8,128)(2,1)} %bitcast.28), calls=%async_computation | async-start | bytes 1048576 | tf_op jit(solution)/shard_map/all_to_all | solution.py:143
  9.7 1.6 %copy-done = bf16[128,8192]{1,0:T(8,128)(2,1)S(1)} copy-done((bf16[128,8192]{1,0:T(8,128)(2,1)S(1)}, bf16[128,8192]{1,0:T(8,128)(2,1)}, u32[]{:S(2)}) %copy-start) | copy-done | bytes 2097176
  11.3 1.1 shard_map.84
  12.4 1.0 collective-permute-start
  13.3 14.4 %all-to-all-done = bf16[8,128,256]{2,1,0:T(8,128)(2,1)} async-done(((bf16[8,128,256]{2,1,0:T(8,128)(2,1)}), bf16[8,128,256]{2,1,0:T(8,128)(2,1)}, u32[]{:S(2)}, u32[]{:S(2)}) %all-to-all-start) | async-done | bytes 524320 | tf_op jit(solution)/shard_map/all_to_all | solution.py:143
  27.7 0.5 collective-permute-start.4
  28.2 0.0 collective-permute-done.peer
  28.2 0.2 shard_map.85
  28.4 1.4 collective-permute-start.1
  29.8 0.1 collective-permute-done.4
  30.0 1.1 pad_maximum_fusion.g0
  31.1 1.4 collective-permute-start.5
  32.5 2.6 %collective-permute-start.6 = (bf16[2,8,128,256]{3,2,1,0:T(8,128)(2,1)S(1)}, bf16[2,8,128,256]{3,2,1,0:T(8,128)(2,1)S(1)}, u32[]{:S(2)}, u32[]{:S(2)}) collective-permute-start(bf16[2,8,128,256]{3,2,1,0:T(8,128)(2,1)S(1)} %pad_maximum_fusion.g0), channel_id=1, source_target_pairs={{0,128},{8,40},{16,144},{24,56},{32,160},{40,8},{48,176},{56,24},{... | collective-permute-start | bytes 3145736 | tf_op jit(solution)/shard_map/ppermute | solution.py:145
  35.1 1.1 collective-permute-start.7
  36.2 0.2 collective-permute-start.2
  36.4 1.7 %collective-permute-done.1.a1 = bf16[2,128,1024]{2,1,0:T(8,128)(2,1)S(1)} collective-permute-done((bf16[2,128,1024]{2,1,0:T(8,128)(2,1)S(1)}, bf16[2,128,1024]{2,1,0:T(8,128)(2,1)S(1)}, u32[]{:S(2)}, u32[]{:S(2)}) %collective-permute-start.1) | collective-permute-done | bytes 524320 | tf_op jit(solution)/shard_map/ppermute | solution.py:141
  38.1 1.5 %collective-permute-start.3 = (bf16[2,128,1024]{2,1,0:T(8,128)(2,1)S(1)}, bf16[2,128,1024]{2,1,0:T(8,128)(2,1)S(1)}, u32[]{:S(2)}, u32[]{:S(2)}) collective-permute-start(bf16[2,128,1024]{2,1,0:T(8,128)(2,1)S(1)} %get-tuple-element.19), channel_id=1, source_target_pairs={{0,192},{8,56},{16,208},{24,8},{32,224},{40,24},{48,240},{56,40},{... | collective-permute-start | bytes 1572872 | tf_op jit(solution)/shard_map/ppermute | solution.py:141
  39.6 27.8 %collective-permute-done.2.a2 = bf16[2,128,1024]{2,1,0:T(8,128)(2,1)S(1)} collective-permute-done((bf16[2,128,1024]{2,1,0:T(8,128)(2,1)S(1)}, bf16[2,128,1024]{2,1,0:T(8,128)(2,1)S(1)}, u32[]{:S(2)}, u32[]{:S(2)}) %collective-permute-start.2) | collective-permute-done | bytes 524320 | tf_op jit(solution)/shard_map/ppermute | solution.py:141
  67.4 2.2 %collective-permute-done.3.a3 = bf16[2,128,1024]{2,1,0:T(8,128)(2,1)S(1)} collective-permute-done((bf16[2,128,1024]{2,1,0:T(8,128)(2,1)S(1)}, bf16[2,128,1024]{2,1,0:T(8,128)(2,1)S(1)}, u32[]{:S(2)}, u32[]{:S(2)}) %collective-permute-start.3) | collective-permute-done | bytes 524320 | tf_op jit(solution)/shard_map/ppermute | solution.py:141
  69.6 0.0 collective-permute-done.5.g1
  69.6 1.5 %shard_map.88 = (bf16[3,256,256]{2,1,0:T(8,128)(2,1)S(1)}, bf16[3,256,256]{2,1,0:T(8,128)(2,1)S(1)}, bf16[3,256,256]{2,1,0:T(8,128)(2,1)S(1)}) custom-call(bf16[2,128,1024]{2,1,0:T(8,128)(2,1)S(1)} %get-tuple-element.16.a0, bf16[2,128,1024]{2,1,0:T(8,128)(2,1)S(1)} %collective-permute-done.1.a1, bf16[2,128,1024]{2,1,0:T(8,128)(2,1)S(1)} %collective-permute-done.2.a2, ...), custom_call_target="tpu_custom_call" | custom-call | tf_op jit(solution)/shard_map/pallas_call | solution.py:148
  71.1 2.8 %collective-permute-start.11 = (bf16[3,256,256]{2,1,0:T(8,128)(2,1)S(1)}, bf16[3,256,256]{2,1,0:T(8,128)(2,1)S(1)}, u32[]{:S(2)}, u32[]{:S(2)}) collective-permute-start(bf16[3,256,256]{2,1,0:T(8,128)(2,1)S(1)} %get-tuple-element.25), channel_id=1, source_target_pairs={{0,32},{8,136},{16,48},{24,152},{32,0},{40,168},{48,16},{56,184},{... | collective-permute-start | bytes 1179656 | tf_op jit(solution)/shard_map/ppermute | solution.py:158
  73.9 0.3 collective-permute-start.12
  74.3 2.4 %collective-permute-start.13 = (bf16[3,256,256]{2,1,0:T(8,128)(2,1)S(1)}, bf16[3,256,256]{2,1,0:T(8,128)(2,1)S(1)}, u32[]{:S(2)}, u32[]{:S(2)}) collective-permute-start(bf16[3,256,256]{2,1,0:T(8,128)(2,1)S(1)} %get-tuple-element.27), channel_id=1, source_target_pairs={{0,48},{8,200},{16,0},{24,216},{32,16},{40,232},{48,32},{56,248},{... | collective-permute-start | bytes 1179656 | tf_op jit(solution)/shard_map/ppermute | solution.py:158
  76.6 2.3 %shard_map.87 = (bf16[5,256,256]{2,1,0:T(8,128)(2,1)S(1)}, bf16[5,256,256]{2,1,0:T(8,128)(2,1)S(1)}, bf16[5,256,256]{2,1,0:T(8,128)(2,1)S(1)}) custom-call(bf16[2,128,1024]{2,1,0:T(8,128)(2,1)S(1)} %get-tuple-element.16.a0, bf16[2,128,1024]{2,1,0:T(8,128)(2,1)S(1)} %collective-permute-done.1.a1, bf16[2,128,1024]{2,1,0:T(8,128)(2,1)S(1)} %collective-permute-done.2.a2, ...), custom_call_target="tpu_custom_call" | custom-call | tf_op jit(solution)/shard_map/pallas_call | solution.py:148
  78.9 0.1 collective-permute-start.10
  79.0 0.9 collective-permute-start.8
  79.9 1.0 collective-permute-start.9
  80.9 1.3 shard_map.86
  82.2 1.7 %collective-permute-done.12 = bf16[3,256,256]{2,1,0:T(8,128)(2,1)S(1)} collective-permute-done((bf16[3,256,256]{2,1,0:T(8,128)(2,1)S(1)}, bf16[3,256,256]{2,1,0:T(8,128)(2,1)S(1)}, u32[]{:S(2)}, u32[]{:S(2)}) %collective-permute-start.12) | collective-permute-done | bytes 393248 | tf_op jit(solution)/shard_map/ppermute | solution.py:158
  83.8 0.1 collective-permute-done.13
  83.9 0.2 add_convert_fusion.1
  84.2 0.1 collective-permute-start.14
  84.3 1.6 %collective-permute-start.15 = (bf16[256,256]{1,0:T(8,128)(2,1)S(1)}, bf16[256,256]{1,0:T(8,128)(2,1)S(1)}, u32[]{:S(2)}, u32[]{:S(2)}) collective-permute-start(bf16[256,256]{1,0:T(8,128)(2,1)S(1)} %get-tuple-element.38), channel_id=1, source_target_pairs={{0,4},{1,5},{2,6},{3,7},{4,0},{5,1},{6,2},{7,3},{8,12},{9,13},{10,... | collective-permute-start | bytes 393224 | tf_op jit(solution)/shard_map/ppermute | solution.py:167
  85.9 5.1 %collective-permute-done.10 = bf16[5,256,256]{2,1,0:T(8,128)(2,1)S(1)} collective-permute-done((bf16[5,256,256]{2,1,0:T(8,128)(2,1)S(1)}, bf16[5,256,256]{2,1,0:T(8,128)(2,1)S(1)}, u32[]{:S(2)}, u32[]{:S(2)}) %collective-permute-start.10) | collective-permute-done | bytes 655392 | tf_op jit(solution)/shard_map/ppermute | solution.py:158
  91.0 0.3 collective-permute-start.16
  91.2 6.7 %collective-permute-done.9 = bf16[5,256,256]{2,1,0:T(8,128)(2,1)S(1)} collective-permute-done((bf16[5,256,256]{2,1,0:T(8,128)(2,1)S(1)}, bf16[5,256,256]{2,1,0:T(8,128)(2,1)S(1)}, u32[]{:S(2)}, u32[]{:S(2)}) %collective-permute-start.9) | collective-permute-done | bytes 655392 | tf_op jit(solution)/shard_map/ppermute | solution.py:158
  97.9 0.3 add_convert_fusion
  98.3 0.4 collective-permute-start.17
  98.7 3.6 %collective-permute-start.19 = (bf16[256,256]{1,0:T(8,128)(2,1)S(1)}, bf16[256,256]{1,0:T(8,128)(2,1)S(1)}, u32[]{:S(2)}, u32[]{:S(2)}) collective-permute-start(bf16[256,256]{1,0:T(8,128)(2,1)S(1)} %get-tuple-element.34), channel_id=1, source_target_pairs={{0,6},{1,7},{2,0},{3,1},{4,2},{5,3},{6,4},{7,5},{8,14},{9,15},{10,... | collective-permute-start | bytes 393224 | tf_op jit(solution)/shard_map/ppermute | solution.py:167
  102.3 1.2 collective-permute-start.20
  103.4 0.7 collective-permute-done.17
  104.1 2.0 %collective-permute-done.18 = bf16[256,256]{1,0:T(8,128)(2,1)S(1)} collective-permute-done((bf16[256,256]{1,0:T(8,128)(2,1)S(1)}, bf16[256,256]{1,0:T(8,128)(2,1)S(1)}, u32[]{:S(2)}, u32[]{:S(2)}) %collective-permute-start.18) | collective-permute-done | bytes 131104 | tf_op jit(solution)/shard_map/ppermute | solution.py:167
  106.1 1.7 %collective-permute-done.19 = bf16[256,256]{1,0:T(8,128)(2,1)S(1)} collective-permute-done((bf16[256,256]{1,0:T(8,128)(2,1)S(1)}, bf16[256,256]{1,0:T(8,128)(2,1)S(1)}, u32[]{:S(2)}, u32[]{:S(2)}) %collective-permute-start.19) | collective-permute-done | bytes 131104 | tf_op jit(solution)/shard_map/ppermute | solution.py:167
  107.9 3.0 %collective-permute-done.20 = bf16[256,256]{1,0:T(8,128)(2,1)S(1)} collective-permute-done((bf16[256,256]{1,0:T(8,128)(2,1)S(1)}, bf16[256,256]{1,0:T(8,128)(2,1)S(1)}, u32[]{:S(2)}, u32[]{:S(2)}) %collective-permute-start.20) | collective-permute-done | bytes 131104 | tf_op jit(solution)/shard_map/ppermute | solution.py:167
  110.8 1.1 fusion.7
  112.0 1.0 collective-permute-start.21
  112.9 2.6 %collective-permute-start.22 = (bf16[256,256]{1,0:T(8,128)(2,1)S(1)}, bf16[256,256]{1,0:T(8,128)(2,1)S(1)}, u32[]{:S(2)}, u32[]{:S(2)}) collective-permute-start(bf16[256,256]{1,0:T(8,128)(2,1)S(1)} %get-tuple-element.28), channel_id=1, source_target_pairs={{0,128},{8,40},{16,144},{24,56},{32,160},{40,8},{48,176},{56,24},{... | collective-permute-start | bytes 393224 | tf_op jit(solution)/shard_map/ppermute | solution.py:182
  115.5 1.0 collective-permute-start.23
  116.5 0.5 collective-permute-done.21
  117.0 2.3 %collective-permute-done.22 = bf16[256,256]{1,0:T(8,128)(2,1)S(1)} collective-permute-done((bf16[256,256]{1,0:T(8,128)(2,1)S(1)}, bf16[256,256]{1,0:T(8,128)(2,1)S(1)}, u32[]{:S(2)}, u32[]{:S(2)}) %collective-permute-start.22) | collective-permute-done | bytes 131104 | tf_op jit(solution)/shard_map/ppermute | solution.py:182
  119.3 0.4 collective-permute-done.23
  119.6 0.1 pad_maximum_fusion.1.refs_0_
  119.7 0.3 collective-permute-start.24
  120.0 3.2 %collective-permute-start.25 = (bf16[4,256,256]{2,1,0:T(8,128)(2,1)S(1)}, bf16[4,256,256]{2,1,0:T(8,128)(2,1)S(1)}, u32[]{:S(2)}, u32[]{:S(2)}) collective-permute-start(bf16[4,256,256]{2,1,0:T(8,128)(2,1)S(1)} %pad_maximum_fusion.1.refs_0_), channel_id=1, source_target_pairs={{0,32},{8,136},{16,48},{24,152},{32,0},{40,168},{48,16},{56,184},{... | collective-permute-start | bytes 1572872 | tf_op jit(solution)/shard_map/ppermute | solution.py:183
  123.2 5.5 %collective-permute-start.27 = (bf16[4,256,256]{2,1,0:T(8,128)(2,1)S(1)}, bf16[4,256,256]{2,1,0:T(8,128)(2,1)S(1)}, u32[]{:S(2)}, u32[]{:S(2)}) collective-permute-start(bf16[4,256,256]{2,1,0:T(8,128)(2,1)S(1)} %pad_maximum_fusion.1.refs_0_), channel_id=1, source_target_pairs={{0,8},{8,0},{16,24},{24,16},{32,40},{40,32},{48,56},{56,48},{64,72... | collective-permute-start | bytes 1572872 | tf_op jit(solution)/shard_map/ppermute | solution.py:184
  128.7 0.6 collective-permute-done.24.refs_1_
  129.3 4.5 %collective-permute-start.28 = (bf16[4,256,256]{2,1,0:T(8,128)(2,1)S(1)}, bf16[4,256,256]{2,1,0:T(8,128)(2,1)S(1)}, u32[]{:S(2)}, u32[]{:S(2)}) collective-permute-start(bf16[4,256,256]{2,1,0:T(8,128)(2,1)S(1)} %collective-permute-done.24.refs_1_), channel_id=1, source_target_pairs={{0,8},{8,0},{16,24},{24,16},{32,40},{40,32},{48,56},{56,48},{64,72... | collective-permute-start | bytes 1572872 | tf_op jit(solution)/shard_map/ppermute | solution.py:184
  133.8 1.9 %collective-permute-done.25.refs_2_ = bf16[4,256,256]{2,1,0:T(8,128)(2,1)S(1)} collective-permute-done((bf16[4,256,256]{2,1,0:T(8,128)(2,1)S(1)}, bf16[4,256,256]{2,1,0:T(8,128)(2,1)S(1)}, u32[]{:S(2)}, u32[]{:S(2)}) %collective-permute-start.25) | collective-permute-done | bytes 524320 | tf_op jit(solution)/shard_map/ppermute | solution.py:183
  135.7 4.5 %collective-permute-start.29 = (bf16[4,256,256]{2,1,0:T(8,128)(2,1)S(1)}, bf16[4,256,256]{2,1,0:T(8,128)(2,1)S(1)}, u32[]{:S(2)}, u32[]{:S(2)}) collective-permute-start(bf16[4,256,256]{2,1,0:T(8,128)(2,1)S(1)} %collective-permute-done.25.refs_2_), channel_id=1, source_target_pairs={{0,8},{8,0},{16,24},{24,16},{32,40},{40,32},{48,56},{56,48},{64,72... | collective-permute-start | bytes 1572872 | tf_op jit(solution)/shard_map/ppermute | solution.py:184
  140.2 0.1 collective-permute-start.30
  140.3 1.4 collective-permute-done.29.refs_6_
  141.7 0.7 collective-permute-done.30.refs_7_
  142.5 2.5 %shard_map.89 = bf16[4,4,2,256,256]{4,3,2,1,0:T(8,128)(2,1)} custom-call(bf16[4,256,256]{2,1,0:T(8,128)(2,1)S(1)} %pad_maximum_fusion.1.refs_0_, bf16[4,256,256]{2,1,0:T(8,128)(2,1)S(1)} %collective-permute-done.24.refs_1_, bf16[4,256,256]{2,1,0:T(8,128)(2,1)S(1)} %collective-permute-done.25.refs_2_, ...), custom_call_target="tpu_custom_call" | custom-call | tf_op jit(solution)/shard_map/pallas_call | solution.py:185
  (23 shorter events, 0.1 us)
Async XLA Ops:
  0.6 27.1 %all-to-all-start = ((bf16[8,128,256]{2,1,0:T(8,128)(2,1)}), bf16[8,128,256]{2,1,0:T(8,128)(2,1)}, u32[]{:S(2)}, u32[]{:S(2)}) async-start(bf16[8,128,256]{2,1,0:T(8,128)(2,1)} %bitcast.28), calls=%async_computation | async-start | bytes 1048576 | tf_op jit(solution)/shard_map/all_to_all | solution.py:143
  9.7 1.6 %copy-start = (bf16[128,8192]{1,0:T(8,128)(2,1)S(1)}, bf16[128,8192]{1,0:T(8,128)(2,1)}, u32[]{:S(2)}) copy-start(bf16[128,8192]{1,0:T(8,128)(2,1)} %acts.3) | copy-start | bytes 6291460
  11.2 17.0 %copy-start.1 = (bf16[128,8192]{1,0:T(8,128)(2,1)S(1)}, bf16[128,8192]{1,0:T(8,128)(2,1)}, u32[]{:S(2)}) copy-start(bf16[128,8192]{1,0:T(8,128)(2,1)} %acts.3) | copy-start | bytes 6291460
  12.4 15.9 %collective-permute-start = (bf16[4,128,1024]{2,1,0:T(8,128)(2,1)}, bf16[4,128,1024]{2,1,0:T(8,128)(2,1)S(1)}, u32[]{:S(2)}, u32[]{:S(2)}) collective-permute-start(bf16[4,128,1024]{2,1,0:T(8,128)(2,1)} %shard_map.84), channel_id=1, source_target_pairs={{0,8},{8,0},{16,24},{24,16},{32,40},{40,32},{48,56},{56,48},{64,72... | collective-permute-start | bytes 3145736 | tf_op jit(solution)/shard_map/ppermute | solution.py:136
  27.7 2.2 %collective-permute-start.4 = (bf16[8,128,256]{2,1,0:T(8,128)(2,1)}, bf16[8,128,256]{2,1,0:T(8,128)(2,1)S(1)}, u32[]{:S(2)}, u32[]{:S(2)}) collective-permute-start(bf16[8,128,256]{2,1,0:T(8,128)(2,1)} %all-to-all-done), channel_id=1, source_target_pairs={{0,8},{8,0},{16,24},{24,16},{32,40},{40,32},{48,56},{56,48},{64,72... | collective-permute-start | bytes 1572872 | tf_op jit(solution)/shard_map/ppermute | solution.py:144
  28.4 9.7 %collective-permute-start.1 = (bf16[2,128,1024]{2,1,0:T(8,128)(2,1)S(1)}, bf16[2,128,1024]{2,1,0:T(8,128)(2,1)S(1)}, u32[]{:S(2)}, u32[]{:S(2)}) collective-permute-start(bf16[2,128,1024]{2,1,0:T(8,128)(2,1)S(1)} %get-tuple-element.17), channel_id=1, source_target_pairs={{0,64},{8,24},{16,80},{24,40},{32,96},{40,56},{48,112},{56,8},{64,... | collective-permute-start | bytes 1572872 | tf_op jit(solution)/shard_map/ppermute | solution.py:141
  31.1 38.5 %collective-permute-start.5 = (bf16[2,8,128,256]{3,2,1,0:T(8,128)(2,1)S(1)}, bf16[2,8,128,256]{3,2,1,0:T(8,128)(2,1)S(1)}, u32[]{:S(2)}, u32[]{:S(2)}) collective-permute-start(bf16[2,8,128,256]{3,2,1,0:T(8,128)(2,1)S(1)} %pad_maximum_fusion.g0), channel_id=1, source_target_pairs={{0,64},{8,24},{16,80},{24,40},{32,96},{40,56},{48,112},{56,8},{64,... | collective-permute-start | bytes 3145736 | tf_op jit(solution)/shard_map/ppermute | solution.py:145
  32.5 37.2 %collective-permute-start.6 = (bf16[2,8,128,256]{3,2,1,0:T(8,128)(2,1)S(1)}, bf16[2,8,128,256]{3,2,1,0:T(8,128)(2,1)S(1)}, u32[]{:S(2)}, u32[]{:S(2)}) collective-permute-start(bf16[2,8,128,256]{3,2,1,0:T(8,128)(2,1)S(1)} %pad_maximum_fusion.g0), channel_id=1, source_target_pairs={{0,128},{8,40},{16,144},{24,56},{32,160},{40,8},{48,176},{56,24},{... | collective-permute-start | bytes 3145736 | tf_op jit(solution)/shard_map/ppermute | solution.py:145
  35.1 34.5 %collective-permute-start.7 = (bf16[2,8,128,256]{3,2,1,0:T(8,128)(2,1)S(1)}, bf16[2,8,128,256]{3,2,1,0:T(8,128)(2,1)S(1)}, u32[]{:S(2)}, u32[]{:S(2)}) collective-permute-start(bf16[2,8,128,256]{3,2,1,0:T(8,128)(2,1)S(1)} %pad_maximum_fusion.g0), channel_id=1, source_target_pairs={{0,192},{8,56},{16,208},{24,8},{32,224},{40,24},{48,240},{56,40},{... | collective-permute-start | bytes 3145736 | tf_op jit(solution)/shard_map/ppermute | solution.py:145
  36.2 31.2 %collective-permute-start.2 = (bf16[2,128,1024]{2,1,0:T(8,128)(2,1)S(1)}, bf16[2,128,1024]{2,1,0:T(8,128)(2,1)S(1)}, u32[]{:S(2)}, u32[]{:S(2)}) collective-permute-start(bf16[2,128,1024]{2,1,0:T(8,128)(2,1)S(1)} %get-tuple-element.18), channel_id=1, source_target_pairs={{0,128},{8,40},{16,144},{24,56},{32,160},{40,8},{48,176},{56,24},{... | collective-permute-start | bytes 1572872 | tf_op jit(solution)/shard_map/ppermute | solution.py:141
  38.1 31.5 %collective-permute-start.3 = (bf16[2,128,1024]{2,1,0:T(8,128)(2,1)S(1)}, bf16[2,128,1024]{2,1,0:T(8,128)(2,1)S(1)}, u32[]{:S(2)}, u32[]{:S(2)}) collective-permute-start(bf16[2,128,1024]{2,1,0:T(8,128)(2,1)S(1)} %get-tuple-element.19), channel_id=1, source_target_pairs={{0,192},{8,56},{16,208},{24,8},{32,224},{40,24},{48,240},{56,40},{... | collective-permute-start | bytes 1572872 | tf_op jit(solution)/shard_map/ppermute | solution.py:141
  71.1 8.8 %collective-permute-start.11 = (bf16[3,256,256]{2,1,0:T(8,128)(2,1)S(1)}, bf16[3,256,256]{2,1,0:T(8,128)(2,1)S(1)}, u32[]{:S(2)}, u32[]{:S(2)}) collective-permute-start(bf16[3,256,256]{2,1,0:T(8,128)(2,1)S(1)} %get-tuple-element.25), channel_id=1, source_target_pairs={{0,32},{8,136},{16,48},{24,152},{32,0},{40,168},{48,16},{56,184},{... | collective-permute-start | bytes 1179656 | tf_op jit(solution)/shard_map/ppermute | solution.py:158
  73.9 9.9 %collective-permute-start.12 = (bf16[3,256,256]{2,1,0:T(8,128)(2,1)S(1)}, bf16[3,256,256]{2,1,0:T(8,128)(2,1)S(1)}, u32[]{:S(2)}, u32[]{:S(2)}) collective-permute-start(bf16[3,256,256]{2,1,0:T(8,128)(2,1)S(1)} %get-tuple-element.26), channel_id=1, source_target_pairs={{0,16},{8,72},{16,32},{24,88},{32,48},{40,104},{48,0},{56,120},{64... | collective-permute-start | bytes 1179656 | tf_op jit(solution)/shard_map/ppermute | solution.py:158
  74.3 9.7 %collective-permute-start.13 = (bf16[3,256,256]{2,1,0:T(8,128)(2,1)S(1)}, bf16[3,256,256]{2,1,0:T(8,128)(2,1)S(1)}, u32[]{:S(2)}, u32[]{:S(2)}) collective-permute-start(bf16[3,256,256]{2,1,0:T(8,128)(2,1)S(1)} %get-tuple-element.27), channel_id=1, source_target_pairs={{0,48},{8,200},{16,0},{24,216},{32,16},{40,232},{48,32},{56,248},{... | collective-permute-start | bytes 1179656 | tf_op jit(solution)/shard_map/ppermute | solution.py:158
  78.9 12.1 %collective-permute-start.10 = (bf16[5,256,256]{2,1,0:T(8,128)(2,1)S(1)}, bf16[5,256,256]{2,1,0:T(8,128)(2,1)S(1)}, u32[]{:S(2)}, u32[]{:S(2)}) collective-permute-start(bf16[5,256,256]{2,1,0:T(8,128)(2,1)S(1)} %get-tuple-element.23), channel_id=1, source_target_pairs={{0,48},{8,200},{16,0},{24,216},{32,16},{40,232},{48,32},{56,248},{... | collective-permute-start | bytes 1966088 | tf_op jit(solution)/shard_map/ppermute | solution.py:158
  79.0 12.2 %collective-permute-start.8 = (bf16[5,256,256]{2,1,0:T(8,128)(2,1)S(1)}, bf16[5,256,256]{2,1,0:T(8,128)(2,1)S(1)}, u32[]{:S(2)}, u32[]{:S(2)}) collective-permute-start(bf16[5,256,256]{2,1,0:T(8,128)(2,1)S(1)} %get-tuple-element.21), channel_id=1, source_target_pairs={{0,32},{8,136},{16,48},{24,152},{32,0},{40,168},{48,16},{56,184},{... | collective-permute-start | bytes 1966088 | tf_op jit(solution)/shard_map/ppermute | solution.py:158
  79.9 18.0 %collective-permute-start.9 = (bf16[5,256,256]{2,1,0:T(8,128)(2,1)S(1)}, bf16[5,256,256]{2,1,0:T(8,128)(2,1)S(1)}, u32[]{:S(2)}, u32[]{:S(2)}) collective-permute-start(bf16[5,256,256]{2,1,0:T(8,128)(2,1)S(1)} %get-tuple-element.22), channel_id=1, source_target_pairs={{0,16},{8,72},{16,32},{24,88},{32,48},{40,104},{48,0},{56,120},{64... | collective-permute-start | bytes 1966088 | tf_op jit(solution)/shard_map/ppermute | solution.py:158
  84.2 14.5 %collective-permute-start.14 = (bf16[256,256]{1,0:T(8,128)(2,1)S(1)}, bf16[256,256]{1,0:T(8,128)(2,1)S(1)}, u32[]{:S(2)}, u32[]{:S(2)}) collective-permute-start(bf16[256,256]{1,0:T(8,128)(2,1)S(1)} %get-tuple-element.36), channel_id=1, source_target_pairs={{0,3},{1,4},{2,5},{3,6},{4,7},{5,0},{6,1},{7,2},{8,11},{9,12},{10,... | collective-permute-start | bytes 393224 | tf_op jit(solution)/shard_map/ppermute | solution.py:167
  84.3 18.0 %collective-permute-start.15 = (bf16[256,256]{1,0:T(8,128)(2,1)S(1)}, bf16[256,256]{1,0:T(8,128)(2,1)S(1)}, u32[]{:S(2)}, u32[]{:S(2)}) collective-permute-start(bf16[256,256]{1,0:T(8,128)(2,1)S(1)} %get-tuple-element.38), channel_id=1, source_target_pairs={{0,4},{1,5},{2,6},{3,7},{4,0},{5,1},{6,2},{7,3},{8,12},{9,13},{10,... | collective-permute-start | bytes 393224 | tf_op jit(solution)/shard_map/ppermute | solution.py:167
  91.0 12.5 %collective-permute-start.16 = (bf16[256,256]{1,0:T(8,128)(2,1)S(1)}, bf16[256,256]{1,0:T(8,128)(2,1)S(1)}, u32[]{:S(2)}, u32[]{:S(2)}) collective-permute-start(bf16[256,256]{1,0:T(8,128)(2,1)S(1)} %get-tuple-element.37), channel_id=1, source_target_pairs={{0,5},{1,6},{2,7},{3,0},{4,1},{5,2},{6,3},{7,4},{8,13},{9,14},{10,... | collective-permute-start | bytes 393224 | tf_op jit(solution)/shard_map/ppermute | solution.py:167
  97.9 12.9 %copy-start.2 = (f32[256,256]{1,0:T(8,128)S(1)}, f32[256,256]{1,0:T(8,128)}, u32[]{:S(2)}) copy-start(f32[256,256]{1,0:T(8,128)} %param.7) | copy-start | bytes 786436
  97.9 12.9 %copy-start.3 = (f32[256,256]{1,0:T(8,128)S(1)}, f32[256,256]{1,0:T(8,128)}, u32[]{:S(2)}) copy-start(f32[256,256]{1,0:T(8,128)} %param.8) | copy-start | bytes 786436
  97.9 12.9 %copy-start.4 = (f32[256,256]{1,0:T(8,128)S(1)}, f32[256,256]{1,0:T(8,128)}, u32[]{:S(2)}) copy-start(f32[256,256]{1,0:T(8,128)} %param.9) | copy-start | bytes 786436
  98.3 5.8 %collective-permute-start.17 = (bf16[256,256]{1,0:T(8,128)(2,1)S(1)}, bf16[256,256]{1,0:T(8,128)(2,1)S(1)}, u32[]{:S(2)}, u32[]{:S(2)}) collective-permute-start(bf16[256,256]{1,0:T(8,128)(2,1)S(1)} %get-tuple-element.32), channel_id=1, source_target_pairs={{0,1},{1,2},{2,3},{3,4},{4,5},{5,6},{6,7},{7,0},{8,9},{9,10},{10,1... | collective-permute-start | bytes 393224 | tf_op jit(solution)/shard_map/ppermute | solution.py:167
  98.7 7.4 %collective-permute-start.18 = (bf16[256,256]{1,0:T(8,128)(2,1)S(1)}, bf16[256,256]{1,0:T(8,128)(2,1)S(1)}, u32[]{:S(2)}, u32[]{:S(2)}) collective-permute-start(bf16[256,256]{1,0:T(8,128)(2,1)S(1)} %get-tuple-element.35), channel_id=1, source_target_pairs={{0,2},{1,3},{2,4},{3,5},{4,6},{5,7},{6,0},{7,1},{8,10},{9,11},{10,... | collective-permute-start | bytes 393224 | tf_op jit(solution)/shard_map/ppermute | solution.py:167
  98.7 9.2 %collective-permute-start.19 = (bf16[256,256]{1,0:T(8,128)(2,1)S(1)}, bf16[256,256]{1,0:T(8,128)(2,1)S(1)}, u32[]{:S(2)}, u32[]{:S(2)}) collective-permute-start(bf16[256,256]{1,0:T(8,128)(2,1)S(1)} %get-tuple-element.34), channel_id=1, source_target_pairs={{0,6},{1,7},{2,0},{3,1},{4,2},{5,3},{6,4},{7,5},{8,14},{9,15},{10,... | collective-permute-start | bytes 393224 | tf_op jit(solution)/shard_map/ppermute | solution.py:167
  102.3 8.6 %collective-permute-start.20 = (bf16[256,256]{1,0:T(8,128)(2,1)S(1)}, bf16[256,256]{1,0:T(8,128)(2,1)S(1)}, u32[]{:S(2)}, u32[]{:S(2)}) collective-permute-start(bf16[256,256]{1,0:T(8,128)(2,1)S(1)} %get-tuple-element.33), channel_id=1, source_target_pairs={{0,7},{1,0},{2,1},{3,2},{4,3},{5,4},{6,5},{7,6},{8,15},{9,8},{10,9... | collective-permute-start | bytes 393224 | tf_op jit(solution)/shard_map/ppermute | solution.py:167
  112.0 5.0 %collective-permute-start.21 = (bf16[256,256]{1,0:T(8,128)(2,1)S(1)}, bf16[256,256]{1,0:T(8,128)(2,1)S(1)}, u32[]{:S(2)}, u32[]{:S(2)}) collective-permute-start(bf16[256,256]{1,0:T(8,128)(2,1)S(1)} %get-tuple-element.28), channel_id=1, source_target_pairs={{0,64},{8,24},{16,80},{24,40},{32,96},{40,56},{48,112},{56,8},{64,... | collective-permute-start | bytes 393224 | tf_op jit(solution)/shard_map/ppermute | solution.py:182
  112.9 6.3 %collective-permute-start.22 = (bf16[256,256]{1,0:T(8,128)(2,1)S(1)}, bf16[256,256]{1,0:T(8,128)(2,1)S(1)}, u32[]{:S(2)}, u32[]{:S(2)}) collective-permute-start(bf16[256,256]{1,0:T(8,128)(2,1)S(1)} %get-tuple-element.28), channel_id=1, source_target_pairs={{0,128},{8,40},{16,144},{24,56},{32,160},{40,8},{48,176},{56,24},{... | collective-permute-start | bytes 393224 | tf_op jit(solution)/shard_map/ppermute | solution.py:182
  115.5 4.1 %collective-permute-start.23 = (bf16[256,256]{1,0:T(8,128)(2,1)S(1)}, bf16[256,256]{1,0:T(8,128)(2,1)S(1)}, u32[]{:S(2)}, u32[]{:S(2)}) collective-permute-start(bf16[256,256]{1,0:T(8,128)(2,1)S(1)} %get-tuple-element.28), channel_id=1, source_target_pairs={{0,192},{8,56},{16,208},{24,8},{32,224},{40,24},{48,240},{56,40},{... | collective-permute-start | bytes 393224 | tf_op jit(solution)/shard_map/ppermute | solution.py:182
  119.7 9.6 %collective-permute-start.24 = (bf16[4,256,256]{2,1,0:T(8,128)(2,1)S(1)}, bf16[4,256,256]{2,1,0:T(8,128)(2,1)S(1)}, u32[]{:S(2)}, u32[]{:S(2)}) collective-permute-start(bf16[4,256,256]{2,1,0:T(8,128)(2,1)S(1)} %pad_maximum_fusion.1.refs_0_), channel_id=1, source_target_pairs={{0,16},{8,72},{16,32},{24,88},{32,48},{40,104},{48,0},{56,120},{64... | collective-permute-start | bytes 1572872 | tf_op jit(solution)/shard_map/ppermute | solution.py:183
  120.0 15.7 %collective-permute-start.25 = (bf16[4,256,256]{2,1,0:T(8,128)(2,1)S(1)}, bf16[4,256,256]{2,1,0:T(8,128)(2,1)S(1)}, u32[]{:S(2)}, u32[]{:S(2)}) collective-permute-start(bf16[4,256,256]{2,1,0:T(8,128)(2,1)S(1)} %pad_maximum_fusion.1.refs_0_), channel_id=1, source_target_pairs={{0,32},{8,136},{16,48},{24,152},{32,0},{40,168},{48,16},{56,184},{... | collective-permute-start | bytes 1572872 | tf_op jit(solution)/shard_map/ppermute | solution.py:183
  123.2 17.0 %collective-permute-start.26 = (bf16[4,256,256]{2,1,0:T(8,128)(2,1)S(1)}, bf16[4,256,256]{2,1,0:T(8,128)(2,1)S(1)}, u32[]{:S(2)}, u32[]{:S(2)}) collective-permute-start(bf16[4,256,256]{2,1,0:T(8,128)(2,1)S(1)} %pad_maximum_fusion.1.refs_0_), channel_id=1, source_target_pairs={{0,48},{8,200},{16,0},{24,216},{32,16},{40,232},{48,32},{56,248},{... | collective-permute-start | bytes 1572872 | tf_op jit(solution)/shard_map/ppermute | solution.py:183
  123.2 17.1 %collective-permute-start.27 = (bf16[4,256,256]{2,1,0:T(8,128)(2,1)S(1)}, bf16[4,256,256]{2,1,0:T(8,128)(2,1)S(1)}, u32[]{:S(2)}, u32[]{:S(2)}) collective-permute-start(bf16[4,256,256]{2,1,0:T(8,128)(2,1)S(1)} %pad_maximum_fusion.1.refs_0_), channel_id=1, source_target_pairs={{0,8},{8,0},{16,24},{24,16},{32,40},{40,32},{48,56},{56,48},{64,72... | collective-permute-start | bytes 1572872 | tf_op jit(solution)/shard_map/ppermute | solution.py:184
  129.3 11.0 %collective-permute-start.28 = (bf16[4,256,256]{2,1,0:T(8,128)(2,1)S(1)}, bf16[4,256,256]{2,1,0:T(8,128)(2,1)S(1)}, u32[]{:S(2)}, u32[]{:S(2)}) collective-permute-start(bf16[4,256,256]{2,1,0:T(8,128)(2,1)S(1)} %collective-permute-done.24.refs_1_), channel_id=1, source_target_pairs={{0,8},{8,0},{16,24},{24,16},{32,40},{40,32},{48,56},{56,48},{64,72... | collective-permute-start | bytes 1572872 | tf_op jit(solution)/shard_map/ppermute | solution.py:184
  135.7 6.1 %collective-permute-start.29 = (bf16[4,256,256]{2,1,0:T(8,128)(2,1)S(1)}, bf16[4,256,256]{2,1,0:T(8,128)(2,1)S(1)}, u32[]{:S(2)}, u32[]{:S(2)}) collective-permute-start(bf16[4,256,256]{2,1,0:T(8,128)(2,1)S(1)} %collective-permute-done.25.refs_2_), channel_id=1, source_target_pairs={{0,8},{8,0},{16,24},{24,16},{32,40},{40,32},{48,56},{56,48},{64,72... | collective-permute-start | bytes 1572872 | tf_op jit(solution)/shard_map/ppermute | solution.py:184
  140.2 2.3 %collective-permute-start.30 = (bf16[4,256,256]{2,1,0:T(8,128)(2,1)S(1)}, bf16[4,256,256]{2,1,0:T(8,128)(2,1)S(1)}, u32[]{:S(2)}, u32[]{:S(2)}) collective-permute-start(bf16[4,256,256]{2,1,0:T(8,128)(2,1)S(1)} %collective-permute-done.26.refs_3_), channel_id=1, source_target_pairs={{0,8},{8,0},{16,24},{24,16},{32,40},{40,32},{48,56},{56,48},{64,72... | collective-permute-start | bytes 1572872 | tf_op jit(solution)/shard_map/ppermute | solution.py:184

commit v4 on v3

--- a/solution.py
+++ b/solution.py
@@ -55,37 +55,29 @@
     return array[:, pl.ds(pl.multiple_of(block * rows, rows), rows)]
 
 
-def for_peer_kernel(rows, acts, out):
+def blocks_kernel(rows, acts, *outs):
     x, y, core = place()
     for split in range(SIDE):
         for reduce in range(SIDE):
-            block = block_of(x, y, 1 - core, split, reduce)
-            out[split, :, reduce * rows : (reduce + 1) * rows] = block_at(acts, block, rows)
-
-
-def chunks_kernel(rows, acts, peer, *outs):
-    x, y, core = place()
-    for split in range(SIDE):
-        for reduce in range(SIDE):
-            block = block_of(x, y, core, split, reduce)
-            outs[split][0, :, reduce * rows : (reduce + 1) * rows] = block_at(acts, block, rows)
-        outs[split][1] = peer[split]
-
-
-def product_kernel(which, rows, a0, a1, a2, a3, g0, g1, g2, g3, *outs):
-    acts, grads = (a0, a1, a2, a3), (g0, g1, g2, g3)
-    panels = g0.shape[1]
+            at = slice(reduce * rows, (reduce + 1) * rows)
+            outs[split][:, at] = block_at(acts, block_of(x, y, core, split, reduce), rows)
+            outs[SIDE + split][:, at] = block_at(acts, block_of(x, y, 1 - core, split, reduce), rows)
+
+
+def product_kernel(which, rows, *refs):
+    acts, grads, outs = refs[: 2 * SIDE], refs[2 * SIDE : 4 * SIDE], refs[4 * SIDE :]
+    panels = grads[0].shape[0]
     here = lax.axis_index("tensor")
     left = {
         reduce: jnp.concatenate(
-            [piece[core, :, reduce * rows : (reduce + 1) * rows].T for piece in acts for core in range(2)], axis=1
+            [piece[:, reduce * rows : (reduce + 1) * rows].T for piece in acts], axis=1
         )
         for reduce in sorted({reduce for reduce, _ in which})
     }
     for (reduce, away), out in zip(which, outs):
         for i, step in enumerate(away):
             panel = lax.rem(here + step, panels)
-            right = jnp.concatenate([piece[core, panel] for piece in grads for core in range(2)], axis=0)
+            right = jnp.concatenate([piece[panel] for piece in grads], axis=0)
             out[i] = jnp.dot(left[reduce], right, preferred_element_type=jnp.float32).astype(out.dtype)
 
 
@@ -130,28 +122,30 @@
     kept = jax.ShapeDtypeStruct
     wide = SIDE * rows
 
-    for_peer = mover(
-        functools.partial(for_peer_kernel, rows), kept((SIDE, tokens, wide), jnp.bfloat16), 1
-    )(activations)
-    from_peer = lax.ppermute(for_peer, "dp", CORE_SWAP)
-    chunk = kept((2, tokens, wide), jnp.bfloat16)
-    chunks = mover(
-        functools.partial(chunks_kernel, rows), [chunk] * SIDE, 2
-    )(activations, from_peer)
-    acts = [chunks[0]] + [lax.ppermute(chunks[i], "dp", ring(i, 0)) for i in range(1, SIDE)]
+    chunk = kept((tokens, wide), jnp.bfloat16)
+    chunks = mover(functools.partial(blocks_kernel, rows), [chunk] * (2 * SIDE), 1)(activations)
+    from_peer = [lax.ppermute(part, "dp", CORE_SWAP) for part in chunks[SIDE:]]
+    acts = [
+        part[i] if i == 0 else lax.ppermute(part[i], "dp", ring(i, 0))
+        for part in (chunks[:SIDE], from_peer)
+        for i in range(SIDE)
+    ]
 
     mine = lax.all_to_all(out_grads.reshape(panels, tokens, cols), "tensor", 0, 0)
-    both = jnp.stack([mine, lax.ppermute(mine, "dp", CORE_SWAP)])
-    grads = [both] + [lax.ppermute(both, "dp", ring(i, 0)) for i in range(1, SIDE)]
+    mine, acts = lax.optimization_barrier((mine, acts))
+    peer = lax.ppermute(mine, "dp", CORE_SWAP)
+    grads = [
+        part if i == 0 else lax.ppermute(part, "dp", ring(i, 0)) for part in (mine, peer) for i in range(SIDE)
+    ]
 
     def product(*which):
         return mover(
             functools.partial(product_kernel, which, rows),
             [kept((len(away), rows, cols), jnp.bfloat16) for _, away in which],
-            2 * SIDE,
+            4 * SIDE,
         )(*acts, *grads)
 
-    far = tuple(range(panels // 2 - 1, panels // 2 + 2))
+    far = (panels // 2, panels // 2 - 1, panels // 2 + 1)
     near = tuple(step for step in range(panels) if step not in far)
     f32 = jnp.float32
     moved = [

time: 145 us -> 135 us (0.931)
  waiting for transfers between devices: 75.1 us -> 44.6 us
  starting transfers between devices: 55.7 us -> 78.2 us
    all_to_all x1, waiting for transfers between devices: 14.4 us -> 0.01 us  [per_device(): lax.all_to_all(out_grads.reshape(panels, tokens, cols), 'tensor', 0, 0)]
    ppermute x8 -> x17, starting transfers between devices: 9.56 us -> 21.6 us  [the longest x6 10.5 us: per_device(): lax.ppermute(part[i], 'dp', ring(i, 0))]
    ppermute x7, starting transfers between devices: 7.06 us -> 16.4 us  [along_tensor(): lax.ppermute(part, 'tensor', [(i, (i + step) % panels) for i in range(pan...]
    ppermute x6, waiting for transfers between devices: 13.6 us -> 4.7 us  [per_device(): lax.ppermute(part, 'dp', ring(i, 1))]
    ppermute x8 -> x17, waiting for transfers between devices: 31.9 us -> 25.3 us  [the longest x6 19.7 us: per_device(): lax.ppermute(part, 'dp', ring(i, 0))]
  transfers between devices with their start and end apart: 32 -> 41, of which waited for: 20 -> 20; matrix products, arithmetic and copies ran while one was open for 1% -> 0% of each run, Pallas kernels for 3% -> 3%
where the time goes in v4:
time: 135 us
  starting transfers between devices  78.2 us (58%)
  waiting for transfers between devices  44.6 us (33%)
  Pallas kernels  7.8 us (6%)
  other arithmetic  1.72 us (1%)
  local copies, waits for them, and re-layouts  1.66 us (1%)
    ppermute x6, waiting for transfers between devices, per_device(): lax.ppermute(part, 'dp', ring(i, 0))  19.7 us
    ppermute x7, starting transfers between devices, along_tensor(): lax.ppermute(part, 'tensor', [(i, (i + step) % panels) for i in range(pan...  16.4 us
    ppermute x4, starting transfers between devices, per_device(): peer = [lax.ppermute(part, 'dp', CORE_SWAP) for part in own]  13.9 us
    ppermute x6, starting transfers between devices, per_device(): lax.ppermute(part[i], 'dp', ring(i, 0))  10.5 us
    all_to_all x1, starting transfers between devices, per_device(): lax.all_to_all(out_grads.reshape(panels, tokens, cols), 'tensor', 0, 0)  9.03 us
    ppermute x7, waiting for transfers between devices, along_tensor(): lax.ppermute(part, 'tensor', [(i, (i + step) % panels) for i in range(pan...  8.13 us
    ppermute x6, starting transfers between devices, per_device(): lax.ppermute(part, 'dp', ring(i, 0))  7.64 us
    ppermute x6, starting transfers between devices, per_device(): lax.ppermute(part, 'dp', ring(i, 1))  7.49 us
  transfers between devices with their start and end apart: 41, of which 20 were waited for; matrix products, arithmetic and copies ran while one was open for 0% of the time, Pallas kernels for 3%

profile of v4, /device:TPU:1, one launch (start us, length us, event | category | flops | bytes accessed | tf_op | source)
XLA Modules:
  0.0 134.8 jit_solution(14476431529274815579)
XLA Ops:
  0.6 9.0 %all-to-all-start = ((bf16[8,128,256]{2,1,0:T(8,128)(2,1)}), bf16[8,128,256]{2,1,0:T(8,128)(2,1)S(1)}, u32[]{:S(2)}, u32[]{:S(2)}) async-start(bf16[8,128,256]{2,1,0:T(8,128)(2,1)} %bitcast.26), calls=%async_computation | async-start | bytes 1048576 | tf_op jit(solution)/shard_map/all_to_all | solution.py:134
  9.7 1.6 %copy-done = bf16[128,8192]{1,0:T(8,128)(2,1)S(1)} copy-done((bf16[128,8192]{1,0:T(8,128)(2,1)S(1)}, bf16[128,8192]{1,0:T(8,128)(2,1)}, u32[]{:S(2)}) %copy-start) | copy-done | bytes 2097176
  11.2 0.3 shard_map.84
  11.6 1.0 collective-permute-start.4
  12.7 0.4 collective-permute-start.8
  13.1 1.3 collective-permute-start
  14.4 2.6 %collective-permute-start.1 = (bf16[128,1024]{1,0:T(8,128)(2,1)S(1)}, bf16[128,1024]{1,0:T(8,128)(2,1)S(1)}, u32[]{:S(2)}, u32[]{:S(2)}) collective-permute-start(bf16[128,1024]{1,0:T(8,128)(2,1)S(1)} %get-tuple-element.31), channel_id=1, source_target_pairs={{0,128},{8,40},{16,144},{24,56},{32,160},{40,8},{48,176},{56,24},{... | collective-permute-start | bytes 786440 | tf_op jit(solution)/shard_map/ppermute | solution.py:129
  17.0 1.1 collective-permute-start.2
  18.1 0.8 collective-permute-start.3
  18.9 1.3 collective-permute-start.5
  20.2 4.2 %collective-permute-start.7 = (bf16[128,1024]{1,0:T(8,128)(2,1)S(1)}, bf16[128,1024]{1,0:T(8,128)(2,1)S(1)}, u32[]{:S(2)}, u32[]{:S(2)}) collective-permute-start(bf16[128,1024]{1,0:T(8,128)(2,1)S(1)} %collective-permute-done.6), channel_id=1, source_target_pairs={{0,128},{8,40},{16,144},{24,56},{32,160},{40,8},{48,176},{56,24},{... | collective-permute-start | bytes 786440 | tf_op jit(solution)/shard_map/ppermute | solution.py:129
  24.4 2.3 %collective-permute-done.5.refs_5_ = bf16[128,1024]{1,0:T(8,128)(2,1)S(1)} collective-permute-done((bf16[128,1024]{1,0:T(8,128)(2,1)S(1)}, bf16[128,1024]{1,0:T(8,128)(2,1)S(1)}, u32[]{:S(2)}, u32[]{:S(2)}) %collective-permute-start.5) | collective-permute-done | bytes 262176 | tf_op jit(solution)/shard_map/ppermute | solution.py:129
  26.7 3.0 %collective-permute-done.7.refs_6_ = bf16[128,1024]{1,0:T(8,128)(2,1)S(1)} collective-permute-done((bf16[128,1024]{1,0:T(8,128)(2,1)S(1)}, bf16[128,1024]{1,0:T(8,128)(2,1)S(1)}, u32[]{:S(2)}, u32[]{:S(2)}) %collective-permute-start.7) | collective-permute-done | bytes 262176 | tf_op jit(solution)/shard_map/ppermute | solution.py:129
  29.9 1.2 collective-permute-start.13
  31.1 1.3 collective-permute-start.10
  32.4 2.6 %collective-permute-start.11 = (bf16[8,128,256]{2,1,0:T(8,128)(2,1)S(1)}, bf16[8,128,256]{2,1,0:T(8,128)(2,1)S(1)}, u32[]{:S(2)}, u32[]{:S(2)}) collective-permute-start(bf16[8,128,256]{2,1,0:T(8,128)(2,1)S(1)} %all-to-all-done.refs_8_), channel_id=1, source_target_pairs={{0,128},{8,40},{16,144},{24,56},{32,160},{40,8},{48,176},{56,24},{... | collective-permute-start | bytes 1572872 | tf_op jit(solution)/shard_map/ppermute | solution.py:138
  35.0 1.1 collective-permute-start.12
  36.1 0.4 collective-permute-start.14
  36.5 0.8 collective-permute-start.15
  37.2 3.4 %collective-permute-done.10.refs_9_ = bf16[8,128,256]{2,1,0:T(8,128)(2,1)S(1)} collective-permute-done((bf16[8,128,256]{2,1,0:T(8,128)(2,1)S(1)}, bf16[8,128,256]{2,1,0:T(8,128)(2,1)S(1)}, u32[]{:S(2)}, u32[]{:S(2)}) %collective-permute-start.10) | collective-permute-done | bytes 524320 | tf_op jit(solution)/shard_map/ppermute | solution.py:138
  40.7 1.5 %collective-permute-start.16 = (bf16[8,128,256]{2,1,0:T(8,128)(2,1)S(1)}, bf16[8,128,256]{2,1,0:T(8,128)(2,1)S(1)}, u32[]{:S(2)}, u32[]{:S(2)}) collective-permute-start(bf16[8,128,256]{2,1,0:T(8,128)(2,1)S(1)} %collective-permute-done.13.refs_12_), channel_id=1, source_target_pairs={{0,192},{8,56},{16,208},{24,8},{32,224},{40,24},{48,240},{56,40},{... | collective-permute-start | bytes 1572872 | tf_op jit(solution)/shard_map/ppermute | solution.py:138
  42.1 5.1 %collective-permute-done.11.refs_10_ = bf16[8,128,256]{2,1,0:T(8,128)(2,1)S(1)} collective-permute-done((bf16[8,128,256]{2,1,0:T(8,128)(2,1)S(1)}, bf16[8,128,256]{2,1,0:T(8,128)(2,1)S(1)}, u32[]{:S(2)}, u32[]{:S(2)}) %collective-permute-start.11) | collective-permute-done | bytes 524320 | tf_op jit(solution)/shard_map/ppermute | solution.py:138
  47.3 4.6 %collective-permute-done.14.refs_13_ = bf16[8,128,256]{2,1,0:T(8,128)(2,1)S(1)} collective-permute-done((bf16[8,128,256]{2,1,0:T(8,128)(2,1)S(1)}, bf16[8,128,256]{2,1,0:T(8,128)(2,1)S(1)}, u32[]{:S(2)}, u32[]{:S(2)}) %collective-permute-start.14) | collective-permute-done | bytes 524320 | tf_op jit(solution)/shard_map/ppermute | solution.py:138
  51.9 6.6 %collective-permute-done.15.refs_14_ = bf16[8,128,256]{2,1,0:T(8,128)(2,1)S(1)} collective-permute-done((bf16[8,128,256]{2,1,0:T(8,128)(2,1)S(1)}, bf16[8,128,256]{2,1,0:T(8,128)(2,1)S(1)}, u32[]{:S(2)}, u32[]{:S(2)}) %collective-permute-start.15) | collective-permute-done | bytes 524320 | tf_op jit(solution)/shard_map/ppermute | solution.py:138
  58.5 1.5 %shard_map.87 = (bf16[3,256,256]{2,1,0:T(8,128)(2,1)S(1)}, bf16[3,256,256]{2,1,0:T(8,128)(2,1)S(1)}, bf16[3,256,256]{2,1,0:T(8,128)(2,1)S(1)}) custom-call(bf16[128,1024]{1,0:T(8,128)(2,1)S(1)} %get-tuple-element.37.refs_0_, bf16[128,1024]{1,0:T(8,128)(2,1)S(1)} %collective-permute-done.refs_1_, bf16[128,1024]{1,0:T(8,128)(2,1)S(1)} %collective-permute-done.1.refs_2_, ...), custom_call_target="tpu_custom_call" | custom-call | tf_op jit(solution)/shard_map/pallas_call | solution.py:142
  59.9 1.9 %collective-permute-start.20 = (bf16[3,256,256]{2,1,0:T(8,128)(2,1)S(1)}, bf16[3,256,256]{2,1,0:T(8,128)(2,1)S(1)}, u32[]{:S(2)}, u32[]{:S(2)}) collective-permute-start(bf16[3,256,256]{2,1,0:T(8,128)(2,1)S(1)} %get-tuple-element.51), channel_id=1, source_target_pairs={{0,32},{8,136},{16,48},{24,152},{32,0},{40,168},{48,16},{56,184},{... | collective-permute-start | bytes 1179656 | tf_op jit(solution)/shard_map/ppermute | solution.py:152
  61.9 0.4 collective-permute-start.21
  62.3 2.3 %collective-permute-start.22 = (bf16[3,256,256]{2,1,0:T(8,128)(2,1)S(1)}, bf16[3,256,256]{2,1,0:T(8,128)(2,1)S(1)}, u32[]{:S(2)}, u32[]{:S(2)}) collective-permute-start(bf16[3,256,256]{2,1,0:T(8,128)(2,1)S(1)} %get-tuple-element.53), channel_id=1, source_target_pairs={{0,48},{8,200},{16,0},{24,216},{32,16},{40,232},{48,32},{56,248},{... | collective-permute-start | bytes 1179656 | tf_op jit(solution)/shard_map/ppermute | solution.py:152
  64.5 2.3 %shard_map.86 = (bf16[5,256,256]{2,1,0:T(8,128)(2,1)S(1)}, bf16[5,256,256]{2,1,0:T(8,128)(2,1)S(1)}, bf16[5,256,256]{2,1,0:T(8,128)(2,1)S(1)}) custom-call(bf16[128,1024]{1,0:T(8,128)(2,1)S(1)} %get-tuple-element.37.refs_0_, bf16[128,1024]{1,0:T(8,128)(2,1)S(1)} %collective-permute-done.refs_1_, bf16[128,1024]{1,0:T(8,128)(2,1)S(1)} %collective-permute-done.1.refs_2_, ...), custom_call_target="tpu_custom_call" | custom-call | tf_op jit(solution)/shard_map/pallas_call | solution.py:142
  66.8 0.3 collective-permute-start.17
  67.2 0.9 collective-permute-start.18
  68.0 0.5 collective-permute-done.20
  68.5 1.7 %collective-permute-start.19 = (bf16[5,256,256]{2,1,0:T(8,128)(2,1)S(1)}, bf16[5,256,256]{2,1,0:T(8,128)(2,1)S(1)}, u32[]{:S(2)}, u32[]{:S(2)}) collective-permute-start(bf16[5,256,256]{2,1,0:T(8,128)(2,1)S(1)} %get-tuple-element.49), channel_id=1, source_target_pairs={{0,48},{8,200},{16,0},{24,216},{32,16},{40,232},{48,32},{56,248},{... | collective-permute-start | bytes 1966088 | tf_op jit(solution)/shard_map/ppermute | solution.py:152
  70.1 1.3 shard_map.85
  71.4 1.2 collective-permute-done.21
  72.9 5.7 %collective-permute-start.23 = (bf16[256,256]{1,0:T(8,128)(2,1)S(1)}, bf16[256,256]{1,0:T(8,128)(2,1)S(1)}, u32[]{:S(2)}, u32[]{:S(2)}) collective-permute-start(bf16[256,256]{1,0:T(8,128)(2,1)S(1)} %get-tuple-element.62), channel_id=1, source_target_pairs={{0,4},{1,5},{2,6},{3,7},{4,0},{5,1},{6,2},{7,3},{8,12},{9,13},{10,... | collective-permute-start | bytes 393224 | tf_op jit(solution)/shard_map/ppermute | solution.py:161
  78.9 0.8 collective-permute-done.17
  79.8 4.8 %collective-permute-start.25 = (bf16[256,256]{1,0:T(8,128)(2,1)S(1)}, bf16[256,256]{1,0:T(8,128)(2,1)S(1)}, u32[]{:S(2)}, u32[]{:S(2)}) collective-permute-start(bf16[256,256]{1,0:T(8,128)(2,1)S(1)} %get-tuple-element.63), channel_id=1, source_target_pairs={{0,5},{1,6},{2,7},{3,0},{4,1},{5,2},{6,3},{7,4},{8,13},{9,14},{10,... | collective-permute-start | bytes 393224 | tf_op jit(solution)/shard_map/ppermute | solution.py:161
  84.5 2.2 %collective-permute-done.18 = bf16[5,256,256]{2,1,0:T(8,128)(2,1)S(1)} collective-permute-done((bf16[5,256,256]{2,1,0:T(8,128)(2,1)S(1)}, bf16[5,256,256]{2,1,0:T(8,128)(2,1)S(1)}, u32[]{:S(2)}, u32[]{:S(2)}) %collective-permute-start.18) | collective-permute-done | bytes 655392 | tf_op jit(solution)/shard_map/ppermute | solution.py:152
  86.7 0.3 add_convert_fusion
  87.1 1.8 %collective-permute-start.26 = (bf16[256,256]{1,0:T(8,128)(2,1)S(1)}, bf16[256,256]{1,0:T(8,128)(2,1)S(1)}, u32[]{:S(2)}, u32[]{:S(2)}) collective-permute-start(bf16[256,256]{1,0:T(8,128)(2,1)S(1)} %get-tuple-element.58), channel_id=1, source_target_pairs={{0,1},{1,2},{2,3},{3,4},{4,5},{5,6},{6,7},{7,0},{8,9},{9,10},{10,1... | collective-permute-start | bytes 393224 | tf_op jit(solution)/shard_map/ppermute | solution.py:161
  88.9 2.1 %collective-permute-start.27 = (bf16[256,256]{1,0:T(8,128)(2,1)S(1)}, bf16[256,256]{1,0:T(8,128)(2,1)S(1)}, u32[]{:S(2)}, u32[]{:S(2)}) collective-permute-start(bf16[256,256]{1,0:T(8,128)(2,1)S(1)} %get-tuple-element.61), channel_id=1, source_target_pairs={{0,2},{1,3},{2,4},{3,5},{4,6},{5,7},{6,0},{7,1},{8,10},{9,11},{10,... | collective-permute-start | bytes 393224 | tf_op jit(solution)/shard_map/ppermute | solution.py:161
  91.0 1.5 %collective-permute-start.28 = (bf16[256,256]{1,0:T(8,128)(2,1)S(1)}, bf16[256,256]{1,0:T(8,128)(2,1)S(1)}, u32[]{:S(2)}, u32[]{:S(2)}) collective-permute-start(bf16[256,256]{1,0:T(8,128)(2,1)S(1)} %get-tuple-element.60), channel_id=1, source_target_pairs={{0,6},{1,7},{2,0},{3,1},{4,2},{5,3},{6,4},{7,5},{8,14},{9,15},{10,... | collective-permute-start | bytes 393224 | tf_op jit(solution)/shard_map/ppermute | solution.py:161
  92.8 4.2 %collective-permute-done.26 = bf16[256,256]{1,0:T(8,128)(2,1)S(1)} collective-permute-done((bf16[256,256]{1,0:T(8,128)(2,1)S(1)}, bf16[256,256]{1,0:T(8,128)(2,1)S(1)}, u32[]{:S(2)}, u32[]{:S(2)}) %collective-permute-start.26) | collective-permute-done | bytes 131104 | tf_op jit(solution)/shard_map/ppermute | solution.py:161
  97.0 2.3 %collective-permute-done.27 = bf16[256,256]{1,0:T(8,128)(2,1)S(1)} collective-permute-done((bf16[256,256]{1,0:T(8,128)(2,1)S(1)}, bf16[256,256]{1,0:T(8,128)(2,1)S(1)}, u32[]{:S(2)}, u32[]{:S(2)}) %collective-permute-start.27) | collective-permute-done | bytes 131104 | tf_op jit(solution)/shard_map/ppermute | solution.py:161
  99.3 1.6 %collective-permute-done.29 = bf16[256,256]{1,0:T(8,128)(2,1)S(1)} collective-permute-done((bf16[256,256]{1,0:T(8,128)(2,1)S(1)}, bf16[256,256]{1,0:T(8,128)(2,1)S(1)}, u32[]{:S(2)}, u32[]{:S(2)}) %collective-permute-start.29) | collective-permute-done | bytes 131104 | tf_op jit(solution)/shard_map/ppermute | solution.py:161
  100.9 1.1 fusion.7
  102.0 2.2 %collective-permute-start.30 = (bf16[256,256]{1,0:T(8,128)(2,1)S(1)}, bf16[256,256]{1,0:T(8,128)(2,1)S(1)}, u32[]{:S(2)}, u32[]{:S(2)}) collective-permute-start(bf16[256,256]{1,0:T(8,128)(2,1)S(1)} %get-tuple-element.54), channel_id=1, source_target_pairs={{0,64},{8,24},{16,80},{24,40},{32,96},{40,56},{48,112},{56,8},{64,... | collective-permute-start | bytes 393224 | tf_op jit(solution)/shard_map/ppermute | solution.py:176
  104.2 1.5 %collective-permute-start.31 = (bf16[256,256]{1,0:T(8,128)(2,1)S(1)}, bf16[256,256]{1,0:T(8,128)(2,1)S(1)}, u32[]{:S(2)}, u32[]{:S(2)}) collective-permute-start(bf16[256,256]{1,0:T(8,128)(2,1)S(1)} %get-tuple-element.54), channel_id=1, source_target_pairs={{0,128},{8,40},{16,144},{24,56},{32,160},{40,8},{48,176},{56,24},{... | collective-permute-start | bytes 393224 | tf_op jit(solution)/shard_map/ppermute | solution.py:176
  105.7 2.1 %collective-permute-start.32 = (bf16[256,256]{1,0:T(8,128)(2,1)S(1)}, bf16[256,256]{1,0:T(8,128)(2,1)S(1)}, u32[]{:S(2)}, u32[]{:S(2)}) collective-permute-start(bf16[256,256]{1,0:T(8,128)(2,1)S(1)} %get-tuple-element.54), channel_id=1, source_target_pairs={{0,192},{8,56},{16,208},{24,8},{32,224},{40,24},{48,240},{56,40},{... | collective-permute-start | bytes 393224 | tf_op jit(solution)/shard_map/ppermute | solution.py:176
  107.8 1.8 %collective-permute-done.31 = bf16[256,256]{1,0:T(8,128)(2,1)S(1)} collective-permute-done((bf16[256,256]{1,0:T(8,128)(2,1)S(1)}, bf16[256,256]{1,0:T(8,128)(2,1)S(1)}, u32[]{:S(2)}, u32[]{:S(2)}) %collective-permute-start.31) | collective-permute-done | bytes 131104 | tf_op jit(solution)/shard_map/ppermute | solution.py:176
  109.5 0.3 collective-permute-done.32
  109.9 1.2 collective-permute-start.33
  111.1 2.1 %collective-permute-start.34 = (bf16[4,256,256]{2,1,0:T(8,128)(2,1)S(1)}, bf16[4,256,256]{2,1,0:T(8,128)(2,1)S(1)}, u32[]{:S(2)}, u32[]{:S(2)}) collective-permute-start(bf16[4,256,256]{2,1,0:T(8,128)(2,1)S(1)} %pad_maximum_fusion.refs_0_), channel_id=1, source_target_pairs={{0,32},{8,136},{16,48},{24,152},{32,0},{40,168},{48,16},{56,184},{... | collective-permute-start | bytes 1572872 | tf_op jit(solution)/shard_map/ppermute | solution.py:177
  113.2 0.7 collective-permute-start.35
  113.8 4.9 %collective-permute-start.36 = (bf16[4,256,256]{2,1,0:T(8,128)(2,1)S(1)}, bf16[4,256,256]{2,1,0:T(8,128)(2,1)S(1)}, u32[]{:S(2)}, u32[]{:S(2)}) collective-permute-start(bf16[4,256,256]{2,1,0:T(8,128)(2,1)S(1)} %pad_maximum_fusion.refs_0_), channel_id=1, source_target_pairs={{0,8},{8,0},{16,24},{24,16},{32,40},{40,32},{48,56},{56,48},{64,72... | collective-permute-start | bytes 1572872 | tf_op jit(solution)/shard_map/ppermute | solution.py:178
  118.7 0.8 collective-permute-done.33.refs_1_
  119.5 4.3 %collective-permute-start.37 = (bf16[4,256,256]{2,1,0:T(8,128)(2,1)S(1)}, bf16[4,256,256]{2,1,0:T(8,128)(2,1)S(1)}, u32[]{:S(2)}, u32[]{:S(2)}) collective-permute-start(bf16[4,256,256]{2,1,0:T(8,128)(2,1)S(1)} %collective-permute-done.33.refs_1_), channel_id=1, source_target_pairs={{0,8},{8,0},{16,24},{24,16},{32,40},{40,32},{48,56},{56,48},{64,72... | collective-permute-start | bytes 1572872 | tf_op jit(solution)/shard_map/ppermute | solution.py:178
  123.8 1.8 %collective-permute-done.34.refs_2_ = bf16[4,256,256]{2,1,0:T(8,128)(2,1)S(1)} collective-permute-done((bf16[4,256,256]{2,1,0:T(8,128)(2,1)S(1)}, bf16[4,256,256]{2,1,0:T(8,128)(2,1)S(1)}, u32[]{:S(2)}, u32[]{:S(2)}) %collective-permute-start.34) | collective-permute-done | bytes 524320 | tf_op jit(solution)/shard_map/ppermute | solution.py:177
  125.6 4.3 %collective-permute-start.38 = (bf16[4,256,256]{2,1,0:T(8,128)(2,1)S(1)}, bf16[4,256,256]{2,1,0:T(8,128)(2,1)S(1)}, u32[]{:S(2)}, u32[]{:S(2)}) collective-permute-start(bf16[4,256,256]{2,1,0:T(8,128)(2,1)S(1)} %collective-permute-done.34.refs_2_), channel_id=1, source_target_pairs={{0,8},{8,0},{16,24},{24,16},{32,40},{40,32},{48,56},{56,48},{64,72... | collective-permute-start | bytes 1572872 | tf_op jit(solution)/shard_map/ppermute | solution.py:178
  130.0 0.4 collective-permute-start.39
  130.3 1.2 collective-permute-done.38.refs_6_
  131.5 0.7 collective-permute-done.39.refs_7_
  132.3 2.5 %shard_map.88 = bf16[4,4,2,256,256]{4,3,2,1,0:T(8,128)(2,1)} custom-call(bf16[4,256,256]{2,1,0:T(8,128)(2,1)S(1)} %pad_maximum_fusion.refs_0_, bf16[4,256,256]{2,1,0:T(8,128)(2,1)S(1)} %collective-permute-done.33.refs_1_, bf16[4,256,256]{2,1,0:T(8,128)(2,1)S(1)} %collective-permute-done.34.refs_2_, bf16[4,256,256]{2,1,0:T(8,128)(2,1)S(1)} %collective-permute-done.35.refs_3_, ...), custom_call_target="tpu_custom_call" | custom-call | tf_op jit(solution)/shard_map/pallas_call | solution.py:179
  (37 shorter events, 1.3 us)
Async XLA Ops:
  0.6 29.3 %all-to-all-start = ((bf16[8,128,256]{2,1,0:T(8,128)(2,1)}), bf16[8,128,256]{2,1,0:T(8,128)(2,1)S(1)}, u32[]{:S(2)}, u32[]{:S(2)}) async-start(bf16[8,128,256]{2,1,0:T(8,128)(2,1)} %bitcast.26), calls=%async_computation | async-start | bytes 1048576 | tf_op jit(solution)/shard_map/all_to_all | solution.py:134
  9.7 1.6 %copy-start = (bf16[128,8192]{1,0:T(8,128)(2,1)S(1)}, bf16[128,8192]{1,0:T(8,128)(2,1)}, u32[]{:S(2)}) copy-start(bf16[128,8192]{1,0:T(8,128)(2,1)} %acts.1) | copy-start | bytes 6291460
  11.6 5.5 %collective-permute-start.4 = (bf16[128,1024]{1,0:T(8,128)(2,1)S(1)}, bf16[128,1024]{1,0:T(8,128)(2,1)S(1)}, u32[]{:S(2)}, u32[]{:S(2)}) collective-permute-start(bf16[128,1024]{1,0:T(8,128)(2,1)S(1)} %get-tuple-element.34), channel_id=1, source_target_pairs={{0,8},{8,0},{16,24},{24,16},{32,40},{40,32},{48,56},{56,48},{64,72... | collective-permute-start | bytes 786440 | tf_op jit(solution)/shard_map/ppermute | solution.py:127
  12.6 5.5 %collective-permute-start.6 = (bf16[128,1024]{1,0:T(8,128)(2,1)S(1)}, bf16[128,1024]{1,0:T(8,128)(2,1)S(1)}, u32[]{:S(2)}, u32[]{:S(2)}) collective-permute-start(bf16[128,1024]{1,0:T(8,128)(2,1)S(1)} %get-tuple-element.35), channel_id=1, source_target_pairs={{0,8},{8,0},{16,24},{24,16},{32,40},{40,32},{48,56},{56,48},{64,72... | collective-permute-start | bytes 786440 | tf_op jit(solution)/shard_map/ppermute | solution.py:127
  12.7 6.2 %collective-permute-start.8 = (bf16[128,1024]{1,0:T(8,128)(2,1)S(1)}, bf16[128,1024]{1,0:T(8,128)(2,1)S(1)}, u32[]{:S(2)}, u32[]{:S(2)}) collective-permute-start(bf16[128,1024]{1,0:T(8,128)(2,1)S(1)} %get-tuple-element.36), channel_id=1, source_target_pairs={{0,8},{8,0},{16,24},{24,16},{32,40},{40,32},{48,56},{56,48},{64,72... | collective-permute-start | bytes 786440 | tf_op jit(solution)/shard_map/ppermute | solution.py:127
  13.1 7.1 %collective-permute-start = (bf16[128,1024]{1,0:T(8,128)(2,1)S(1)}, bf16[128,1024]{1,0:T(8,128)(2,1)S(1)}, u32[]{:S(2)}, u32[]{:S(2)}) collective-permute-start(bf16[128,1024]{1,0:T(8,128)(2,1)S(1)} %get-tuple-element.30), channel_id=1, source_target_pairs={{0,64},{8,24},{16,80},{24,40},{32,96},{40,56},{48,112},{56,8},{64,... | collective-permute-start | bytes 786440 | tf_op jit(solution)/shard_map/ppermute | solution.py:129
  14.4 9.9 %collective-permute-start.1 = (bf16[128,1024]{1,0:T(8,128)(2,1)S(1)}, bf16[128,1024]{1,0:T(8,128)(2,1)S(1)}, u32[]{:S(2)}, u32[]{:S(2)}) collective-permute-start(bf16[128,1024]{1,0:T(8,128)(2,1)S(1)} %get-tuple-element.31), channel_id=1, source_target_pairs={{0,128},{8,40},{16,144},{24,56},{32,160},{40,8},{48,176},{56,24},{... | collective-permute-start | bytes 786440 | tf_op jit(solution)/shard_map/ppermute | solution.py:129
  17.0 7.3 %collective-permute-start.2 = (bf16[128,1024]{1,0:T(8,128)(2,1)S(1)}, bf16[128,1024]{1,0:T(8,128)(2,1)S(1)}, u32[]{:S(2)}, u32[]{:S(2)}) collective-permute-start(bf16[128,1024]{1,0:T(8,128)(2,1)S(1)} %get-tuple-element.32), channel_id=1, source_target_pairs={{0,192},{8,56},{16,208},{24,8},{32,224},{40,24},{48,240},{56,40},{... | collective-permute-start | bytes 786440 | tf_op jit(solution)/shard_map/ppermute | solution.py:129
  18.1 6.3 %collective-permute-start.3 = (bf16[128,1024]{1,0:T(8,128)(2,1)S(1)}, bf16[128,1024]{1,0:T(8,128)(2,1)S(1)}, u32[]{:S(2)}, u32[]{:S(2)}) collective-permute-start(bf16[128,1024]{1,0:T(8,128)(2,1)S(1)} %get-tuple-element.33), channel_id=1, source_target_pairs={{0,8},{8,0},{16,24},{24,16},{32,40},{40,32},{48,56},{56,48},{64,72... | collective-permute-start | bytes 786440 | tf_op jit(solution)/shard_map/ppermute | solution.py:127
  18.9 7.8 %collective-permute-start.5 = (bf16[128,1024]{1,0:T(8,128)(2,1)S(1)}, bf16[128,1024]{1,0:T(8,128)(2,1)S(1)}, u32[]{:S(2)}, u32[]{:S(2)}) collective-permute-start(bf16[128,1024]{1,0:T(8,128)(2,1)S(1)} %collective-permute-done.4), channel_id=1, source_target_pairs={{0,64},{8,24},{16,80},{24,40},{32,96},{40,56},{48,112},{56,8},{64,... | collective-permute-start | bytes 786440 | tf_op jit(solution)/shard_map/ppermute | solution.py:129
  20.2 9.5 %collective-permute-start.7 = (bf16[128,1024]{1,0:T(8,128)(2,1)S(1)}, bf16[128,1024]{1,0:T(8,128)(2,1)S(1)}, u32[]{:S(2)}, u32[]{:S(2)}) collective-permute-start(bf16[128,1024]{1,0:T(8,128)(2,1)S(1)} %collective-permute-done.6), channel_id=1, source_target_pairs={{0,128},{8,40},{16,144},{24,56},{32,160},{40,8},{48,176},{56,24},{... | collective-permute-start | bytes 786440 | tf_op jit(solution)/shard_map/ppermute | solution.py:129
  24.4 5.5 %collective-permute-start.9 = (bf16[128,1024]{1,0:T(8,128)(2,1)S(1)}, bf16[128,1024]{1,0:T(8,128)(2,1)S(1)}, u32[]{:S(2)}, u32[]{:S(2)}) collective-permute-start(bf16[128,1024]{1,0:T(8,128)(2,1)S(1)} %collective-permute-done.8), channel_id=1, source_target_pairs={{0,192},{8,56},{16,208},{24,8},{32,224},{40,24},{48,240},{56,40},{... | collective-permute-start | bytes 786440 | tf_op jit(solution)/shard_map/ppermute | solution.py:129
  29.9 6.2 %collective-permute-start.13 = (bf16[8,128,256]{2,1,0:T(8,128)(2,1)S(1)}, bf16[8,128,256]{2,1,0:T(8,128)(2,1)S(1)}, u32[]{:S(2)}, u32[]{:S(2)}) collective-permute-start(bf16[8,128,256]{2,1,0:T(8,128)(2,1)S(1)} %all-to-all-done.refs_8_), channel_id=1, source_target_pairs={{0,8},{8,0},{16,24},{24,16},{32,40},{40,32},{48,56},{56,48},{64,72... | collective-permute-start | bytes 1572872 | tf_op jit(solution)/shard_map/ppermute | solution.py:136
  31.1 9.6 %collective-permute-start.10 = (bf16[8,128,256]{2,1,0:T(8,128)(2,1)S(1)}, bf16[8,128,256]{2,1,0:T(8,128)(2,1)S(1)}, u32[]{:S(2)}, u32[]{:S(2)}) collective-permute-start(bf16[8,128,256]{2,1,0:T(8,128)(2,1)S(1)} %all-to-all-done.refs_8_), channel_id=1, source_target_pairs={{0,64},{8,24},{16,80},{24,40},{32,96},{40,56},{48,112},{56,8},{64,... | collective-permute-start | bytes 1572872 | tf_op jit(solution)/shard_map/ppermute | solution.py:138
  32.4 14.9 %collective-permute-start.11 = (bf16[8,128,256]{2,1,0:T(8,128)(2,1)S(1)}, bf16[8,128,256]{2,1,0:T(8,128)(2,1)S(1)}, u32[]{:S(2)}, u32[]{:S(2)}) collective-permute-start(bf16[8,128,256]{2,1,0:T(8,128)(2,1)S(1)} %all-to-all-done.refs_8_), channel_id=1, source_target_pairs={{0,128},{8,40},{16,144},{24,56},{32,160},{40,8},{48,176},{56,24},{... | collective-permute-start | bytes 1572872 | tf_op jit(solution)/shard_map/ppermute | solution.py:138
  35.0 12.3 %collective-permute-start.12 = (bf16[8,128,256]{2,1,0:T(8,128)(2,1)S(1)}, bf16[8,128,256]{2,1,0:T(8,128)(2,1)S(1)}, u32[]{:S(2)}, u32[]{:S(2)}) collective-permute-start(bf16[8,128,256]{2,1,0:T(8,128)(2,1)S(1)} %all-to-all-done.refs_8_), channel_id=1, source_target_pairs={{0,192},{8,56},{16,208},{24,8},{32,224},{40,24},{48,240},{56,40},{... | collective-permute-start | bytes 1572872 | tf_op jit(solution)/shard_map/ppermute | solution.py:138
  36.1 15.8 %collective-permute-start.14 = (bf16[8,128,256]{2,1,0:T(8,128)(2,1)S(1)}, bf16[8,128,256]{2,1,0:T(8,128)(2,1)S(1)}, u32[]{:S(2)}, u32[]{:S(2)}) collective-permute-start(bf16[8,128,256]{2,1,0:T(8,128)(2,1)S(1)} %collective-permute-done.13.refs_12_), channel_id=1, source_target_pairs={{0,64},{8,24},{16,80},{24,40},{32,96},{40,56},{48,112},{56,8},{64,... | collective-permute-start | bytes 1572872 | tf_op jit(solution)/shard_map/ppermute | solution.py:138
  36.5 22.0 %collective-permute-start.15 = (bf16[8,128,256]{2,1,0:T(8,128)(2,1)S(1)}, bf16[8,128,256]{2,1,0:T(8,128)(2,1)S(1)}, u32[]{:S(2)}, u32[]{:S(2)}) collective-permute-start(bf16[8,128,256]{2,1,0:T(8,128)(2,1)S(1)} %collective-permute-done.13.refs_12_), channel_id=1, source_target_pairs={{0,128},{8,40},{16,144},{24,56},{32,160},{40,8},{48,176},{56,24},{... | collective-permute-start | bytes 1572872 | tf_op jit(solution)/shard_map/ppermute | solution.py:138
  40.7 17.8 %collective-permute-start.16 = (bf16[8,128,256]{2,1,0:T(8,128)(2,1)S(1)}, bf16[8,128,256]{2,1,0:T(8,128)(2,1)S(1)}, u32[]{:S(2)}, u32[]{:S(2)}) collective-permute-start(bf16[8,128,256]{2,1,0:T(8,128)(2,1)S(1)} %collective-permute-done.13.refs_12_), channel_id=1, source_target_pairs={{0,192},{8,56},{16,208},{24,8},{32,224},{40,24},{48,240},{56,40},{... | collective-permute-start | bytes 1572872 | tf_op jit(solution)/shard_map/ppermute | solution.py:138
  59.9 8.6 %collective-permute-start.20 = (bf16[3,256,256]{2,1,0:T(8,128)(2,1)S(1)}, bf16[3,256,256]{2,1,0:T(8,128)(2,1)S(1)}, u32[]{:S(2)}, u32[]{:S(2)}) collective-permute-start(bf16[3,256,256]{2,1,0:T(8,128)(2,1)S(1)} %get-tuple-element.51), channel_id=1, source_target_pairs={{0,32},{8,136},{16,48},{24,152},{32,0},{40,168},{48,16},{56,184},{... | collective-permute-start | bytes 1179656 | tf_op jit(solution)/shard_map/ppermute | solution.py:152
  61.9 10.8 %collective-permute-start.21 = (bf16[3,256,256]{2,1,0:T(8,128)(2,1)S(1)}, bf16[3,256,256]{2,1,0:T(8,128)(2,1)S(1)}, u32[]{:S(2)}, u32[]{:S(2)}) collective-permute-start(bf16[3,256,256]{2,1,0:T(8,128)(2,1)S(1)} %get-tuple-element.52), channel_id=1, source_target_pairs={{0,16},{8,72},{16,32},{24,88},{32,48},{40,104},{48,0},{56,120},{64... | collective-permute-start | bytes 1179656 | tf_op jit(solution)/shard_map/ppermute | solution.py:152
  62.3 10.4 %collective-permute-start.22 = (bf16[3,256,256]{2,1,0:T(8,128)(2,1)S(1)}, bf16[3,256,256]{2,1,0:T(8,128)(2,1)S(1)}, u32[]{:S(2)}, u32[]{:S(2)}) collective-permute-start(bf16[3,256,256]{2,1,0:T(8,128)(2,1)S(1)} %get-tuple-element.53), channel_id=1, source_target_pairs={{0,48},{8,200},{16,0},{24,216},{32,16},{40,232},{48,32},{56,248},{... | collective-permute-start | bytes 1179656 | tf_op jit(solution)/shard_map/ppermute | solution.py:152
  66.8 12.9 %collective-permute-start.17 = (bf16[5,256,256]{2,1,0:T(8,128)(2,1)S(1)}, bf16[5,256,256]{2,1,0:T(8,128)(2,1)S(1)}, u32[]{:S(2)}, u32[]{:S(2)}) collective-permute-start(bf16[5,256,256]{2,1,0:T(8,128)(2,1)S(1)} %get-tuple-element.47), channel_id=1, source_target_pairs={{0,32},{8,136},{16,48},{24,152},{32,0},{40,168},{48,16},{56,184},{... | collective-permute-start | bytes 1966088 | tf_op jit(solution)/shard_map/ppermute | solution.py:152
  67.2 19.5 %collective-permute-start.18 = (bf16[5,256,256]{2,1,0:T(8,128)(2,1)S(1)}, bf16[5,256,256]{2,1,0:T(8,128)(2,1)S(1)}, u32[]{:S(2)}, u32[]{:S(2)}) collective-permute-start(bf16[5,256,256]{2,1,0:T(8,128)(2,1)S(1)} %get-tuple-element.48), channel_id=1, source_target_pairs={{0,16},{8,72},{16,32},{24,88},{32,48},{40,104},{48,0},{56,120},{64... | collective-permute-start | bytes 1966088 | tf_op jit(solution)/shard_map/ppermute | solution.py:152
  68.5 18.2 %collective-permute-start.19 = (bf16[5,256,256]{2,1,0:T(8,128)(2,1)S(1)}, bf16[5,256,256]{2,1,0:T(8,128)(2,1)S(1)}, u32[]{:S(2)}, u32[]{:S(2)}) collective-permute-start(bf16[5,256,256]{2,1,0:T(8,128)(2,1)S(1)} %get-tuple-element.49), channel_id=1, source_target_pairs={{0,48},{8,200},{16,0},{24,216},{32,16},{40,232},{48,32},{56,248},{... | collective-permute-start | bytes 1966088 | tf_op jit(solution)/shard_map/ppermute | solution.py:152
  72.9 18.1 %collective-permute-start.23 = (bf16[256,256]{1,0:T(8,128)(2,1)S(1)}, bf16[256,256]{1,0:T(8,128)(2,1)S(1)}, u32[]{:S(2)}, u32[]{:S(2)}) collective-permute-start(bf16[256,256]{1,0:T(8,128)(2,1)S(1)} %get-tuple-element.62), channel_id=1, source_target_pairs={{0,4},{1,5},{2,6},{3,7},{4,0},{5,1},{6,2},{7,3},{8,12},{9,13},{10,... | collective-permute-start | bytes 393224 | tf_op jit(solution)/shard_map/ppermute | solution.py:161
  78.6 13.9 %collective-permute-start.24 = (bf16[256,256]{1,0:T(8,128)(2,1)S(1)}, bf16[256,256]{1,0:T(8,128)(2,1)S(1)}, u32[]{:S(2)}, u32[]{:S(2)}) collective-permute-start(bf16[256,256]{1,0:T(8,128)(2,1)S(1)} %get-tuple-element.64), channel_id=1, source_target_pairs={{0,3},{1,4},{2,5},{3,6},{4,7},{5,0},{6,1},{7,2},{8,11},{9,12},{10,... | collective-permute-start | bytes 393224 | tf_op jit(solution)/shard_map/ppermute | solution.py:161
  79.8 13.1 %collective-permute-start.25 = (bf16[256,256]{1,0:T(8,128)(2,1)S(1)}, bf16[256,256]{1,0:T(8,128)(2,1)S(1)}, u32[]{:S(2)}, u32[]{:S(2)}) collective-permute-start(bf16[256,256]{1,0:T(8,128)(2,1)S(1)} %get-tuple-element.63), channel_id=1, source_target_pairs={{0,5},{1,6},{2,7},{3,0},{4,1},{5,2},{6,3},{7,4},{8,13},{9,14},{10,... | collective-permute-start | bytes 393224 | tf_op jit(solution)/shard_map/ppermute | solution.py:161
  86.7 14.2 %copy-start.1 = (f32[256,256]{1,0:T(8,128)S(1)}, f32[256,256]{1,0:T(8,128)}, u32[]{:S(2)}) copy-start(f32[256,256]{1,0:T(8,128)} %param.7) | copy-start | bytes 786436
  86.7 14.2 %copy-start.2 = (f32[256,256]{1,0:T(8,128)S(1)}, f32[256,256]{1,0:T(8,128)}, u32[]{:S(2)}) copy-start(f32[256,256]{1,0:T(8,128)} %param.8) | copy-start | bytes 786436
  86.7 14.2 %copy-start.3 = (f32[256,256]{1,0:T(8,128)S(1)}, f32[256,256]{1,0:T(8,128)}, u32[]{:S(2)}) copy-start(f32[256,256]{1,0:T(8,128)} %param.9) | copy-start | bytes 786436
  87.1 9.9 %collective-permute-start.26 = (bf16[256,256]{1,0:T(8,128)(2,1)S(1)}, bf16[256,256]{1,0:T(8,128)(2,1)S(1)}, u32[]{:S(2)}, u32[]{:S(2)}) collective-permute-start(bf16[256,256]{1,0:T(8,128)(2,1)S(1)} %get-tuple-element.58), channel_id=1, source_target_pairs={{0,1},{1,2},{2,3},{3,4},{4,5},{5,6},{6,7},{7,0},{8,9},{9,10},{10,1... | collective-permute-start | bytes 393224 | tf_op jit(solution)/shard_map/ppermute | solution.py:161
  88.9 10.4 %collective-permute-start.27 = (bf16[256,256]{1,0:T(8,128)(2,1)S(1)}, bf16[256,256]{1,0:T(8,128)(2,1)S(1)}, u32[]{:S(2)}, u32[]{:S(2)}) collective-permute-start(bf16[256,256]{1,0:T(8,128)(2,1)S(1)} %get-tuple-element.61), channel_id=1, source_target_pairs={{0,2},{1,3},{2,4},{3,5},{4,6},{5,7},{6,0},{7,1},{8,10},{9,11},{10,... | collective-permute-start | bytes 393224 | tf_op jit(solution)/shard_map/ppermute | solution.py:161
  91.0 8.3 %collective-permute-start.28 = (bf16[256,256]{1,0:T(8,128)(2,1)S(1)}, bf16[256,256]{1,0:T(8,128)(2,1)S(1)}, u32[]{:S(2)}, u32[]{:S(2)}) collective-permute-start(bf16[256,256]{1,0:T(8,128)(2,1)S(1)} %get-tuple-element.60), channel_id=1, source_target_pairs={{0,6},{1,7},{2,0},{3,1},{4,2},{5,3},{6,4},{7,5},{8,14},{9,15},{10,... | collective-permute-start | bytes 393224 | tf_op jit(solution)/shard_map/ppermute | solution.py:161
  92.5 8.4 %collective-permute-start.29 = (bf16[256,256]{1,0:T(8,128)(2,1)S(1)}, bf16[256,256]{1,0:T(8,128)(2,1)S(1)}, u32[]{:S(2)}, u32[]{:S(2)}) collective-permute-start(bf16[256,256]{1,0:T(8,128)(2,1)S(1)} %get-tuple-element.59), channel_id=1, source_target_pairs={{0,7},{1,0},{2,1},{3,2},{4,3},{5,4},{6,5},{7,6},{8,15},{9,8},{10,9... | collective-permute-start | bytes 393224 | tf_op jit(solution)/shard_map/ppermute | solution.py:161
  102.0 5.7 %collective-permute-start.30 = (bf16[256,256]{1,0:T(8,128)(2,1)S(1)}, bf16[256,256]{1,0:T(8,128)(2,1)S(1)}, u32[]{:S(2)}, u32[]{:S(2)}) collective-permute-start(bf16[256,256]{1,0:T(8,128)(2,1)S(1)} %get-tuple-element.54), channel_id=1, source_target_pairs={{0,64},{8,24},{16,80},{24,40},{32,96},{40,56},{48,112},{56,8},{64,... | collective-permute-start | bytes 393224 | tf_op jit(solution)/shard_map/ppermute | solution.py:176
  104.2 5.3 %collective-permute-start.31 = (bf16[256,256]{1,0:T(8,128)(2,1)S(1)}, bf16[256,256]{1,0:T(8,128)(2,1)S(1)}, u32[]{:S(2)}, u32[]{:S(2)}) collective-permute-start(bf16[256,256]{1,0:T(8,128)(2,1)S(1)} %get-tuple-element.54), channel_id=1, source_target_pairs={{0,128},{8,40},{16,144},{24,56},{32,160},{40,8},{48,176},{56,24},{... | collective-permute-start | bytes 393224 | tf_op jit(solution)/shard_map/ppermute | solution.py:176
  105.7 4.1 %collective-permute-start.32 = (bf16[256,256]{1,0:T(8,128)(2,1)S(1)}, bf16[256,256]{1,0:T(8,128)(2,1)S(1)}, u32[]{:S(2)}, u32[]{:S(2)}) collective-permute-start(bf16[256,256]{1,0:T(8,128)(2,1)S(1)} %get-tuple-element.54), channel_id=1, source_target_pairs={{0,192},{8,56},{16,208},{24,8},{32,224},{40,24},{48,240},{56,40},{... | collective-permute-start | bytes 393224 | tf_op jit(solution)/shard_map/ppermute | solution.py:176
  109.9 9.6 %collective-permute-start.33 = (bf16[4,256,256]{2,1,0:T(8,128)(2,1)S(1)}, bf16[4,256,256]{2,1,0:T(8,128)(2,1)S(1)}, u32[]{:S(2)}, u32[]{:S(2)}) collective-permute-start(bf16[4,256,256]{2,1,0:T(8,128)(2,1)S(1)} %pad_maximum_fusion.refs_0_), channel_id=1, source_target_pairs={{0,16},{8,72},{16,32},{24,88},{32,48},{40,104},{48,0},{56,120},{64... | collective-permute-start | bytes 1572872 | tf_op jit(solution)/shard_map/ppermute | solution.py:177
  111.1 14.5 %collective-permute-start.34 = (bf16[4,256,256]{2,1,0:T(8,128)(2,1)S(1)}, bf16[4,256,256]{2,1,0:T(8,128)(2,1)S(1)}, u32[]{:S(2)}, u32[]{:S(2)}) collective-permute-start(bf16[4,256,256]{2,1,0:T(8,128)(2,1)S(1)} %pad_maximum_fusion.refs_0_), channel_id=1, source_target_pairs={{0,32},{8,136},{16,48},{24,152},{32,0},{40,168},{48,16},{56,184},{... | collective-permute-start | bytes 1572872 | tf_op jit(solution)/shard_map/ppermute | solution.py:177
  113.2 16.8 %collective-permute-start.35 = (bf16[4,256,256]{2,1,0:T(8,128)(2,1)S(1)}, bf16[4,256,256]{2,1,0:T(8,128)(2,1)S(1)}, u32[]{:S(2)}, u32[]{:S(2)}) collective-permute-start(bf16[4,256,256]{2,1,0:T(8,128)(2,1)S(1)} %pad_maximum_fusion.refs_0_), channel_id=1, source_target_pairs={{0,48},{8,200},{16,0},{24,216},{32,16},{40,232},{48,32},{56,248},{... | collective-permute-start | bytes 1572872 | tf_op jit(solution)/shard_map/ppermute | solution.py:177
  113.8 16.5 %collective-permute-start.36 = (bf16[4,256,256]{2,1,0:T(8,128)(2,1)S(1)}, bf16[4,256,256]{2,1,0:T(8,128)(2,1)S(1)}, u32[]{:S(2)}, u32[]{:S(2)}) collective-permute-start(bf16[4,256,256]{2,1,0:T(8,128)(2,1)S(1)} %pad_maximum_fusion.refs_0_), channel_id=1, source_target_pairs={{0,8},{8,0},{16,24},{24,16},{32,40},{40,32},{48,56},{56,48},{64,72... | collective-permute-start | bytes 1572872 | tf_op jit(solution)/shard_map/ppermute | solution.py:178
  119.5 10.9 %collective-permute-start.37 = (bf16[4,256,256]{2,1,0:T(8,128)(2,1)S(1)}, bf16[4,256,256]{2,1,0:T(8,128)(2,1)S(1)}, u32[]{:S(2)}, u32[]{:S(2)}) collective-permute-start(bf16[4,256,256]{2,1,0:T(8,128)(2,1)S(1)} %collective-permute-done.33.refs_1_), channel_id=1, source_target_pairs={{0,8},{8,0},{16,24},{24,16},{32,40},{40,32},{48,56},{56,48},{64,72... | collective-permute-start | bytes 1572872 | tf_op jit(solution)/shard_map/ppermute | solution.py:178
  125.6 5.9 %collective-permute-start.38 = (bf16[4,256,256]{2,1,0:T(8,128)(2,1)S(1)}, bf16[4,256,256]{2,1,0:T(8,128)(2,1)S(1)}, u32[]{:S(2)}, u32[]{:S(2)}) collective-permute-start(bf16[4,256,256]{2,1,0:T(8,128)(2,1)S(1)} %collective-permute-done.34.refs_2_), channel_id=1, source_target_pairs={{0,8},{8,0},{16,24},{24,16},{32,40},{40,32},{48,56},{56,48},{64,72... | collective-permute-start | bytes 1572872 | tf_op jit(solution)/shard_map/ppermute | solution.py:178
  130.0 2.3 %collective-permute-start.39 = (bf16[4,256,256]{2,1,0:T(8,128)(2,1)S(1)}, bf16[4,256,256]{2,1,0:T(8,128)(2,1)S(1)}, u32[]{:S(2)}, u32[]{:S(2)}) collective-permute-start(bf16[4,256,256]{2,1,0:T(8,128)(2,1)S(1)} %collective-permute-done.35.refs_3_), channel_id=1, source_target_pairs={{0,8},{8,0},{16,24},{24,16},{32,40},{40,32},{48,56},{56,48},{64,72... | collective-permute-start | bytes 1572872 | tf_op jit(solution)/shard_map/ppermute | solution.py:178

commit v5 on v4

--- a/solution.py
+++ b/solution.py
@@ -134,9 +134,10 @@
     mine = lax.all_to_all(out_grads.reshape(panels, tokens, cols), "tensor", 0, 0)
     mine, acts = lax.optimization_barrier((mine, acts))
     peer = lax.ppermute(mine, "dp", CORE_SWAP)
-    grads = [
-        part if i == 0 else lax.ppermute(part, "dp", ring(i, 0)) for part in (mine, peer) for i in range(SIDE)
-    ]
+    up, down = lax.ppermute(mine, "dp", ring(1, 0)), lax.ppermute(mine, "dp", ring(3, 0))
+    grads = [mine, up, lax.ppermute(up, "dp", ring(1, 0)), down]
+    up, down = lax.ppermute(peer, "dp", ring(1, 0)), lax.ppermute(peer, "dp", ring(3, 0))
+    grads += [peer, up, lax.ppermute(down, "dp", ring(3, 0)), down]
 
     def product(*which):
         return mover(
@@ -149,22 +150,26 @@
     near = tuple(step for step in range(panels) if step not in far)
     f32 = jnp.float32
     moved = [
-        [lax.ppermute(part, "dp", ring(i, 1)) for i, part in zip((2, 1, 3), product((2, away), (1, away), (3, away)))]
+        [lax.ppermute(part, "dp", ring(i, 1)) for i, part in zip((2, 1, 3), product((2, away)) + product((1, away), (3, away)))]
         for away in (far, near)
     ]
     kept_parts = product((0, far), (0, near))
 
     def line(at):
-        return sum((part.astype(f32) for part in moved[at]), kept_parts[at].astype(f32)).astype(jnp.bfloat16)
+        return sum((part.astype(f32) for part in moved[at]), kept_parts[at].astype(f32))
 
     def along_tensor(part, step):
         return lax.ppermute(part, "tensor", [(i, (i + step) % panels) for i in range(panels)])
 
-    line_far = line(0)
-    terms = [along_tensor(line_far[i], step) for i, step in enumerate(far)]
-    line_near = line(1)
-    terms += [along_tensor(line_near[i], step) for i, step in enumerate(near) if step]
-    grad = sum((term.astype(f32) for term in terms), line_near[0].astype(f32))
+    half = panels // 2
+    at_half, at_up, at_down = line(0).astype(jnp.bfloat16)
+    joins_up, joins_down = along_tensor(at_up, 1), along_tensor(at_down, panels - 1)
+    halfway = along_tensor(at_half, half)
+    totals = dict(zip(near, line(1)))
+    totals[half // 2] += joins_up.astype(f32)
+    totals[panels - half // 2] += joins_down.astype(f32)
+    terms = [halfway] + [along_tensor(totals[step].astype(jnp.bfloat16), step) for step in near if step]
+    grad = sum((term.astype(f32) for term in terms), totals[0])
 
     new_first = 0.9 * first_moment + 0.1 * grad
     new_second = 0.999 * second_moment + 0.001 * grad * grad
@@ -173,8 +178,10 @@
     new_master = master * (1.0 - 0.05 * 0.1) - 0.05 * first_fix / (jnp.sqrt(second_fix) + 1e-08)
 
     own = new_master.astype(jnp.bfloat16)
-    line = jnp.stack([own] + [lax.ppermute(own, "dp", ring(i, 0)) for i in range(1, SIDE)])
-    own = [line] + [lax.ppermute(line, "dp", ring(i, 1)) for i in range(1, SIDE)]
+    moved = {i: lax.ppermute(own, "dp", ring(i, 0)) for i in (2, 1, 3)}
+    line = jnp.stack([own] + [moved[i] for i in range(1, SIDE)])
+    moved = {i: lax.ppermute(line, "dp", ring(i, 1)) for i in (2, 1, 3)}
+    own = [line] + [moved[i] for i in range(1, SIDE)]
     peer = [lax.ppermute(part, "dp", CORE_SWAP) for part in own]
     weights = pl.pallas_call(
         weights_kernel,

time: 135 us -> 129 us (0.956)
  starting transfers between devices: 78.2 us -> 72.7 us
    ppermute x4, starting transfers between devices: 13.9 us -> 8.18 us  [per_device(): peer = [lax.ppermute(part, 'dp', CORE_SWAP) for part in own]]
    ppermute x7, waiting for transfers between devices: 8.13 us -> 5.74 us  [along_tensor(): lax.ppermute(part, 'tensor', [(i, (i + step) % panels) for i in range(pan...]
    pallas_call x3 -> x5, Pallas kernels: 5.01 us -> 5.4 us  [product(): mover(functools.partial(product_kernel, which, rows), [kept((len(away), r...]
  transfers between devices with their start and end apart: 41 -> 41, of which waited for: 20 -> 21; matrix products, arithmetic and copies ran while one was open for 0% -> 1% of each run, Pallas kernels for 3% -> 4%
where the time goes in v5:
time: 129 us; the launch traced here: 128 us
  starting transfers between devices  72.7 us (56%)
  waiting for transfers between devices  43.4 us (34%)
  Pallas kernels  8.2 us (6%)
  other arithmetic  1.78 us (1%)
  local copies, waits for them, and re-layouts  1.65 us (1%)
    ppermute x7, starting transfers between devices, along_tensor(): lax.ppermute(part, 'tensor', [(i, (i + step) % panels) for i in range(pan...  15.8 us
    ppermute x6, starting transfers between devices, per_device(): lax.ppermute(part[i], 'dp', ring(i, 0))  10.5 us
    all_to_all x1, starting transfers between devices, per_device(): lax.all_to_all(out_grads.reshape(panels, tokens, cols), 'tensor', 0, 0)  9.03 us
    ppermute x4, starting transfers between devices, per_device(): peer = [lax.ppermute(part, 'dp', CORE_SWAP) for part in own]  8.18 us
    ppermute x3, waiting for transfers between devices, per_device(): moved = {i: lax.ppermute(line, 'dp', ring(i, 1)) for i in (2, 1, 3)}  7.87 us
    ppermute x6, starting transfers between devices, per_device(): lax.ppermute(part, 'dp', ring(i, 1))  7.79 us
    ppermute x7, waiting for transfers between devices, along_tensor(): lax.ppermute(part, 'tensor', [(i, (i + step) % panels) for i in range(pan...  5.74 us
    ppermute x6, waiting for transfers between devices, per_device(): lax.ppermute(part[i], 'dp', ring(i, 0))  5.51 us
  transfers between devices with their start and end apart: 41, of which 21 were waited for; matrix products, arithmetic and copies ran while one was open for 1% of the time, Pallas kernels for 4%

profile of v5, /device:TPU:1, one launch (start us, length us, event | category | flops | bytes accessed | tf_op | source)
XLA Modules:
  0.0 128.5 jit_solution(13858300439838521316)
XLA Ops:
  0.6 9.0 %all-to-all-start = ((bf16[8,128,256]{2,1,0:T(8,128)(2,1)}), bf16[8,128,256]{2,1,0:T(8,128)(2,1)S(1)}, u32[]{:S(2)}, u32[]{:S(2)}) async-start(bf16[8,128,256]{2,1,0:T(8,128)(2,1)} %bitcast.41), calls=%async_computation | async-start | bytes 1048576 | tf_op jit(solution)/shard_map/all_to_all | solution.py:134
  9.7 1.6 %copy-done = bf16[128,8192]{1,0:T(8,128)(2,1)S(1)} copy-done((bf16[128,8192]{1,0:T(8,128)(2,1)S(1)}, bf16[128,8192]{1,0:T(8,128)(2,1)}, u32[]{:S(2)}) %copy-start) | copy-done | bytes 2097176
  11.2 0.3 shard_map.84
  11.6 1.0 collective-permute-start.4
  12.7 0.4 collective-permute-start.8
  13.1 1.3 %collective-permute-start = (bf16[128,1024]{1,0:T(8,128)(2,1)S(1)}, bf16[128,1024]{1,0:T(8,128)(2,1)S(1)}, u32[]{:S(2)}, u32[]{:S(2)}) collective-permute-start(bf16[128,1024]{1,0:T(8,128)(2,1)S(1)} %get-tuple-element.28), channel_id=1, source_target_pairs={{0,64},{8,24},{16,80},{24,40},{32,96},{40,56},{48,112},{56,8},{64,... | collective-permute-start | bytes 786440 | tf_op jit(solution)/shard_map/ppermute | solution.py:129
  14.4 2.6 %collective-permute-start.1 = (bf16[128,1024]{1,0:T(8,128)(2,1)S(1)}, bf16[128,1024]{1,0:T(8,128)(2,1)S(1)}, u32[]{:S(2)}, u32[]{:S(2)}) collective-permute-start(bf16[128,1024]{1,0:T(8,128)(2,1)S(1)} %get-tuple-element.29), channel_id=1, source_target_pairs={{0,128},{8,40},{16,144},{24,56},{32,160},{40,8},{48,176},{56,24},{... | collective-permute-start | bytes 786440 | tf_op jit(solution)/shard_map/ppermute | solution.py:129
  17.0 1.1 collective-permute-start.2
  18.1 0.8 collective-permute-start.3
  18.9 1.3 %collective-permute-start.5 = (bf16[128,1024]{1,0:T(8,128)(2,1)S(1)}, bf16[128,1024]{1,0:T(8,128)(2,1)S(1)}, u32[]{:S(2)}, u32[]{:S(2)}) collective-permute-start(bf16[128,1024]{1,0:T(8,128)(2,1)S(1)} %collective-permute-done.4), channel_id=1, source_target_pairs={{0,64},{8,24},{16,80},{24,40},{32,96},{40,56},{48,112},{56,8},{64,... | collective-permute-start | bytes 786440 | tf_op jit(solution)/shard_map/ppermute | solution.py:129
  20.2 4.2 %collective-permute-start.7 = (bf16[128,1024]{1,0:T(8,128)(2,1)S(1)}, bf16[128,1024]{1,0:T(8,128)(2,1)S(1)}, u32[]{:S(2)}, u32[]{:S(2)}) collective-permute-start(bf16[128,1024]{1,0:T(8,128)(2,1)S(1)} %collective-permute-done.6), channel_id=1, source_target_pairs={{0,128},{8,40},{16,144},{24,56},{32,160},{40,8},{48,176},{56,24},{... | collective-permute-start | bytes 786440 | tf_op jit(solution)/shard_map/ppermute | solution.py:129
  24.4 2.3 %collective-permute-done.5.refs_5_ = bf16[128,1024]{1,0:T(8,128)(2,1)S(1)} collective-permute-done((bf16[128,1024]{1,0:T(8,128)(2,1)S(1)}, bf16[128,1024]{1,0:T(8,128)(2,1)S(1)}, u32[]{:S(2)}, u32[]{:S(2)}) %collective-permute-start.5) | collective-permute-done | bytes 262176 | tf_op jit(solution)/shard_map/ppermute | solution.py:129
  26.7 3.0 %collective-permute-done.7.refs_6_ = bf16[128,1024]{1,0:T(8,128)(2,1)S(1)} collective-permute-done((bf16[128,1024]{1,0:T(8,128)(2,1)S(1)}, bf16[128,1024]{1,0:T(8,128)(2,1)S(1)}, u32[]{:S(2)}, u32[]{:S(2)}) %collective-permute-start.7) | collective-permute-done | bytes 262176 | tf_op jit(solution)/shard_map/ppermute | solution.py:129
  29.7 0.2 collective-permute-done.9.refs_7_
  29.9 1.2 collective-permute-start.13
  31.1 1.3 %collective-permute-start.10 = (bf16[8,128,256]{2,1,0:T(8,128)(2,1)S(1)}, bf16[8,128,256]{2,1,0:T(8,128)(2,1)S(1)}, u32[]{:S(2)}, u32[]{:S(2)}) collective-permute-start(bf16[8,128,256]{2,1,0:T(8,128)(2,1)S(1)} %all-to-all-done.refs_8_), channel_id=1, source_target_pairs={{0,64},{8,24},{16,80},{24,40},{32,96},{40,56},{48,112},{56,8},{64,... | collective-permute-start | bytes 1572872 | tf_op jit(solution)/shard_map/ppermute | solution.py:137
  32.4 0.2 collective-permute-done.13.refs_12_
  32.6 2.7 %collective-permute-start.15 = (bf16[8,128,256]{2,1,0:T(8,128)(2,1)S(1)}, bf16[8,128,256]{2,1,0:T(8,128)(2,1)S(1)}, u32[]{:S(2)}, u32[]{:S(2)}) collective-permute-start(bf16[8,128,256]{2,1,0:T(8,128)(2,1)S(1)} %collective-permute-done.13.refs_12_), channel_id=1, source_target_pairs={{0,192},{8,56},{16,208},{24,8},{32,224},{40,24},{48,240},{56,40},{... | collective-permute-start | bytes 1572872 | tf_op jit(solution)/shard_map/ppermute | solution.py:139
  35.3 0.5 collective-permute-start.12
  35.8 1.0 collective-permute-start.14
  36.8 3.9 %collective-permute-done.10.refs_9_ = bf16[8,128,256]{2,1,0:T(8,128)(2,1)S(1)} collective-permute-done((bf16[8,128,256]{2,1,0:T(8,128)(2,1)S(1)}, bf16[8,128,256]{2,1,0:T(8,128)(2,1)S(1)}, u32[]{:S(2)}, u32[]{:S(2)}) %collective-permute-start.10) | collective-permute-done | bytes 524320 | tf_op jit(solution)/shard_map/ppermute | solution.py:137
  40.7 0.8 collective-permute-done.15.refs_15_
  41.5 3.4 %collective-permute-start.16 = (bf16[8,128,256]{2,1,0:T(8,128)(2,1)S(1)}, bf16[8,128,256]{2,1,0:T(8,128)(2,1)S(1)}, u32[]{:S(2)}, u32[]{:S(2)}) collective-permute-start(bf16[8,128,256]{2,1,0:T(8,128)(2,1)S(1)} %collective-permute-done.15.refs_15_), channel_id=1, source_target_pairs={{0,192},{8,56},{16,208},{24,8},{32,224},{40,24},{48,240},{56,40},{... | collective-permute-start | bytes 1572872 | tf_op jit(solution)/shard_map/ppermute | solution.py:140
  44.9 2.2 %collective-permute-done.12.refs_11_ = bf16[8,128,256]{2,1,0:T(8,128)(2,1)S(1)} collective-permute-done((bf16[8,128,256]{2,1,0:T(8,128)(2,1)S(1)}, bf16[8,128,256]{2,1,0:T(8,128)(2,1)S(1)}, u32[]{:S(2)}, u32[]{:S(2)}) %collective-permute-start.12) | collective-permute-done | bytes 524320 | tf_op jit(solution)/shard_map/ppermute | solution.py:137
  47.1 4.8 %collective-permute-done.11.refs_10_ = bf16[8,128,256]{2,1,0:T(8,128)(2,1)S(1)} collective-permute-done((bf16[8,128,256]{2,1,0:T(8,128)(2,1)S(1)}, bf16[8,128,256]{2,1,0:T(8,128)(2,1)S(1)}, u32[]{:S(2)}, u32[]{:S(2)}) %collective-permute-start.11) | collective-permute-done | bytes 524320 | tf_op jit(solution)/shard_map/ppermute | solution.py:138
  51.9 0.8 collective-permute-done.16.refs_14_
  52.7 0.6 shard_map.88
  53.3 1.9 %collective-permute-start.20 = (bf16[3,256,256]{2,1,0:T(8,128)(2,1)S(1)}, bf16[3,256,256]{2,1,0:T(8,128)(2,1)S(1)}, u32[]{:S(2)}, u32[]{:S(2)}) collective-permute-start(bf16[3,256,256]{2,1,0:T(8,128)(2,1)S(1)} %shard_map.88), channel_id=1, source_target_pairs={{0,32},{8,136},{16,48},{24,152},{32,0},{40,168},{48,16},{56,184},{... | collective-permute-start | bytes 1179656 | tf_op jit(solution)/shard_map/ppermute | solution.py:153
  55.3 1.0 shard_map.89
  56.3 0.5 collective-permute-start.21
  56.8 2.3 %collective-permute-start.22 = (bf16[3,256,256]{2,1,0:T(8,128)(2,1)S(1)}, bf16[3,256,256]{2,1,0:T(8,128)(2,1)S(1)}, u32[]{:S(2)}, u32[]{:S(2)}) collective-permute-start(bf16[3,256,256]{2,1,0:T(8,128)(2,1)S(1)} %get-tuple-element.49), channel_id=1, source_target_pairs={{0,48},{8,200},{16,0},{24,216},{32,16},{40,232},{48,32},{56,248},{... | collective-permute-start | bytes 1179656 | tf_op jit(solution)/shard_map/ppermute | solution.py:153
  59.1 0.9 shard_map.86
  60.0 0.3 collective-permute-start.17
  60.3 1.6 %shard_map.87 = (bf16[5,256,256]{2,1,0:T(8,128)(2,1)S(1)}, bf16[5,256,256]{2,1,0:T(8,128)(2,1)S(1)}) custom-call(bf16[128,1024]{1,0:T(8,128)(2,1)S(1)} %get-tuple-element.35.refs_0_, bf16[128,1024]{1,0:T(8,128)(2,1)S(1)} %collective-permute-done.refs_1_, bf16[128,1024]{1,0:T(8,128)(2,1)S(1)} %collective-permute-done.1.refs_2_, ...), custom_call_target="tpu_custom_call" | custom-call | tf_op jit(solution)/shard_map/pallas_call | solution.py:143
  61.9 0.9 collective-permute-start.18
  62.8 1.8 %collective-permute-start.19 = (bf16[5,256,256]{2,1,0:T(8,128)(2,1)S(1)}, bf16[5,256,256]{2,1,0:T(8,128)(2,1)S(1)}, u32[]{:S(2)}, u32[]{:S(2)}) collective-permute-start(bf16[5,256,256]{2,1,0:T(8,128)(2,1)S(1)} %get-tuple-element.46), channel_id=1, source_target_pairs={{0,48},{8,200},{16,0},{24,216},{32,16},{40,232},{48,32},{56,248},{... | collective-permute-start | bytes 1966088 | tf_op jit(solution)/shard_map/ppermute | solution.py:153
  64.6 1.3 shard_map.85
  65.9 0.1 collective-permute-done.21
  66.1 0.2 add_convert_fusion
  66.3 1.8 %collective-permute-start.25 = (bf16[256,256]{1,0:T(8,128)(2,1)S(1)}, bf16[256,256]{1,0:T(8,128)(2,1)S(1)}, u32[]{:S(2)}, u32[]{:S(2)}) collective-permute-start(bf16[256,256]{1,0:T(8,128)(2,1)S(1)} %get-tuple-element.62), channel_id=1, source_target_pairs={{0,1},{1,2},{2,3},{3,4},{4,5},{5,6},{6,7},{7,0},{8,9},{9,10},{10,1... | collective-permute-start | bytes 393224 | tf_op jit(solution)/shard_map/ppermute | solution.py:162
  68.1 1.3 %collective-permute-start.27 = (bf16[256,256]{1,0:T(8,128)(2,1)S(1)}, bf16[256,256]{1,0:T(8,128)(2,1)S(1)}, u32[]{:S(2)}, u32[]{:S(2)}) collective-permute-start(bf16[256,256]{1,0:T(8,128)(2,1)S(1)} %get-tuple-element.61), channel_id=1, source_target_pairs={{0,7},{1,0},{2,1},{3,2},{4,3},{5,4},{6,5},{7,6},{8,15},{9,8},{10,9... | collective-permute-start | bytes 393224 | tf_op jit(solution)/shard_map/ppermute | solution.py:162
  69.4 3.7 %collective-permute-done.17 = bf16[5,256,256]{2,1,0:T(8,128)(2,1)S(1)} collective-permute-done((bf16[5,256,256]{2,1,0:T(8,128)(2,1)S(1)}, bf16[5,256,256]{2,1,0:T(8,128)(2,1)S(1)}, u32[]{:S(2)}, u32[]{:S(2)}) %collective-permute-start.17) | collective-permute-done | bytes 655392 | tf_op jit(solution)/shard_map/ppermute | solution.py:153
  73.1 5.7 %collective-permute-start.23 = (bf16[256,256]{1,0:T(8,128)(2,1)S(1)}, bf16[256,256]{1,0:T(8,128)(2,1)S(1)}, u32[]{:S(2)}, u32[]{:S(2)}) collective-permute-start(bf16[256,256]{1,0:T(8,128)(2,1)S(1)} %get-tuple-element.60), channel_id=1, source_target_pairs={{0,4},{1,5},{2,6},{3,7},{4,0},{5,1},{6,2},{7,3},{8,12},{9,13},{10,... | collective-permute-start | bytes 393224 | tf_op jit(solution)/shard_map/ppermute | solution.py:162
  78.8 1.3 %collective-permute-done.18 = bf16[5,256,256]{2,1,0:T(8,128)(2,1)S(1)} collective-permute-done((bf16[5,256,256]{2,1,0:T(8,128)(2,1)S(1)}, bf16[5,256,256]{2,1,0:T(8,128)(2,1)S(1)}, u32[]{:S(2)}, u32[]{:S(2)}) %collective-permute-start.18) | collective-permute-done | bytes 655392 | tf_op jit(solution)/shard_map/ppermute | solution.py:153
  80.1 0.4 fusion.12
  80.6 2.7 %collective-permute-start.26 = (bf16[256,256]{1,0:T(8,128)(2,1)S(1)}, bf16[256,256]{1,0:T(8,128)(2,1)S(1)}, u32[]{:S(2)}, u32[]{:S(2)}) collective-permute-start(bf16[256,256]{1,0:T(8,128)(2,1)S(1)} %get-tuple-element.56), channel_id=1, source_target_pairs={{0,2},{1,3},{2,4},{3,5},{4,6},{5,7},{6,0},{7,1},{8,10},{9,11},{10,... | collective-permute-start | bytes 393224 | tf_op jit(solution)/shard_map/ppermute | solution.py:162
  83.3 1.5 %collective-permute-start.28 = (bf16[256,256]{1,0:T(8,128)(2,1)S(1)}, bf16[256,256]{1,0:T(8,128)(2,1)S(1)}, u32[]{:S(2)}, u32[]{:S(2)}) collective-permute-start(bf16[256,256]{1,0:T(8,128)(2,1)S(1)} %get-tuple-element.57), channel_id=1, source_target_pairs={{0,6},{1,7},{2,0},{3,1},{4,2},{5,3},{6,4},{7,5},{8,14},{9,15},{10,... | collective-permute-start | bytes 393224 | tf_op jit(solution)/shard_map/ppermute | solution.py:162
  84.9 1.2 collective-permute-start.24
  86.1 1.5 %collective-permute-start.29 = (bf16[256,256]{1,0:T(8,128)(2,1)S(1)}, bf16[256,256]{1,0:T(8,128)(2,1)S(1)}, u32[]{:S(2)}, u32[]{:S(2)}) collective-permute-start(bf16[256,256]{1,0:T(8,128)(2,1)S(1)} %get-tuple-element.59), channel_id=1, source_target_pairs={{0,7},{1,0},{2,1},{3,2},{4,3},{5,4},{6,5},{7,6},{8,15},{9,8},{10,9... | collective-permute-start | bytes 393224 | tf_op jit(solution)/shard_map/ppermute | solution.py:162
  87.8 4.3 %collective-permute-done.28 = bf16[256,256]{1,0:T(8,128)(2,1)S(1)} collective-permute-done((bf16[256,256]{1,0:T(8,128)(2,1)S(1)}, bf16[256,256]{1,0:T(8,128)(2,1)S(1)}, u32[]{:S(2)}, u32[]{:S(2)}) %collective-permute-start.28) | collective-permute-done | bytes 131104 | tf_op jit(solution)/shard_map/ppermute | solution.py:162
  92.1 1.3 %collective-permute-done.24 = bf16[256,256]{1,0:T(8,128)(2,1)S(1)} collective-permute-done((bf16[256,256]{1,0:T(8,128)(2,1)S(1)}, bf16[256,256]{1,0:T(8,128)(2,1)S(1)}, u32[]{:S(2)}, u32[]{:S(2)}) %collective-permute-start.24) | collective-permute-done | bytes 131104 | tf_op jit(solution)/shard_map/ppermute | solution.py:162
  93.4 1.1 fusion.10
  94.5 4.9 %collective-permute-start.31 = (bf16[256,256]{1,0:T(8,128)(2,1)S(1)}, bf16[256,256]{1,0:T(8,128)(2,1)S(1)}, u32[]{:S(2)}, u32[]{:S(2)}) collective-permute-start(bf16[256,256]{1,0:T(8,128)(2,1)S(1)} %get-tuple-element.50), channel_id=1, source_target_pairs={{0,128},{8,40},{16,144},{24,56},{32,160},{40,8},{48,176},{56,24},{... | collective-permute-start | bytes 393224 | tf_op jit(solution)/shard_map/ppermute | solution.py:181
  99.4 1.2 collective-permute-done.30
  100.6 2.9 %collective-permute-done.31 = bf16[256,256]{1,0:T(8,128)(2,1)S(1)} collective-permute-done((bf16[256,256]{1,0:T(8,128)(2,1)S(1)}, bf16[256,256]{1,0:T(8,128)(2,1)S(1)}, u32[]{:S(2)}, u32[]{:S(2)}) %collective-permute-start.31) | collective-permute-done | bytes 131104 | tf_op jit(solution)/shard_map/ppermute | solution.py:181
  103.6 1.3 collective-permute-start.33
  104.9 0.9 collective-permute-start.34
  105.8 1.9 %collective-permute-start.35 = (bf16[4,256,256]{2,1,0:T(8,128)(2,1)S(1)}, bf16[4,256,256]{2,1,0:T(8,128)(2,1)S(1)}, u32[]{:S(2)}, u32[]{:S(2)}) collective-permute-start(bf16[4,256,256]{2,1,0:T(8,128)(2,1)S(1)} %pad_maximum_fusion.refs_0_), channel_id=1, source_target_pairs={{0,48},{8,200},{16,0},{24,216},{32,16},{40,232},{48,32},{56,248},{... | collective-permute-start | bytes 1572872 | tf_op jit(solution)/shard_map/ppermute | solution.py:183
  107.7 3.3 %collective-permute-start.36 = (bf16[4,256,256]{2,1,0:T(8,128)(2,1)S(1)}, bf16[4,256,256]{2,1,0:T(8,128)(2,1)S(1)}, u32[]{:S(2)}, u32[]{:S(2)}) collective-permute-start(bf16[4,256,256]{2,1,0:T(8,128)(2,1)S(1)} %pad_maximum_fusion.refs_0_), channel_id=1, source_target_pairs={{0,8},{8,0},{16,24},{24,16},{32,40},{40,32},{48,56},{56,48},{64,72... | collective-permute-start | bytes 1572872 | tf_op jit(solution)/shard_map/ppermute | solution.py:185
  110.9 7.9 %collective-permute-done.33.refs_1_ = bf16[4,256,256]{2,1,0:T(8,128)(2,1)S(1)} collective-permute-done((bf16[4,256,256]{2,1,0:T(8,128)(2,1)S(1)}, bf16[4,256,256]{2,1,0:T(8,128)(2,1)S(1)}, u32[]{:S(2)}, u32[]{:S(2)}) %collective-permute-start.33) | collective-permute-done | bytes 524320 | tf_op jit(solution)/shard_map/ppermute | solution.py:183
  118.8 4.9 %collective-permute-start.38 = (bf16[4,256,256]{2,1,0:T(8,128)(2,1)S(1)}, bf16[4,256,256]{2,1,0:T(8,128)(2,1)S(1)}, u32[]{:S(2)}, u32[]{:S(2)}) collective-permute-start(bf16[4,256,256]{2,1,0:T(8,128)(2,1)S(1)} %collective-permute-done.34.refs_2_), channel_id=1, source_target_pairs={{0,8},{8,0},{16,24},{24,16},{32,40},{40,32},{48,56},{56,48},{64,72... | collective-permute-start | bytes 1572872 | tf_op jit(solution)/shard_map/ppermute | solution.py:185
  123.7 1.5 %collective-permute-done.38.refs_6_ = bf16[4,256,256]{2,1,0:T(8,128)(2,1)S(1)} collective-permute-done((bf16[4,256,256]{2,1,0:T(8,128)(2,1)S(1)}, bf16[4,256,256]{2,1,0:T(8,128)(2,1)S(1)}, u32[]{:S(2)}, u32[]{:S(2)}) %collective-permute-start.38) | collective-permute-done | bytes 524320 | tf_op jit(solution)/shard_map/ppermute | solution.py:185
  125.2 0.7 collective-permute-done.39.refs_7_
  126.0 2.5 %shard_map.90 = bf16[4,4,2,256,256]{4,3,2,1,0:T(8,128)(2,1)} custom-call(bf16[4,256,256]{2,1,0:T(8,128)(2,1)S(1)} %pad_maximum_fusion.refs_0_, bf16[4,256,256]{2,1,0:T(8,128)(2,1)S(1)} %collective-permute-done.33.refs_1_, bf16[4,256,256]{2,1,0:T(8,128)(2,1)S(1)} %collective-permute-done.34.refs_2_, bf16[4,256,256]{2,1,0:T(8,128)(2,1)S(1)} %collective-permute-done.35.refs_3_, ...), custom_call_target="tpu_custom_call" | custom-call | tf_op jit(solution)/shard_map/pallas_call | solution.py:186
  (40 shorter events, 0.6 us)
Async XLA Ops:
  0.6 29.3 %all-to-all-start = ((bf16[8,128,256]{2,1,0:T(8,128)(2,1)}), bf16[8,128,256]{2,1,0:T(8,128)(2,1)S(1)}, u32[]{:S(2)}, u32[]{:S(2)}) async-start(bf16[8,128,256]{2,1,0:T(8,128)(2,1)} %bitcast.41), calls=%async_computation | async-start | bytes 1048576 | tf_op jit(solution)/shard_map/all_to_all | solution.py:134
  9.7 1.6 %copy-start = (bf16[128,8192]{1,0:T(8,128)(2,1)S(1)}, bf16[128,8192]{1,0:T(8,128)(2,1)}, u32[]{:S(2)}) copy-start(bf16[128,8192]{1,0:T(8,128)(2,1)} %acts.1) | copy-start | bytes 6291460
  11.6 5.5 %collective-permute-start.4 = (bf16[128,1024]{1,0:T(8,128)(2,1)S(1)}, bf16[128,1024]{1,0:T(8,128)(2,1)S(1)}, u32[]{:S(2)}, u32[]{:S(2)}) collective-permute-start(bf16[128,1024]{1,0:T(8,128)(2,1)S(1)} %get-tuple-element.32), channel_id=1, source_target_pairs={{0,8},{8,0},{16,24},{24,16},{32,40},{40,32},{48,56},{56,48},{64,72... | collective-permute-start | bytes 786440 | tf_op jit(solution)/shard_map/ppermute | solution.py:127
  12.6 5.5 %collective-permute-start.6 = (bf16[128,1024]{1,0:T(8,128)(2,1)S(1)}, bf16[128,1024]{1,0:T(8,128)(2,1)S(1)}, u32[]{:S(2)}, u32[]{:S(2)}) collective-permute-start(bf16[128,1024]{1,0:T(8,128)(2,1)S(1)} %get-tuple-element.33), channel_id=1, source_target_pairs={{0,8},{8,0},{16,24},{24,16},{32,40},{40,32},{48,56},{56,48},{64,72... | collective-permute-start | bytes 786440 | tf_op jit(solution)/shard_map/ppermute | solution.py:127
  12.7 6.2 %collective-permute-start.8 = (bf16[128,1024]{1,0:T(8,128)(2,1)S(1)}, bf16[128,1024]{1,0:T(8,128)(2,1)S(1)}, u32[]{:S(2)}, u32[]{:S(2)}) collective-permute-start(bf16[128,1024]{1,0:T(8,128)(2,1)S(1)} %get-tuple-element.34), channel_id=1, source_target_pairs={{0,8},{8,0},{16,24},{24,16},{32,40},{40,32},{48,56},{56,48},{64,72... | collective-permute-start | bytes 786440 | tf_op jit(solution)/shard_map/ppermute | solution.py:127
  13.1 7.1 %collective-permute-start = (bf16[128,1024]{1,0:T(8,128)(2,1)S(1)}, bf16[128,1024]{1,0:T(8,128)(2,1)S(1)}, u32[]{:S(2)}, u32[]{:S(2)}) collective-permute-start(bf16[128,1024]{1,0:T(8,128)(2,1)S(1)} %get-tuple-element.28), channel_id=1, source_target_pairs={{0,64},{8,24},{16,80},{24,40},{32,96},{40,56},{48,112},{56,8},{64,... | collective-permute-start | bytes 786440 | tf_op jit(solution)/shard_map/ppermute | solution.py:129
  14.4 9.9 %collective-permute-start.1 = (bf16[128,1024]{1,0:T(8,128)(2,1)S(1)}, bf16[128,1024]{1,0:T(8,128)(2,1)S(1)}, u32[]{:S(2)}, u32[]{:S(2)}) collective-permute-start(bf16[128,1024]{1,0:T(8,128)(2,1)S(1)} %get-tuple-element.29), channel_id=1, source_target_pairs={{0,128},{8,40},{16,144},{24,56},{32,160},{40,8},{48,176},{56,24},{... | collective-permute-start | bytes 786440 | tf_op jit(solution)/shard_map/ppermute | solution.py:129
  17.0 7.3 %collective-permute-start.2 = (bf16[128,1024]{1,0:T(8,128)(2,1)S(1)}, bf16[128,1024]{1,0:T(8,128)(2,1)S(1)}, u32[]{:S(2)}, u32[]{:S(2)}) collective-permute-start(bf16[128,1024]{1,0:T(8,128)(2,1)S(1)} %get-tuple-element.30), channel_id=1, source_target_pairs={{0,192},{8,56},{16,208},{24,8},{32,224},{40,24},{48,240},{56,40},{... | collective-permute-start | bytes 786440 | tf_op jit(solution)/shard_map/ppermute | solution.py:129
  18.1 6.3 %collective-permute-start.3 = (bf16[128,1024]{1,0:T(8,128)(2,1)S(1)}, bf16[128,1024]{1,0:T(8,128)(2,1)S(1)}, u32[]{:S(2)}, u32[]{:S(2)}) collective-permute-start(bf16[128,1024]{1,0:T(8,128)(2,1)S(1)} %get-tuple-element.31), channel_id=1, source_target_pairs={{0,8},{8,0},{16,24},{24,16},{32,40},{40,32},{48,56},{56,48},{64,72... | collective-permute-start | bytes 786440 | tf_op jit(solution)/shard_map/ppermute | solution.py:127
  18.9 7.8 %collective-permute-start.5 = (bf16[128,1024]{1,0:T(8,128)(2,1)S(1)}, bf16[128,1024]{1,0:T(8,128)(2,1)S(1)}, u32[]{:S(2)}, u32[]{:S(2)}) collective-permute-start(bf16[128,1024]{1,0:T(8,128)(2,1)S(1)} %collective-permute-done.4), channel_id=1, source_target_pairs={{0,64},{8,24},{16,80},{24,40},{32,96},{40,56},{48,112},{56,8},{64,... | collective-permute-start | bytes 786440 | tf_op jit(solution)/shard_map/ppermute | solution.py:129
  20.2 9.5 %collective-permute-start.7 = (bf16[128,1024]{1,0:T(8,128)(2,1)S(1)}, bf16[128,1024]{1,0:T(8,128)(2,1)S(1)}, u32[]{:S(2)}, u32[]{:S(2)}) collective-permute-start(bf16[128,1024]{1,0:T(8,128)(2,1)S(1)} %collective-permute-done.6), channel_id=1, source_target_pairs={{0,128},{8,40},{16,144},{24,56},{32,160},{40,8},{48,176},{56,24},{... | collective-permute-start | bytes 786440 | tf_op jit(solution)/shard_map/ppermute | solution.py:129
  24.4 5.5 %collective-permute-start.9 = (bf16[128,1024]{1,0:T(8,128)(2,1)S(1)}, bf16[128,1024]{1,0:T(8,128)(2,1)S(1)}, u32[]{:S(2)}, u32[]{:S(2)}) collective-permute-start(bf16[128,1024]{1,0:T(8,128)(2,1)S(1)} %collective-permute-done.8), channel_id=1, source_target_pairs={{0,192},{8,56},{16,208},{24,8},{32,224},{40,24},{48,240},{56,40},{... | collective-permute-start | bytes 786440 | tf_op jit(solution)/shard_map/ppermute | solution.py:129
  29.9 2.7 %collective-permute-start.13 = (bf16[8,128,256]{2,1,0:T(8,128)(2,1)S(1)}, bf16[8,128,256]{2,1,0:T(8,128)(2,1)S(1)}, u32[]{:S(2)}, u32[]{:S(2)}) collective-permute-start(bf16[8,128,256]{2,1,0:T(8,128)(2,1)S(1)} %all-to-all-done.refs_8_), channel_id=1, source_target_pairs={{0,8},{8,0},{16,24},{24,16},{32,40},{40,32},{48,56},{56,48},{64,72... | collective-permute-start | bytes 1572872 | tf_op jit(solution)/shard_map/ppermute | solution.py:136
  31.1 9.6 %collective-permute-start.10 = (bf16[8,128,256]{2,1,0:T(8,128)(2,1)S(1)}, bf16[8,128,256]{2,1,0:T(8,128)(2,1)S(1)}, u32[]{:S(2)}, u32[]{:S(2)}) collective-permute-start(bf16[8,128,256]{2,1,0:T(8,128)(2,1)S(1)} %all-to-all-done.refs_8_), channel_id=1, source_target_pairs={{0,64},{8,24},{16,80},{24,40},{32,96},{40,56},{48,112},{56,8},{64,... | collective-permute-start | bytes 1572872 | tf_op jit(solution)/shard_map/ppermute | solution.py:137
  32.6 8.9 %collective-permute-start.15 = (bf16[8,128,256]{2,1,0:T(8,128)(2,1)S(1)}, bf16[8,128,256]{2,1,0:T(8,128)(2,1)S(1)}, u32[]{:S(2)}, u32[]{:S(2)}) collective-permute-start(bf16[8,128,256]{2,1,0:T(8,128)(2,1)S(1)} %collective-permute-done.13.refs_12_), channel_id=1, source_target_pairs={{0,192},{8,56},{16,208},{24,8},{32,224},{40,24},{48,240},{56,40},{... | collective-permute-start | bytes 1572872 | tf_op jit(solution)/shard_map/ppermute | solution.py:139
  35.3 11.7 %collective-permute-start.12 = (bf16[8,128,256]{2,1,0:T(8,128)(2,1)S(1)}, bf16[8,128,256]{2,1,0:T(8,128)(2,1)S(1)}, u32[]{:S(2)}, u32[]{:S(2)}) collective-permute-start(bf16[8,128,256]{2,1,0:T(8,128)(2,1)S(1)} %all-to-all-done.refs_8_), channel_id=1, source_target_pairs={{0,192},{8,56},{16,208},{24,8},{32,224},{40,24},{48,240},{56,40},{... | collective-permute-start | bytes 1572872 | tf_op jit(solution)/shard_map/ppermute | solution.py:137
  35.8 11.3 %collective-permute-start.14 = (bf16[8,128,256]{2,1,0:T(8,128)(2,1)S(1)}, bf16[8,128,256]{2,1,0:T(8,128)(2,1)S(1)}, u32[]{:S(2)}, u32[]{:S(2)}) collective-permute-start(bf16[8,128,256]{2,1,0:T(8,128)(2,1)S(1)} %collective-permute-done.13.refs_12_), channel_id=1, source_target_pairs={{0,64},{8,24},{16,80},{24,40},{32,96},{40,56},{48,112},{56,8},{64,... | collective-permute-start | bytes 1572872 | tf_op jit(solution)/shard_map/ppermute | solution.py:139
  40.7 11.2 %collective-permute-start.11 = (bf16[8,128,256]{2,1,0:T(8,128)(2,1)S(1)}, bf16[8,128,256]{2,1,0:T(8,128)(2,1)S(1)}, u32[]{:S(2)}, u32[]{:S(2)}) collective-permute-start(bf16[8,128,256]{2,1,0:T(8,128)(2,1)S(1)} %collective-permute-done.10.refs_9_), channel_id=1, source_target_pairs={{0,64},{8,24},{16,80},{24,40},{32,96},{40,56},{48,112},{56,8},{64,... | collective-permute-start | bytes 1572872 | tf_op jit(solution)/shard_map/ppermute | solution.py:138
  41.5 11.2 %collective-permute-start.16 = (bf16[8,128,256]{2,1,0:T(8,128)(2,1)S(1)}, bf16[8,128,256]{2,1,0:T(8,128)(2,1)S(1)}, u32[]{:S(2)}, u32[]{:S(2)}) collective-permute-start(bf16[8,128,256]{2,1,0:T(8,128)(2,1)S(1)} %collective-permute-done.15.refs_15_), channel_id=1, source_target_pairs={{0,192},{8,56},{16,208},{24,8},{32,224},{40,24},{48,240},{56,40},{... | collective-permute-start | bytes 1572872 | tf_op jit(solution)/shard_map/ppermute | solution.py:140
  53.3 9.5 %collective-permute-start.20 = (bf16[3,256,256]{2,1,0:T(8,128)(2,1)S(1)}, bf16[3,256,256]{2,1,0:T(8,128)(2,1)S(1)}, u32[]{:S(2)}, u32[]{:S(2)}) collective-permute-start(bf16[3,256,256]{2,1,0:T(8,128)(2,1)S(1)} %shard_map.88), channel_id=1, source_target_pairs={{0,32},{8,136},{16,48},{24,152},{32,0},{40,168},{48,16},{56,184},{... | collective-permute-start | bytes 1179656 | tf_op jit(solution)/shard_map/ppermute | solution.py:153
  56.3 9.8 %collective-permute-start.21 = (bf16[3,256,256]{2,1,0:T(8,128)(2,1)S(1)}, bf16[3,256,256]{2,1,0:T(8,128)(2,1)S(1)}, u32[]{:S(2)}, u32[]{:S(2)}) collective-permute-start(bf16[3,256,256]{2,1,0:T(8,128)(2,1)S(1)} %get-tuple-element.48), channel_id=1, source_target_pairs={{0,16},{8,72},{16,32},{24,88},{32,48},{40,104},{48,0},{56,120},{64... | collective-permute-start | bytes 1179656 | tf_op jit(solution)/shard_map/ppermute | solution.py:153
  56.8 9.3 %collective-permute-start.22 = (bf16[3,256,256]{2,1,0:T(8,128)(2,1)S(1)}, bf16[3,256,256]{2,1,0:T(8,128)(2,1)S(1)}, u32[]{:S(2)}, u32[]{:S(2)}) collective-permute-start(bf16[3,256,256]{2,1,0:T(8,128)(2,1)S(1)} %get-tuple-element.49), channel_id=1, source_target_pairs={{0,48},{8,200},{16,0},{24,216},{32,16},{40,232},{48,32},{56,248},{... | collective-permute-start | bytes 1179656 | tf_op jit(solution)/shard_map/ppermute | solution.py:153
  60.0 13.2 %collective-permute-start.17 = (bf16[5,256,256]{2,1,0:T(8,128)(2,1)S(1)}, bf16[5,256,256]{2,1,0:T(8,128)(2,1)S(1)}, u32[]{:S(2)}, u32[]{:S(2)}) collective-permute-start(bf16[5,256,256]{2,1,0:T(8,128)(2,1)S(1)} %shard_map.86), channel_id=1, source_target_pairs={{0,32},{8,136},{16,48},{24,152},{32,0},{40,168},{48,16},{56,184},{... | collective-permute-start | bytes 1966088 | tf_op jit(solution)/shard_map/ppermute | solution.py:153
  61.9 18.2 %collective-permute-start.18 = (bf16[5,256,256]{2,1,0:T(8,128)(2,1)S(1)}, bf16[5,256,256]{2,1,0:T(8,128)(2,1)S(1)}, u32[]{:S(2)}, u32[]{:S(2)}) collective-permute-start(bf16[5,256,256]{2,1,0:T(8,128)(2,1)S(1)} %get-tuple-element.45), channel_id=1, source_target_pairs={{0,16},{8,72},{16,32},{24,88},{32,48},{40,104},{48,0},{56,120},{64... | collective-permute-start | bytes 1966088 | tf_op jit(solution)/shard_map/ppermute | solution.py:153
  62.8 17.3 %collective-permute-start.19 = (bf16[5,256,256]{2,1,0:T(8,128)(2,1)S(1)}, bf16[5,256,256]{2,1,0:T(8,128)(2,1)S(1)}, u32[]{:S(2)}, u32[]{:S(2)}) collective-permute-start(bf16[5,256,256]{2,1,0:T(8,128)(2,1)S(1)} %get-tuple-element.46), channel_id=1, source_target_pairs={{0,48},{8,200},{16,0},{24,216},{32,16},{40,232},{48,32},{56,248},{... | collective-permute-start | bytes 1966088 | tf_op jit(solution)/shard_map/ppermute | solution.py:153
  66.3 14.2 %collective-permute-start.25 = (bf16[256,256]{1,0:T(8,128)(2,1)S(1)}, bf16[256,256]{1,0:T(8,128)(2,1)S(1)}, u32[]{:S(2)}, u32[]{:S(2)}) collective-permute-start(bf16[256,256]{1,0:T(8,128)(2,1)S(1)} %get-tuple-element.62), channel_id=1, source_target_pairs={{0,1},{1,2},{2,3},{3,4},{4,5},{5,6},{6,7},{7,0},{8,9},{9,10},{10,1... | collective-permute-start | bytes 393224 | tf_op jit(solution)/shard_map/ppermute | solution.py:162
  68.1 12.4 %collective-permute-start.27 = (bf16[256,256]{1,0:T(8,128)(2,1)S(1)}, bf16[256,256]{1,0:T(8,128)(2,1)S(1)}, u32[]{:S(2)}, u32[]{:S(2)}) collective-permute-start(bf16[256,256]{1,0:T(8,128)(2,1)S(1)} %get-tuple-element.61), channel_id=1, source_target_pairs={{0,7},{1,0},{2,1},{3,2},{4,3},{5,4},{6,5},{7,6},{8,15},{9,8},{10,9... | collective-permute-start | bytes 393224 | tf_op jit(solution)/shard_map/ppermute | solution.py:162
  73.1 14.5 %collective-permute-start.23 = (bf16[256,256]{1,0:T(8,128)(2,1)S(1)}, bf16[256,256]{1,0:T(8,128)(2,1)S(1)}, u32[]{:S(2)}, u32[]{:S(2)}) collective-permute-start(bf16[256,256]{1,0:T(8,128)(2,1)S(1)} %get-tuple-element.60), channel_id=1, source_target_pairs={{0,4},{1,5},{2,6},{3,7},{4,0},{5,1},{6,2},{7,3},{8,12},{9,13},{10,... | collective-permute-start | bytes 393224 | tf_op jit(solution)/shard_map/ppermute | solution.py:162
  80.5 12.9 %copy-start.1 = (f32[256,256]{1,0:T(8,128)S(1)}, f32[256,256]{1,0:T(8,128)}, u32[]{:S(2)}) copy-start(f32[256,256]{1,0:T(8,128)} %param.7) | copy-start | bytes 786436
  80.5 12.9 %copy-start.2 = (f32[256,256]{1,0:T(8,128)S(1)}, f32[256,256]{1,0:T(8,128)}, u32[]{:S(2)}) copy-start(f32[256,256]{1,0:T(8,128)} %param.8) | copy-start | bytes 786436
  80.5 12.9 %copy-start.3 = (f32[256,256]{1,0:T(8,128)S(1)}, f32[256,256]{1,0:T(8,128)}, u32[]{:S(2)}) copy-start(f32[256,256]{1,0:T(8,128)} %param.9) | copy-start | bytes 786436
  80.6 7.1 %collective-permute-start.26 = (bf16[256,256]{1,0:T(8,128)(2,1)S(1)}, bf16[256,256]{1,0:T(8,128)(2,1)S(1)}, u32[]{:S(2)}, u32[]{:S(2)}) collective-permute-start(bf16[256,256]{1,0:T(8,128)(2,1)S(1)} %get-tuple-element.56), channel_id=1, source_target_pairs={{0,2},{1,3},{2,4},{3,5},{4,6},{5,7},{6,0},{7,1},{8,10},{9,11},{10,... | collective-permute-start | bytes 393224 | tf_op jit(solution)/shard_map/ppermute | solution.py:162
  83.3 8.7 %collective-permute-start.28 = (bf16[256,256]{1,0:T(8,128)(2,1)S(1)}, bf16[256,256]{1,0:T(8,128)(2,1)S(1)}, u32[]{:S(2)}, u32[]{:S(2)}) collective-permute-start(bf16[256,256]{1,0:T(8,128)(2,1)S(1)} %get-tuple-element.57), channel_id=1, source_target_pairs={{0,6},{1,7},{2,0},{3,1},{4,2},{5,3},{6,4},{7,5},{8,14},{9,15},{10,... | collective-permute-start | bytes 393224 | tf_op jit(solution)/shard_map/ppermute | solution.py:162
  84.9 8.5 %collective-permute-start.24 = (bf16[256,256]{1,0:T(8,128)(2,1)S(1)}, bf16[256,256]{1,0:T(8,128)(2,1)S(1)}, u32[]{:S(2)}, u32[]{:S(2)}) collective-permute-start(bf16[256,256]{1,0:T(8,128)(2,1)S(1)} %get-tuple-element.58), channel_id=1, source_target_pairs={{0,1},{1,2},{2,3},{3,4},{4,5},{5,6},{6,7},{7,0},{8,9},{9,10},{10,1... | collective-permute-start | bytes 393224 | tf_op jit(solution)/shard_map/ppermute | solution.py:162
  86.1 7.3 %collective-permute-start.29 = (bf16[256,256]{1,0:T(8,128)(2,1)S(1)}, bf16[256,256]{1,0:T(8,128)(2,1)S(1)}, u32[]{:S(2)}, u32[]{:S(2)}) collective-permute-start(bf16[256,256]{1,0:T(8,128)(2,1)S(1)} %get-tuple-element.59), channel_id=1, source_target_pairs={{0,7},{1,0},{2,1},{3,2},{4,3},{5,4},{6,5},{7,6},{8,15},{9,8},{10,9... | collective-permute-start | bytes 393224 | tf_op jit(solution)/shard_map/ppermute | solution.py:162
  94.5 6.1 %collective-permute-start.30 = (bf16[256,256]{1,0:T(8,128)(2,1)S(1)}, bf16[256,256]{1,0:T(8,128)(2,1)S(1)}, u32[]{:S(2)}, u32[]{:S(2)}) collective-permute-start(bf16[256,256]{1,0:T(8,128)(2,1)S(1)} %get-tuple-element.50), channel_id=1, source_target_pairs={{0,64},{8,24},{16,80},{24,40},{32,96},{40,56},{48,112},{56,8},{64,... | collective-permute-start | bytes 393224 | tf_op jit(solution)/shard_map/ppermute | solution.py:181
  94.5 9.0 %collective-permute-start.31 = (bf16[256,256]{1,0:T(8,128)(2,1)S(1)}, bf16[256,256]{1,0:T(8,128)(2,1)S(1)}, u32[]{:S(2)}, u32[]{:S(2)}) collective-permute-start(bf16[256,256]{1,0:T(8,128)(2,1)S(1)} %get-tuple-element.50), channel_id=1, source_target_pairs={{0,128},{8,40},{16,144},{24,56},{32,160},{40,8},{48,176},{56,24},{... | collective-permute-start | bytes 393224 | tf_op jit(solution)/shard_map/ppermute | solution.py:181
  99.4 4.1 %collective-permute-start.32 = (bf16[256,256]{1,0:T(8,128)(2,1)S(1)}, bf16[256,256]{1,0:T(8,128)(2,1)S(1)}, u32[]{:S(2)}, u32[]{:S(2)}) collective-permute-start(bf16[256,256]{1,0:T(8,128)(2,1)S(1)} %get-tuple-element.50), channel_id=1, source_target_pairs={{0,192},{8,56},{16,208},{24,8},{32,224},{40,24},{48,240},{56,40},{... | collective-permute-start | bytes 393224 | tf_op jit(solution)/shard_map/ppermute | solution.py:181
  103.6 15.2 %collective-permute-start.33 = (bf16[4,256,256]{2,1,0:T(8,128)(2,1)S(1)}, bf16[4,256,256]{2,1,0:T(8,128)(2,1)S(1)}, u32[]{:S(2)}, u32[]{:S(2)}) collective-permute-start(bf16[4,256,256]{2,1,0:T(8,128)(2,1)S(1)} %pad_maximum_fusion.refs_0_), channel_id=1, source_target_pairs={{0,16},{8,72},{16,32},{24,88},{32,48},{40,104},{48,0},{56,120},{64... | collective-permute-start | bytes 1572872 | tf_op jit(solution)/shard_map/ppermute | solution.py:183
  104.9 14.0 %collective-permute-start.34 = (bf16[4,256,256]{2,1,0:T(8,128)(2,1)S(1)}, bf16[4,256,256]{2,1,0:T(8,128)(2,1)S(1)}, u32[]{:S(2)}, u32[]{:S(2)}) collective-permute-start(bf16[4,256,256]{2,1,0:T(8,128)(2,1)S(1)} %pad_maximum_fusion.refs_0_), channel_id=1, source_target_pairs={{0,32},{8,136},{16,48},{24,152},{32,0},{40,168},{48,16},{56,184},{... | collective-permute-start | bytes 1572872 | tf_op jit(solution)/shard_map/ppermute | solution.py:183
  105.8 17.9 %collective-permute-start.35 = (bf16[4,256,256]{2,1,0:T(8,128)(2,1)S(1)}, bf16[4,256,256]{2,1,0:T(8,128)(2,1)S(1)}, u32[]{:S(2)}, u32[]{:S(2)}) collective-permute-start(bf16[4,256,256]{2,1,0:T(8,128)(2,1)S(1)} %pad_maximum_fusion.refs_0_), channel_id=1, source_target_pairs={{0,48},{8,200},{16,0},{24,216},{32,16},{40,232},{48,32},{56,248},{... | collective-permute-start | bytes 1572872 | tf_op jit(solution)/shard_map/ppermute | solution.py:183
  107.7 16.1 %collective-permute-start.36 = (bf16[4,256,256]{2,1,0:T(8,128)(2,1)S(1)}, bf16[4,256,256]{2,1,0:T(8,128)(2,1)S(1)}, u32[]{:S(2)}, u32[]{:S(2)}) collective-permute-start(bf16[4,256,256]{2,1,0:T(8,128)(2,1)S(1)} %pad_maximum_fusion.refs_0_), channel_id=1, source_target_pairs={{0,8},{8,0},{16,24},{24,16},{32,40},{40,32},{48,56},{56,48},{64,72... | collective-permute-start | bytes 1572872 | tf_op jit(solution)/shard_map/ppermute | solution.py:185
  118.8 4.9 %collective-permute-start.37 = (bf16[4,256,256]{2,1,0:T(8,128)(2,1)S(1)}, bf16[4,256,256]{2,1,0:T(8,128)(2,1)S(1)}, u32[]{:S(2)}, u32[]{:S(2)}) collective-permute-start(bf16[4,256,256]{2,1,0:T(8,128)(2,1)S(1)} %collective-permute-done.33.refs_1_), channel_id=1, source_target_pairs={{0,8},{8,0},{16,24},{24,16},{32,40},{40,32},{48,56},{56,48},{64,72... | collective-permute-start | bytes 1572872 | tf_op jit(solution)/shard_map/ppermute | solution.py:185
  118.8 6.4 %collective-permute-start.38 = (bf16[4,256,256]{2,1,0:T(8,128)(2,1)S(1)}, bf16[4,256,256]{2,1,0:T(8,128)(2,1)S(1)}, u32[]{:S(2)}, u32[]{:S(2)}) collective-permute-start(bf16[4,256,256]{2,1,0:T(8,128)(2,1)S(1)} %collective-permute-done.34.refs_2_), channel_id=1, source_target_pairs={{0,8},{8,0},{16,24},{24,16},{32,40},{40,32},{48,56},{56,48},{64,72... | collective-permute-start | bytes 1572872 | tf_op jit(solution)/shard_map/ppermute | solution.py:185
  123.7 2.3 %collective-permute-start.39 = (bf16[4,256,256]{2,1,0:T(8,128)(2,1)S(1)}, bf16[4,256,256]{2,1,0:T(8,128)(2,1)S(1)}, u32[]{:S(2)}, u32[]{:S(2)}) collective-permute-start(bf16[4,256,256]{2,1,0:T(8,128)(2,1)S(1)} %collective-permute-done.35.refs_3_), channel_id=1, source_target_pairs={{0,8},{8,0},{16,24},{24,16},{32,40},{40,32},{48,56},{56,48},{64,72... | collective-permute-start | bytes 1572872 | tf_op jit(solution)/shard_map/ppermute | solution.py:185

commit v6 on v5

--- a/solution.py
+++ b/solution.py
@@ -132,7 +132,10 @@
     ]
 
     mine = lax.all_to_all(out_grads.reshape(panels, tokens, cols), "tensor", 0, 0)
-    mine, acts = lax.optimization_barrier((mine, acts))
+    early = (2, 6, 1, 3)
+    mine, first = lax.optimization_barrier((mine, [acts[i] for i in early]))
+    for i, part in zip(early, first):
+        acts[i] = part
     peer = lax.ppermute(mine, "dp", CORE_SWAP)
     up, down = lax.ppermute(mine, "dp", ring(1, 0)), lax.ppermute(mine, "dp", ring(3, 0))
     grads = [mine, up, lax.ppermute(up, "dp", ring(1, 0)), down]

time: 129 us -> 128 us (level)
  starting transfers between devices: 72.7 us -> 71.1 us
    ppermute x6, waiting for transfers between devices: 5.51 us -> 17.4 us  [per_device(): lax.ppermute(part[i], 'dp', ring(i, 0))]
    ppermute x1, waiting for transfers between devices: 4.81 us -> 0.01 us  [per_device(): grads = [mine, up, lax.ppermute(up, 'dp', ring(1, 0)), down]]
    ppermute x6, starting transfers between devices: 10.5 us -> 7.16 us  [per_device(): lax.ppermute(part[i], 'dp', ring(i, 0))]
    ppermute x3, waiting for transfers between devices: 7.87 us -> 4.61 us  [per_device(): moved = {i: lax.ppermute(line, 'dp', ring(i, 1)) for i in (2, 1, 3)}]
    ppermute x1, waiting for transfers between devices: 3.86 us -> 0.65 us  [per_device(): lax.ppermute(mine, 'dp', ring(1, 0))]
    all_to_all x1, waiting for transfers between devices: 0.01 us -> 2.37 us  [per_device(): lax.all_to_all(out_grads.reshape(panels, tokens, cols), 'tensor', 0, 0)]
    ppermute x7, starting transfers between devices: 15.8 us -> 13.6 us  [along_tensor(): lax.ppermute(part, 'tensor', [(i, (i + step) % panels) for i in range(pan...]
    ppermute x4, starting transfers between devices: 8.18 us -> 10.4 us  [per_device(): peer = [lax.ppermute(part, 'dp', CORE_SWAP) for part in own]]
  transfers between devices with their start and end apart: 41 -> 41, of which waited for: 21 -> 23; matrix products, arithmetic and copies ran while one was open for 1% -> 1% of each run, Pallas kernels for 4% -> 4%
where the time goes in v6:
time: 128 us
  starting transfers between devices  71.1 us (56%)
  waiting for transfers between devices  44.1 us (34%)
  Pallas kernels  8.2 us (6%)
  other arithmetic  1.78 us (1%)
  local copies, waits for them, and re-layouts  1.65 us (1%)
    ppermute x6, waiting for transfers between devices, per_device(): lax.ppermute(part[i], 'dp', ring(i, 0))  17.4 us
    ppermute x7, starting transfers between devices, along_tensor(): lax.ppermute(part, 'tensor', [(i, (i + step) % panels) for i in range(pan...  13.6 us
    ppermute x4, starting transfers between devices, per_device(): peer = [lax.ppermute(part, 'dp', CORE_SWAP) for part in own]  10.4 us
    all_to_all x1, starting transfers between devices, per_device(): lax.all_to_all(out_grads.reshape(panels, tokens, cols), 'tensor', 0, 0)  9.03 us
    ppermute x6, starting transfers between devices, per_device(): lax.ppermute(part, 'dp', ring(i, 1))  8.43 us
    ppermute x6, starting transfers between devices, per_device(): lax.ppermute(part[i], 'dp', ring(i, 0))  7.16 us
    ppermute x6, waiting for transfers between devices, per_device(): lax.ppermute(part, 'dp', ring(i, 1))  6.25 us
    pallas_call x5, Pallas kernels, product(): mover(functools.partial(product_kernel, which, rows), [kept((len(away), r...  5.41 us
  transfers between devices with their start and end apart: 41, of which 23 were waited for; matrix products, arithmetic and copies ran while one was open for 1% of the time, Pallas kernels for 4%

profile of v6, /device:TPU:1, one launch (start us, length us, event | category | flops | bytes accessed | tf_op | source)
XLA Modules:
  0.0 127.7 jit_solution(1672629259523708842)
XLA Ops:
  0.6 9.0 %all-to-all-start = ((bf16[8,128,256]{2,1,0:T(8,128)(2,1)}), bf16[8,128,256]{2,1,0:T(8,128)(2,1)S(1)}, u32[]{:S(2)}, u32[]{:S(2)}) async-start(bf16[8,128,256]{2,1,0:T(8,128)(2,1)} %bitcast.41), calls=%async_computation | async-start | bytes 1048576 | tf_op jit(solution)/shard_map/all_to_all | solution.py:134
  9.7 1.6 %copy-done = bf16[128,8192]{1,0:T(8,128)(2,1)S(1)} copy-done((bf16[128,8192]{1,0:T(8,128)(2,1)S(1)}, bf16[128,8192]{1,0:T(8,128)(2,1)}, u32[]{:S(2)}) %copy-start) | copy-done | bytes 2097176
  11.2 0.3 shard_map.84
  11.6 1.0 collective-permute-start.1
  12.6 2.9 %collective-permute-start = (bf16[128,1024]{1,0:T(8,128)(2,1)S(1)}, bf16[128,1024]{1,0:T(8,128)(2,1)S(1)}, u32[]{:S(2)}, u32[]{:S(2)}) collective-permute-start(bf16[128,1024]{1,0:T(8,128)(2,1)S(1)} %get-tuple-element.24), channel_id=1, source_target_pairs={{0,128},{8,40},{16,144},{24,56},{32,160},{40,8},{48,176},{56,24},{... | collective-permute-start | bytes 786440 | tf_op jit(solution)/shard_map/ppermute | solution.py:129
  15.5 0.4 collective-permute-start.3
  15.9 2.3 %collective-permute-start.4 = (bf16[128,1024]{1,0:T(8,128)(2,1)S(1)}, bf16[128,1024]{1,0:T(8,128)(2,1)S(1)}, u32[]{:S(2)}, u32[]{:S(2)}) collective-permute-start(bf16[128,1024]{1,0:T(8,128)(2,1)S(1)} %get-tuple-element.27), channel_id=1, source_target_pairs={{0,192},{8,56},{16,208},{24,8},{32,224},{40,24},{48,240},{56,40},{... | collective-permute-start | bytes 786440 | tf_op jit(solution)/shard_map/ppermute | solution.py:129
  18.2 1.4 %collective-permute-done.refs_2_ = bf16[128,1024]{1,0:T(8,128)(2,1)S(1)} collective-permute-done((bf16[128,1024]{1,0:T(8,128)(2,1)S(1)}, bf16[128,1024]{1,0:T(8,128)(2,1)S(1)}, u32[]{:S(2)}, u32[]{:S(2)}) %collective-permute-start) | collective-permute-done | bytes 262176 | tf_op jit(solution)/shard_map/ppermute | solution.py:129
  19.6 2.8 %collective-permute-done.3.refs_1_ = bf16[128,1024]{1,0:T(8,128)(2,1)S(1)} collective-permute-done((bf16[128,1024]{1,0:T(8,128)(2,1)S(1)}, bf16[128,1024]{1,0:T(8,128)(2,1)S(1)}, u32[]{:S(2)}, u32[]{:S(2)}) %collective-permute-start.3) | collective-permute-done | bytes 262176 | tf_op jit(solution)/shard_map/ppermute | solution.py:129
  22.4 0.3 collective-permute-done.4.refs_3_
  22.8 2.5 %collective-permute-done.2.refs_6_ = bf16[128,1024]{1,0:T(8,128)(2,1)S(1)} collective-permute-done((bf16[128,1024]{1,0:T(8,128)(2,1)S(1)}, bf16[128,1024]{1,0:T(8,128)(2,1)S(1)}, u32[]{:S(2)}, u32[]{:S(2)}) %collective-permute-start.2) | collective-permute-done | bytes 262176 | tf_op jit(solution)/shard_map/ppermute | solution.py:129
  25.2 2.4 %all-to-all-done.refs_8_ = bf16[8,128,256]{2,1,0:T(8,128)(2,1)S(1)} async-done(((bf16[8,128,256]{2,1,0:T(8,128)(2,1)}), bf16[8,128,256]{2,1,0:T(8,128)(2,1)S(1)}, u32[]{:S(2)}, u32[]{:S(2)}) %all-to-all-start) | async-done | bytes 524320 | tf_op jit(solution)/shard_map/all_to_all | solution.py:134
  27.6 0.5 collective-permute-start.13
  28.1 1.3 %collective-permute-start.10 = (bf16[8,128,256]{2,1,0:T(8,128)(2,1)S(1)}, bf16[8,128,256]{2,1,0:T(8,128)(2,1)S(1)}, u32[]{:S(2)}, u32[]{:S(2)}) collective-permute-start(bf16[8,128,256]{2,1,0:T(8,128)(2,1)S(1)} %all-to-all-done.refs_8_), channel_id=1, source_target_pairs={{0,64},{8,24},{16,80},{24,40},{32,96},{40,56},{48,112},{56,8},{64,... | collective-permute-start | bytes 1572872 | tf_op jit(solution)/shard_map/ppermute | solution.py:140
  29.4 0.2 collective-permute-done.13.refs_12_
  29.6 2.7 %collective-permute-start.15 = (bf16[8,128,256]{2,1,0:T(8,128)(2,1)S(1)}, bf16[8,128,256]{2,1,0:T(8,128)(2,1)S(1)}, u32[]{:S(2)}, u32[]{:S(2)}) collective-permute-start(bf16[8,128,256]{2,1,0:T(8,128)(2,1)S(1)} %collective-permute-done.13.refs_12_), channel_id=1, source_target_pairs={{0,192},{8,56},{16,208},{24,8},{32,224},{40,24},{48,240},{56,40},{... | collective-permute-start | bytes 1572872 | tf_op jit(solution)/shard_map/ppermute | solution.py:142
  32.4 0.4 collective-permute-start.6
  32.9 0.4 collective-permute-start.5
  33.3 0.7 collective-permute-done.6
  33.9 1.3 %collective-permute-start.7 = (bf16[128,1024]{1,0:T(8,128)(2,1)S(1)}, bf16[128,1024]{1,0:T(8,128)(2,1)S(1)}, u32[]{:S(2)}, u32[]{:S(2)}) collective-permute-start(bf16[128,1024]{1,0:T(8,128)(2,1)S(1)} %collective-permute-done.6), channel_id=1, source_target_pairs={{0,64},{8,24},{16,80},{24,40},{32,96},{40,56},{48,112},{56,8},{64,... | collective-permute-start | bytes 786440 | tf_op jit(solution)/shard_map/ppermute | solution.py:129
  35.2 1.8 %collective-permute-start.12 = (bf16[8,128,256]{2,1,0:T(8,128)(2,1)S(1)}, bf16[8,128,256]{2,1,0:T(8,128)(2,1)S(1)}, u32[]{:S(2)}, u32[]{:S(2)}) collective-permute-start(bf16[8,128,256]{2,1,0:T(8,128)(2,1)S(1)} %all-to-all-done.refs_8_), channel_id=1, source_target_pairs={{0,192},{8,56},{16,208},{24,8},{32,224},{40,24},{48,240},{56,40},{... | collective-permute-start | bytes 1572872 | tf_op jit(solution)/shard_map/ppermute | solution.py:140
  37.1 0.6 collective-permute-done.10.refs_9_
  37.7 0.3 collective-permute-start.11
  38.0 0.5 collective-permute-done.15.refs_15_
  38.5 3.4 %collective-permute-start.16 = (bf16[8,128,256]{2,1,0:T(8,128)(2,1)S(1)}, bf16[8,128,256]{2,1,0:T(8,128)(2,1)S(1)}, u32[]{:S(2)}, u32[]{:S(2)}) collective-permute-start(bf16[8,128,256]{2,1,0:T(8,128)(2,1)S(1)} %collective-permute-done.15.refs_15_), channel_id=1, source_target_pairs={{0,192},{8,56},{16,208},{24,8},{32,224},{40,24},{48,240},{56,40},{... | collective-permute-start | bytes 1572872 | tf_op jit(solution)/shard_map/ppermute | solution.py:143
  41.9 0.3 collective-permute-start.9
  42.2 10.4 %collective-permute-done.9.refs_7_ = bf16[128,1024]{1,0:T(8,128)(2,1)S(1)} collective-permute-done((bf16[128,1024]{1,0:T(8,128)(2,1)S(1)}, bf16[128,1024]{1,0:T(8,128)(2,1)S(1)}, u32[]{:S(2)}, u32[]{:S(2)}) %collective-permute-start.9) | collective-permute-done | bytes 262176 | tf_op jit(solution)/shard_map/ppermute | solution.py:129
  52.6 0.6 shard_map.88
  53.2 2.8 %collective-permute-start.20 = (bf16[3,256,256]{2,1,0:T(8,128)(2,1)S(1)}, bf16[3,256,256]{2,1,0:T(8,128)(2,1)S(1)}, u32[]{:S(2)}, u32[]{:S(2)}) collective-permute-start(bf16[3,256,256]{2,1,0:T(8,128)(2,1)S(1)} %shard_map.88), channel_id=1, source_target_pairs={{0,32},{8,136},{16,48},{24,152},{32,0},{40,168},{48,16},{56,184},{... | collective-permute-start | bytes 1179656 | tf_op jit(solution)/shard_map/ppermute | solution.py:156
  56.1 1.0 shard_map.89
  57.1 0.4 collective-permute-start.21
  57.5 2.4 %collective-permute-start.22 = (bf16[3,256,256]{2,1,0:T(8,128)(2,1)S(1)}, bf16[3,256,256]{2,1,0:T(8,128)(2,1)S(1)}, u32[]{:S(2)}, u32[]{:S(2)}) collective-permute-start(bf16[3,256,256]{2,1,0:T(8,128)(2,1)S(1)} %get-tuple-element.41), channel_id=1, source_target_pairs={{0,48},{8,200},{16,0},{24,216},{32,16},{40,232},{48,32},{56,248},{... | collective-permute-start | bytes 1179656 | tf_op jit(solution)/shard_map/ppermute | solution.py:156
  59.8 0.9 shard_map.86
  60.8 1.6 %shard_map.87 = (bf16[5,256,256]{2,1,0:T(8,128)(2,1)S(1)}, bf16[5,256,256]{2,1,0:T(8,128)(2,1)S(1)}) custom-call(bf16[128,1024]{1,0:T(8,128)(2,1)S(1)} %get-tuple-element.23.refs_0_, bf16[128,1024]{1,0:T(8,128)(2,1)S(1)} %collective-permute-done.3.refs_1_, bf16[128,1024]{1,0:T(8,128)(2,1)S(1)} %collective-permute-done.refs_2_, ...), custom_call_target="tpu_custom_call" | custom-call | tf_op jit(solution)/shard_map/pallas_call | solution.py:146
  62.4 0.6 collective-permute-start.18
  63.1 2.1 %collective-permute-start.19 = (bf16[5,256,256]{2,1,0:T(8,128)(2,1)S(1)}, bf16[5,256,256]{2,1,0:T(8,128)(2,1)S(1)}, u32[]{:S(2)}, u32[]{:S(2)}) collective-permute-start(bf16[5,256,256]{2,1,0:T(8,128)(2,1)S(1)} %get-tuple-element.38), channel_id=1, source_target_pairs={{0,48},{8,200},{16,0},{24,216},{32,16},{40,232},{48,32},{56,248},{... | collective-permute-start | bytes 1966088 | tf_op jit(solution)/shard_map/ppermute | solution.py:156
  65.2 1.3 %shard_map.85 = (bf16[3,256,256]{2,1,0:T(8,128)(2,1)S(1)}, bf16[5,256,256]{2,1,0:T(8,128)(2,1)S(1)}) custom-call(bf16[128,1024]{1,0:T(8,128)(2,1)S(1)} %get-tuple-element.23.refs_0_, bf16[128,1024]{1,0:T(8,128)(2,1)S(1)} %collective-permute-done.3.refs_1_, bf16[128,1024]{1,0:T(8,128)(2,1)S(1)} %collective-permute-done.refs_2_, ...), custom_call_target="tpu_custom_call" | custom-call | tf_op jit(solution)/shard_map/pallas_call | solution.py:146
  66.7 0.4 collective-permute-start.25
  67.1 2.4 %collective-permute-start.27 = (bf16[256,256]{1,0:T(8,128)(2,1)S(1)}, bf16[256,256]{1,0:T(8,128)(2,1)S(1)}, u32[]{:S(2)}, u32[]{:S(2)}) collective-permute-start(bf16[256,256]{1,0:T(8,128)(2,1)S(1)} %get-tuple-element.53), channel_id=1, source_target_pairs={{0,7},{1,0},{2,1},{3,2},{4,3},{5,4},{6,5},{7,6},{8,15},{9,8},{10,9... | collective-permute-start | bytes 393224 | tf_op jit(solution)/shard_map/ppermute | solution.py:165
  69.5 3.5 %collective-permute-done.17 = bf16[5,256,256]{2,1,0:T(8,128)(2,1)S(1)} collective-permute-done((bf16[5,256,256]{2,1,0:T(8,128)(2,1)S(1)}, bf16[5,256,256]{2,1,0:T(8,128)(2,1)S(1)}, u32[]{:S(2)}, u32[]{:S(2)}) %collective-permute-start.17) | collective-permute-done | bytes 655392 | tf_op jit(solution)/shard_map/ppermute | solution.py:156
  73.0 4.4 %collective-permute-start.23 = (bf16[256,256]{1,0:T(8,128)(2,1)S(1)}, bf16[256,256]{1,0:T(8,128)(2,1)S(1)}, u32[]{:S(2)}, u32[]{:S(2)}) collective-permute-start(bf16[256,256]{1,0:T(8,128)(2,1)S(1)} %get-tuple-element.52), channel_id=1, source_target_pairs={{0,4},{1,5},{2,6},{3,7},{4,0},{5,1},{6,2},{7,3},{8,12},{9,13},{10,... | collective-permute-start | bytes 393224 | tf_op jit(solution)/shard_map/ppermute | solution.py:165
  77.4 2.6 %collective-permute-done.18 = bf16[5,256,256]{2,1,0:T(8,128)(2,1)S(1)} collective-permute-done((bf16[5,256,256]{2,1,0:T(8,128)(2,1)S(1)}, bf16[5,256,256]{2,1,0:T(8,128)(2,1)S(1)}, u32[]{:S(2)}, u32[]{:S(2)}) %collective-permute-start.18) | collective-permute-done | bytes 655392 | tf_op jit(solution)/shard_map/ppermute | solution.py:156
  80.1 0.4 fusion.12
  80.6 1.3 %collective-permute-start.26 = (bf16[256,256]{1,0:T(8,128)(2,1)S(1)}, bf16[256,256]{1,0:T(8,128)(2,1)S(1)}, u32[]{:S(2)}, u32[]{:S(2)}) collective-permute-start(bf16[256,256]{1,0:T(8,128)(2,1)S(1)} %get-tuple-element.48), channel_id=1, source_target_pairs={{0,2},{1,3},{2,4},{3,5},{4,6},{5,7},{6,0},{7,1},{8,10},{9,11},{10,... | collective-permute-start | bytes 393224 | tf_op jit(solution)/shard_map/ppermute | solution.py:165
  82.0 2.3 %collective-permute-start.28 = (bf16[256,256]{1,0:T(8,128)(2,1)S(1)}, bf16[256,256]{1,0:T(8,128)(2,1)S(1)}, u32[]{:S(2)}, u32[]{:S(2)}) collective-permute-start(bf16[256,256]{1,0:T(8,128)(2,1)S(1)} %get-tuple-element.49), channel_id=1, source_target_pairs={{0,6},{1,7},{2,0},{3,1},{4,2},{5,3},{6,4},{7,5},{8,14},{9,15},{10,... | collective-permute-start | bytes 393224 | tf_op jit(solution)/shard_map/ppermute | solution.py:165
  84.3 0.4 collective-permute-start.24
  84.7 2.3 %collective-permute-start.29 = (bf16[256,256]{1,0:T(8,128)(2,1)S(1)}, bf16[256,256]{1,0:T(8,128)(2,1)S(1)}, u32[]{:S(2)}, u32[]{:S(2)}) collective-permute-start(bf16[256,256]{1,0:T(8,128)(2,1)S(1)} %get-tuple-element.51), channel_id=1, source_target_pairs={{0,7},{1,0},{2,1},{3,2},{4,3},{5,4},{6,5},{7,6},{8,15},{9,8},{10,9... | collective-permute-start | bytes 393224 | tf_op jit(solution)/shard_map/ppermute | solution.py:165
  87.2 3.8 %collective-permute-done.28 = bf16[256,256]{1,0:T(8,128)(2,1)S(1)} collective-permute-done((bf16[256,256]{1,0:T(8,128)(2,1)S(1)}, bf16[256,256]{1,0:T(8,128)(2,1)S(1)}, u32[]{:S(2)}, u32[]{:S(2)}) %collective-permute-start.28) | collective-permute-done | bytes 131104 | tf_op jit(solution)/shard_map/ppermute | solution.py:165
  90.9 1.2 collective-permute-done.24
  92.2 1.1 fusion.10
  93.3 5.2 %collective-permute-start.31 = (bf16[256,256]{1,0:T(8,128)(2,1)S(1)}, bf16[256,256]{1,0:T(8,128)(2,1)S(1)}, u32[]{:S(2)}, u32[]{:S(2)}) collective-permute-start(bf16[256,256]{1,0:T(8,128)(2,1)S(1)} %get-tuple-element.42), channel_id=1, source_target_pairs={{0,128},{8,40},{16,144},{24,56},{32,160},{40,8},{48,176},{56,24},{... | collective-permute-start | bytes 393224 | tf_op jit(solution)/shard_map/ppermute | solution.py:184
  98.5 1.2 collective-permute-done.30
  99.6 2.9 %collective-permute-done.31 = bf16[256,256]{1,0:T(8,128)(2,1)S(1)} collective-permute-done((bf16[256,256]{1,0:T(8,128)(2,1)S(1)}, bf16[256,256]{1,0:T(8,128)(2,1)S(1)}, u32[]{:S(2)}, u32[]{:S(2)}) %collective-permute-start.31) | collective-permute-done | bytes 131104 | tf_op jit(solution)/shard_map/ppermute | solution.py:184
  102.7 1.6 %collective-permute-start.33 = (bf16[4,256,256]{2,1,0:T(8,128)(2,1)S(1)}, bf16[4,256,256]{2,1,0:T(8,128)(2,1)S(1)}, u32[]{:S(2)}, u32[]{:S(2)}) collective-permute-start(bf16[4,256,256]{2,1,0:T(8,128)(2,1)S(1)} %pad_maximum_fusion.refs_0_), channel_id=1, source_target_pairs={{0,16},{8,72},{16,32},{24,88},{32,48},{40,104},{48,0},{56,120},{64... | collective-permute-start | bytes 1572872 | tf_op jit(solution)/shard_map/ppermute | solution.py:186
  104.3 1.7 %collective-permute-start.34 = (bf16[4,256,256]{2,1,0:T(8,128)(2,1)S(1)}, bf16[4,256,256]{2,1,0:T(8,128)(2,1)S(1)}, u32[]{:S(2)}, u32[]{:S(2)}) collective-permute-start(bf16[4,256,256]{2,1,0:T(8,128)(2,1)S(1)} %pad_maximum_fusion.refs_0_), channel_id=1, source_target_pairs={{0,32},{8,136},{16,48},{24,152},{32,0},{40,168},{48,16},{56,184},{... | collective-permute-start | bytes 1572872 | tf_op jit(solution)/shard_map/ppermute | solution.py:186
  106.0 2.0 %collective-permute-start.35 = (bf16[4,256,256]{2,1,0:T(8,128)(2,1)S(1)}, bf16[4,256,256]{2,1,0:T(8,128)(2,1)S(1)}, u32[]{:S(2)}, u32[]{:S(2)}) collective-permute-start(bf16[4,256,256]{2,1,0:T(8,128)(2,1)S(1)} %pad_maximum_fusion.refs_0_), channel_id=1, source_target_pairs={{0,48},{8,200},{16,0},{24,216},{32,16},{40,232},{48,32},{56,248},{... | collective-permute-start | bytes 1572872 | tf_op jit(solution)/shard_map/ppermute | solution.py:186
  107.9 2.2 %collective-permute-start.36 = (bf16[4,256,256]{2,1,0:T(8,128)(2,1)S(1)}, bf16[4,256,256]{2,1,0:T(8,128)(2,1)S(1)}, u32[]{:S(2)}, u32[]{:S(2)}) collective-permute-start(bf16[4,256,256]{2,1,0:T(8,128)(2,1)S(1)} %pad_maximum_fusion.refs_0_), channel_id=1, source_target_pairs={{0,8},{8,0},{16,24},{24,16},{32,40},{40,32},{48,56},{56,48},{64,72... | collective-permute-start | bytes 1572872 | tf_op jit(solution)/shard_map/ppermute | solution.py:188
  110.1 2.1 %collective-permute-done.33.refs_1_ = bf16[4,256,256]{2,1,0:T(8,128)(2,1)S(1)} collective-permute-done((bf16[4,256,256]{2,1,0:T(8,128)(2,1)S(1)}, bf16[4,256,256]{2,1,0:T(8,128)(2,1)S(1)}, u32[]{:S(2)}, u32[]{:S(2)}) %collective-permute-start.33) | collective-permute-done | bytes 524320 | tf_op jit(solution)/shard_map/ppermute | solution.py:186
  112.3 3.6 %collective-permute-start.37 = (bf16[4,256,256]{2,1,0:T(8,128)(2,1)S(1)}, bf16[4,256,256]{2,1,0:T(8,128)(2,1)S(1)}, u32[]{:S(2)}, u32[]{:S(2)}) collective-permute-start(bf16[4,256,256]{2,1,0:T(8,128)(2,1)S(1)} %collective-permute-done.33.refs_1_), channel_id=1, source_target_pairs={{0,8},{8,0},{16,24},{24,16},{32,40},{40,32},{48,56},{56,48},{64,72... | collective-permute-start | bytes 1572872 | tf_op jit(solution)/shard_map/ppermute | solution.py:188
  115.8 2.5 %collective-permute-done.34.refs_2_ = bf16[4,256,256]{2,1,0:T(8,128)(2,1)S(1)} collective-permute-done((bf16[4,256,256]{2,1,0:T(8,128)(2,1)S(1)}, bf16[4,256,256]{2,1,0:T(8,128)(2,1)S(1)}, u32[]{:S(2)}, u32[]{:S(2)}) %collective-permute-start.34) | collective-permute-done | bytes 524320 | tf_op jit(solution)/shard_map/ppermute | solution.py:186
  118.3 4.6 %collective-permute-start.38 = (bf16[4,256,256]{2,1,0:T(8,128)(2,1)S(1)}, bf16[4,256,256]{2,1,0:T(8,128)(2,1)S(1)}, u32[]{:S(2)}, u32[]{:S(2)}) collective-permute-start(bf16[4,256,256]{2,1,0:T(8,128)(2,1)S(1)} %collective-permute-done.34.refs_2_), channel_id=1, source_target_pairs={{0,8},{8,0},{16,24},{24,16},{32,40},{40,32},{48,56},{56,48},{64,72... | collective-permute-start | bytes 1572872 | tf_op jit(solution)/shard_map/ppermute | solution.py:188
  122.9 1.5 %collective-permute-done.38.refs_6_ = bf16[4,256,256]{2,1,0:T(8,128)(2,1)S(1)} collective-permute-done((bf16[4,256,256]{2,1,0:T(8,128)(2,1)S(1)}, bf16[4,256,256]{2,1,0:T(8,128)(2,1)S(1)}, u32[]{:S(2)}, u32[]{:S(2)}) %collective-permute-start.38) | collective-permute-done | bytes 524320 | tf_op jit(solution)/shard_map/ppermute | solution.py:188
  124.5 0.7 collective-permute-done.39.refs_7_
  125.2 2.5 %shard_map.90 = bf16[4,4,2,256,256]{4,3,2,1,0:T(8,128)(2,1)} custom-call(bf16[4,256,256]{2,1,0:T(8,128)(2,1)S(1)} %pad_maximum_fusion.refs_0_, bf16[4,256,256]{2,1,0:T(8,128)(2,1)S(1)} %collective-permute-done.33.refs_1_, bf16[4,256,256]{2,1,0:T(8,128)(2,1)S(1)} %collective-permute-done.34.refs_2_, bf16[4,256,256]{2,1,0:T(8,128)(2,1)S(1)} %collective-permute-done.35.refs_3_, ...), custom_call_target="tpu_custom_call" | custom-call | tf_op jit(solution)/shard_map/pallas_call | solution.py:189
  (40 shorter events, 1.0 us)
Async XLA Ops:
  0.6 27.0 %all-to-all-start = ((bf16[8,128,256]{2,1,0:T(8,128)(2,1)}), bf16[8,128,256]{2,1,0:T(8,128)(2,1)S(1)}, u32[]{:S(2)}, u32[]{:S(2)}) async-start(bf16[8,128,256]{2,1,0:T(8,128)(2,1)} %bitcast.41), calls=%async_computation | async-start | bytes 1048576 | tf_op jit(solution)/shard_map/all_to_all | solution.py:134
  9.7 1.6 %copy-start = (bf16[128,8192]{1,0:T(8,128)(2,1)S(1)}, bf16[128,8192]{1,0:T(8,128)(2,1)}, u32[]{:S(2)}) copy-start(bf16[128,8192]{1,0:T(8,128)(2,1)} %acts.1) | copy-start | bytes 6291460
  11.6 6.6 %collective-permute-start.1 = (bf16[128,1024]{1,0:T(8,128)(2,1)S(1)}, bf16[128,1024]{1,0:T(8,128)(2,1)S(1)}, u32[]{:S(2)}, u32[]{:S(2)}) collective-permute-start(bf16[128,1024]{1,0:T(8,128)(2,1)S(1)} %get-tuple-element.25), channel_id=1, source_target_pairs={{0,8},{8,0},{16,24},{24,16},{32,40},{40,32},{48,56},{56,48},{64,72... | collective-permute-start | bytes 786440 | tf_op jit(solution)/shard_map/ppermute | solution.py:127
  12.6 7.0 %collective-permute-start = (bf16[128,1024]{1,0:T(8,128)(2,1)S(1)}, bf16[128,1024]{1,0:T(8,128)(2,1)S(1)}, u32[]{:S(2)}, u32[]{:S(2)}) collective-permute-start(bf16[128,1024]{1,0:T(8,128)(2,1)S(1)} %get-tuple-element.24), channel_id=1, source_target_pairs={{0,128},{8,40},{16,144},{24,56},{32,160},{40,8},{48,176},{56,24},{... | collective-permute-start | bytes 786440 | tf_op jit(solution)/shard_map/ppermute | solution.py:129
  15.5 6.9 %collective-permute-start.3 = (bf16[128,1024]{1,0:T(8,128)(2,1)S(1)}, bf16[128,1024]{1,0:T(8,128)(2,1)S(1)}, u32[]{:S(2)}, u32[]{:S(2)}) collective-permute-start(bf16[128,1024]{1,0:T(8,128)(2,1)S(1)} %get-tuple-element.26), channel_id=1, source_target_pairs={{0,64},{8,24},{16,80},{24,40},{32,96},{40,56},{48,112},{56,8},{64,... | collective-permute-start | bytes 786440 | tf_op jit(solution)/shard_map/ppermute | solution.py:129
  15.9 6.9 %collective-permute-start.4 = (bf16[128,1024]{1,0:T(8,128)(2,1)S(1)}, bf16[128,1024]{1,0:T(8,128)(2,1)S(1)}, u32[]{:S(2)}, u32[]{:S(2)}) collective-permute-start(bf16[128,1024]{1,0:T(8,128)(2,1)S(1)} %get-tuple-element.27), channel_id=1, source_target_pairs={{0,192},{8,56},{16,208},{24,8},{32,224},{40,24},{48,240},{56,40},{... | collective-permute-start | bytes 786440 | tf_op jit(solution)/shard_map/ppermute | solution.py:129
  18.2 7.0 %collective-permute-start.2 = (bf16[128,1024]{1,0:T(8,128)(2,1)S(1)}, bf16[128,1024]{1,0:T(8,128)(2,1)S(1)}, u32[]{:S(2)}, u32[]{:S(2)}) collective-permute-start(bf16[128,1024]{1,0:T(8,128)(2,1)S(1)} %collective-permute-done.1), channel_id=1, source_target_pairs={{0,128},{8,40},{16,144},{24,56},{32,160},{40,8},{48,176},{56,24},{... | collective-permute-start | bytes 786440 | tf_op jit(solution)/shard_map/ppermute | solution.py:129
  27.6 2.0 %collective-permute-start.13 = (bf16[8,128,256]{2,1,0:T(8,128)(2,1)S(1)}, bf16[8,128,256]{2,1,0:T(8,128)(2,1)S(1)}, u32[]{:S(2)}, u32[]{:S(2)}) collective-permute-start(bf16[8,128,256]{2,1,0:T(8,128)(2,1)S(1)} %all-to-all-done.refs_8_), channel_id=1, source_target_pairs={{0,8},{8,0},{16,24},{24,16},{32,40},{40,32},{48,56},{56,48},{64,72... | collective-permute-start | bytes 1572872 | tf_op jit(solution)/shard_map/ppermute | solution.py:139
  28.1 9.6 %collective-permute-start.10 = (bf16[8,128,256]{2,1,0:T(8,128)(2,1)S(1)}, bf16[8,128,256]{2,1,0:T(8,128)(2,1)S(1)}, u32[]{:S(2)}, u32[]{:S(2)}) collective-permute-start(bf16[8,128,256]{2,1,0:T(8,128)(2,1)S(1)} %all-to-all-done.refs_8_), channel_id=1, source_target_pairs={{0,64},{8,24},{16,80},{24,40},{32,96},{40,56},{48,112},{56,8},{64,... | collective-permute-start | bytes 1572872 | tf_op jit(solution)/shard_map/ppermute | solution.py:140
  29.6 8.9 %collective-permute-start.15 = (bf16[8,128,256]{2,1,0:T(8,128)(2,1)S(1)}, bf16[8,128,256]{2,1,0:T(8,128)(2,1)S(1)}, u32[]{:S(2)}, u32[]{:S(2)}) collective-permute-start(bf16[8,128,256]{2,1,0:T(8,128)(2,1)S(1)} %collective-permute-done.13.refs_12_), channel_id=1, source_target_pairs={{0,192},{8,56},{16,208},{24,8},{32,224},{40,24},{48,240},{56,40},{... | collective-permute-start | bytes 1572872 | tf_op jit(solution)/shard_map/ppermute | solution.py:142
  32.4 1.6 %collective-permute-start.6 = (bf16[128,1024]{1,0:T(8,128)(2,1)S(1)}, bf16[128,1024]{1,0:T(8,128)(2,1)S(1)}, u32[]{:S(2)}, u32[]{:S(2)}) collective-permute-start(bf16[128,1024]{1,0:T(8,128)(2,1)S(1)} %get-tuple-element.32), channel_id=1, source_target_pairs={{0,8},{8,0},{16,24},{24,16},{32,40},{40,32},{48,56},{56,48},{64,72... | collective-permute-start | bytes 786440 | tf_op jit(solution)/shard_map/ppermute | solution.py:127
  32.8 2.5 %collective-permute-start.8 = (bf16[128,1024]{1,0:T(8,128)(2,1)S(1)}, bf16[128,1024]{1,0:T(8,128)(2,1)S(1)}, u32[]{:S(2)}, u32[]{:S(2)}) collective-permute-start(bf16[128,1024]{1,0:T(8,128)(2,1)S(1)} %get-tuple-element.34), channel_id=1, source_target_pairs={{0,8},{8,0},{16,24},{24,16},{32,40},{40,32},{48,56},{56,48},{64,72... | collective-permute-start | bytes 786440 | tf_op jit(solution)/shard_map/ppermute | solution.py:127
  32.9 4.2 %collective-permute-start.5 = (bf16[128,1024]{1,0:T(8,128)(2,1)S(1)}, bf16[128,1024]{1,0:T(8,128)(2,1)S(1)}, u32[]{:S(2)}, u32[]{:S(2)}) collective-permute-start(bf16[128,1024]{1,0:T(8,128)(2,1)S(1)} %get-tuple-element.31), channel_id=1, source_target_pairs={{0,8},{8,0},{16,24},{24,16},{32,40},{40,32},{48,56},{56,48},{64,72... | collective-permute-start | bytes 786440 | tf_op jit(solution)/shard_map/ppermute | solution.py:127
  33.9 8.0 %collective-permute-start.7 = (bf16[128,1024]{1,0:T(8,128)(2,1)S(1)}, bf16[128,1024]{1,0:T(8,128)(2,1)S(1)}, u32[]{:S(2)}, u32[]{:S(2)}) collective-permute-start(bf16[128,1024]{1,0:T(8,128)(2,1)S(1)} %collective-permute-done.6), channel_id=1, source_target_pairs={{0,64},{8,24},{16,80},{24,40},{32,96},{40,56},{48,112},{56,8},{64,... | collective-permute-start | bytes 786440 | tf_op jit(solution)/shard_map/ppermute | solution.py:129
  35.2 17.3 %collective-permute-start.12 = (bf16[8,128,256]{2,1,0:T(8,128)(2,1)S(1)}, bf16[8,128,256]{2,1,0:T(8,128)(2,1)S(1)}, u32[]{:S(2)}, u32[]{:S(2)}) collective-permute-start(bf16[8,128,256]{2,1,0:T(8,128)(2,1)S(1)} %all-to-all-done.refs_8_), channel_id=1, source_target_pairs={{0,192},{8,56},{16,208},{24,8},{32,224},{40,24},{48,240},{56,40},{... | collective-permute-start | bytes 1572872 | tf_op jit(solution)/shard_map/ppermute | solution.py:140
  37.1 15.5 %collective-permute-start.14 = (bf16[8,128,256]{2,1,0:T(8,128)(2,1)S(1)}, bf16[8,128,256]{2,1,0:T(8,128)(2,1)S(1)}, u32[]{:S(2)}, u32[]{:S(2)}) collective-permute-start(bf16[8,128,256]{2,1,0:T(8,128)(2,1)S(1)} %collective-permute-done.13.refs_12_), channel_id=1, source_target_pairs={{0,64},{8,24},{16,80},{24,40},{32,96},{40,56},{48,112},{56,8},{64,... | collective-permute-start | bytes 1572872 | tf_op jit(solution)/shard_map/ppermute | solution.py:142
  37.7 14.9 %collective-permute-start.11 = (bf16[8,128,256]{2,1,0:T(8,128)(2,1)S(1)}, bf16[8,128,256]{2,1,0:T(8,128)(2,1)S(1)}, u32[]{:S(2)}, u32[]{:S(2)}) collective-permute-start(bf16[8,128,256]{2,1,0:T(8,128)(2,1)S(1)} %collective-permute-done.10.refs_9_), channel_id=1, source_target_pairs={{0,64},{8,24},{16,80},{24,40},{32,96},{40,56},{48,112},{56,8},{64,... | collective-permute-start | bytes 1572872 | tf_op jit(solution)/shard_map/ppermute | solution.py:141
  38.5 14.1 %collective-permute-start.16 = (bf16[8,128,256]{2,1,0:T(8,128)(2,1)S(1)}, bf16[8,128,256]{2,1,0:T(8,128)(2,1)S(1)}, u32[]{:S(2)}, u32[]{:S(2)}) collective-permute-start(bf16[8,128,256]{2,1,0:T(8,128)(2,1)S(1)} %collective-permute-done.15.refs_15_), channel_id=1, source_target_pairs={{0,192},{8,56},{16,208},{24,8},{32,224},{40,24},{48,240},{56,40},{... | collective-permute-start | bytes 1572872 | tf_op jit(solution)/shard_map/ppermute | solution.py:143
  41.9 10.6 %collective-permute-start.9 = (bf16[128,1024]{1,0:T(8,128)(2,1)S(1)}, bf16[128,1024]{1,0:T(8,128)(2,1)S(1)}, u32[]{:S(2)}, u32[]{:S(2)}) collective-permute-start(bf16[128,1024]{1,0:T(8,128)(2,1)S(1)} %collective-permute-done.8), channel_id=1, source_target_pairs={{0,192},{8,56},{16,208},{24,8},{32,224},{40,24},{48,240},{56,40},{... | collective-permute-start | bytes 786440 | tf_op jit(solution)/shard_map/ppermute | solution.py:129
  53.2 9.8 %collective-permute-start.20 = (bf16[3,256,256]{2,1,0:T(8,128)(2,1)S(1)}, bf16[3,256,256]{2,1,0:T(8,128)(2,1)S(1)}, u32[]{:S(2)}, u32[]{:S(2)}) collective-permute-start(bf16[3,256,256]{2,1,0:T(8,128)(2,1)S(1)} %shard_map.88), channel_id=1, source_target_pairs={{0,32},{8,136},{16,48},{24,152},{32,0},{40,168},{48,16},{56,184},{... | collective-permute-start | bytes 1179656 | tf_op jit(solution)/shard_map/ppermute | solution.py:156
  57.1 9.4 %collective-permute-start.21 = (bf16[3,256,256]{2,1,0:T(8,128)(2,1)S(1)}, bf16[3,256,256]{2,1,0:T(8,128)(2,1)S(1)}, u32[]{:S(2)}, u32[]{:S(2)}) collective-permute-start(bf16[3,256,256]{2,1,0:T(8,128)(2,1)S(1)} %get-tuple-element.40), channel_id=1, source_target_pairs={{0,16},{8,72},{16,32},{24,88},{32,48},{40,104},{48,0},{56,120},{64... | collective-permute-start | bytes 1179656 | tf_op jit(solution)/shard_map/ppermute | solution.py:156
  57.5 9.0 %collective-permute-start.22 = (bf16[3,256,256]{2,1,0:T(8,128)(2,1)S(1)}, bf16[3,256,256]{2,1,0:T(8,128)(2,1)S(1)}, u32[]{:S(2)}, u32[]{:S(2)}) collective-permute-start(bf16[3,256,256]{2,1,0:T(8,128)(2,1)S(1)} %get-tuple-element.41), channel_id=1, source_target_pairs={{0,48},{8,200},{16,0},{24,216},{32,16},{40,232},{48,32},{56,248},{... | collective-permute-start | bytes 1179656 | tf_op jit(solution)/shard_map/ppermute | solution.py:156
  60.7 12.3 %collective-permute-start.17 = (bf16[5,256,256]{2,1,0:T(8,128)(2,1)S(1)}, bf16[5,256,256]{2,1,0:T(8,128)(2,1)S(1)}, u32[]{:S(2)}, u32[]{:S(2)}) collective-permute-start(bf16[5,256,256]{2,1,0:T(8,128)(2,1)S(1)} %shard_map.86), channel_id=1, source_target_pairs={{0,32},{8,136},{16,48},{24,152},{32,0},{40,168},{48,16},{56,184},{... | collective-permute-start | bytes 1966088 | tf_op jit(solution)/shard_map/ppermute | solution.py:156
  62.4 17.6 %collective-permute-start.18 = (bf16[5,256,256]{2,1,0:T(8,128)(2,1)S(1)}, bf16[5,256,256]{2,1,0:T(8,128)(2,1)S(1)}, u32[]{:S(2)}, u32[]{:S(2)}) collective-permute-start(bf16[5,256,256]{2,1,0:T(8,128)(2,1)S(1)} %get-tuple-element.37), channel_id=1, source_target_pairs={{0,16},{8,72},{16,32},{24,88},{32,48},{40,104},{48,0},{56,120},{64... | collective-permute-start | bytes 1966088 | tf_op jit(solution)/shard_map/ppermute | solution.py:156
  63.1 17.1 %collective-permute-start.19 = (bf16[5,256,256]{2,1,0:T(8,128)(2,1)S(1)}, bf16[5,256,256]{2,1,0:T(8,128)(2,1)S(1)}, u32[]{:S(2)}, u32[]{:S(2)}) collective-permute-start(bf16[5,256,256]{2,1,0:T(8,128)(2,1)S(1)} %get-tuple-element.38), channel_id=1, source_target_pairs={{0,48},{8,200},{16,0},{24,216},{32,16},{40,232},{48,32},{56,248},{... | collective-permute-start | bytes 1966088 | tf_op jit(solution)/shard_map/ppermute | solution.py:156
  66.7 13.8 %collective-permute-start.25 = (bf16[256,256]{1,0:T(8,128)(2,1)S(1)}, bf16[256,256]{1,0:T(8,128)(2,1)S(1)}, u32[]{:S(2)}, u32[]{:S(2)}) collective-permute-start(bf16[256,256]{1,0:T(8,128)(2,1)S(1)} %get-tuple-element.54), channel_id=1, source_target_pairs={{0,1},{1,2},{2,3},{3,4},{4,5},{5,6},{6,7},{7,0},{8,9},{9,10},{10,1... | collective-permute-start | bytes 393224 | tf_op jit(solution)/shard_map/ppermute | solution.py:165
  67.1 13.5 %collective-permute-start.27 = (bf16[256,256]{1,0:T(8,128)(2,1)S(1)}, bf16[256,256]{1,0:T(8,128)(2,1)S(1)}, u32[]{:S(2)}, u32[]{:S(2)}) collective-permute-start(bf16[256,256]{1,0:T(8,128)(2,1)S(1)} %get-tuple-element.53), channel_id=1, source_target_pairs={{0,7},{1,0},{2,1},{3,2},{4,3},{5,4},{6,5},{7,6},{8,15},{9,8},{10,9... | collective-permute-start | bytes 393224 | tf_op jit(solution)/shard_map/ppermute | solution.py:165
  73.0 14.0 %collective-permute-start.23 = (bf16[256,256]{1,0:T(8,128)(2,1)S(1)}, bf16[256,256]{1,0:T(8,128)(2,1)S(1)}, u32[]{:S(2)}, u32[]{:S(2)}) collective-permute-start(bf16[256,256]{1,0:T(8,128)(2,1)S(1)} %get-tuple-element.52), channel_id=1, source_target_pairs={{0,4},{1,5},{2,6},{3,7},{4,0},{5,1},{6,2},{7,3},{8,12},{9,13},{10,... | collective-permute-start | bytes 393224 | tf_op jit(solution)/shard_map/ppermute | solution.py:165
  80.5 11.7 %copy-start.1 = (f32[256,256]{1,0:T(8,128)S(1)}, f32[256,256]{1,0:T(8,128)}, u32[]{:S(2)}) copy-start(f32[256,256]{1,0:T(8,128)} %param.7) | copy-start | bytes 786436
  80.5 11.6 %copy-start.2 = (f32[256,256]{1,0:T(8,128)S(1)}, f32[256,256]{1,0:T(8,128)}, u32[]{:S(2)}) copy-start(f32[256,256]{1,0:T(8,128)} %param.8) | copy-start | bytes 786436
  80.5 11.6 %copy-start.3 = (f32[256,256]{1,0:T(8,128)S(1)}, f32[256,256]{1,0:T(8,128)}, u32[]{:S(2)}) copy-start(f32[256,256]{1,0:T(8,128)} %param.9) | copy-start | bytes 786436
  80.6 6.5 %collective-permute-start.26 = (bf16[256,256]{1,0:T(8,128)(2,1)S(1)}, bf16[256,256]{1,0:T(8,128)(2,1)S(1)}, u32[]{:S(2)}, u32[]{:S(2)}) collective-permute-start(bf16[256,256]{1,0:T(8,128)(2,1)S(1)} %get-tuple-element.48), channel_id=1, source_target_pairs={{0,2},{1,3},{2,4},{3,5},{4,6},{5,7},{6,0},{7,1},{8,10},{9,11},{10,... | collective-permute-start | bytes 393224 | tf_op jit(solution)/shard_map/ppermute | solution.py:165
  82.0 9.0 %collective-permute-start.28 = (bf16[256,256]{1,0:T(8,128)(2,1)S(1)}, bf16[256,256]{1,0:T(8,128)(2,1)S(1)}, u32[]{:S(2)}, u32[]{:S(2)}) collective-permute-start(bf16[256,256]{1,0:T(8,128)(2,1)S(1)} %get-tuple-element.49), channel_id=1, source_target_pairs={{0,6},{1,7},{2,0},{3,1},{4,2},{5,3},{6,4},{7,5},{8,14},{9,15},{10,... | collective-permute-start | bytes 393224 | tf_op jit(solution)/shard_map/ppermute | solution.py:165
  84.3 7.8 %collective-permute-start.24 = (bf16[256,256]{1,0:T(8,128)(2,1)S(1)}, bf16[256,256]{1,0:T(8,128)(2,1)S(1)}, u32[]{:S(2)}, u32[]{:S(2)}) collective-permute-start(bf16[256,256]{1,0:T(8,128)(2,1)S(1)} %get-tuple-element.50), channel_id=1, source_target_pairs={{0,1},{1,2},{2,3},{3,4},{4,5},{5,6},{6,7},{7,0},{8,9},{9,10},{10,1... | collective-permute-start | bytes 393224 | tf_op jit(solution)/shard_map/ppermute | solution.py:165
  84.7 7.4 %collective-permute-start.29 = (bf16[256,256]{1,0:T(8,128)(2,1)S(1)}, bf16[256,256]{1,0:T(8,128)(2,1)S(1)}, u32[]{:S(2)}, u32[]{:S(2)}) collective-permute-start(bf16[256,256]{1,0:T(8,128)(2,1)S(1)} %get-tuple-element.51), channel_id=1, source_target_pairs={{0,7},{1,0},{2,1},{3,2},{4,3},{5,4},{6,5},{7,6},{8,15},{9,8},{10,9... | collective-permute-start | bytes 393224 | tf_op jit(solution)/shard_map/ppermute | solution.py:165
  93.2 6.4 %collective-permute-start.30 = (bf16[256,256]{1,0:T(8,128)(2,1)S(1)}, bf16[256,256]{1,0:T(8,128)(2,1)S(1)}, u32[]{:S(2)}, u32[]{:S(2)}) collective-permute-start(bf16[256,256]{1,0:T(8,128)(2,1)S(1)} %get-tuple-element.42), channel_id=1, source_target_pairs={{0,64},{8,24},{16,80},{24,40},{32,96},{40,56},{48,112},{56,8},{64,... | collective-permute-start | bytes 393224 | tf_op jit(solution)/shard_map/ppermute | solution.py:184
  93.3 9.3 %collective-permute-start.31 = (bf16[256,256]{1,0:T(8,128)(2,1)S(1)}, bf16[256,256]{1,0:T(8,128)(2,1)S(1)}, u32[]{:S(2)}, u32[]{:S(2)}) collective-permute-start(bf16[256,256]{1,0:T(8,128)(2,1)S(1)} %get-tuple-element.42), channel_id=1, source_target_pairs={{0,128},{8,40},{16,144},{24,56},{32,160},{40,8},{48,176},{56,24},{... | collective-permute-start | bytes 393224 | tf_op jit(solution)/shard_map/ppermute | solution.py:184
  98.5 4.1 %collective-permute-start.32 = (bf16[256,256]{1,0:T(8,128)(2,1)S(1)}, bf16[256,256]{1,0:T(8,128)(2,1)S(1)}, u32[]{:S(2)}, u32[]{:S(2)}) collective-permute-start(bf16[256,256]{1,0:T(8,128)(2,1)S(1)} %get-tuple-element.42), channel_id=1, source_target_pairs={{0,192},{8,56},{16,208},{24,8},{32,224},{40,24},{48,240},{56,40},{... | collective-permute-start | bytes 393224 | tf_op jit(solution)/shard_map/ppermute | solution.py:184
  102.7 9.6 %collective-permute-start.33 = (bf16[4,256,256]{2,1,0:T(8,128)(2,1)S(1)}, bf16[4,256,256]{2,1,0:T(8,128)(2,1)S(1)}, u32[]{:S(2)}, u32[]{:S(2)}) collective-permute-start(bf16[4,256,256]{2,1,0:T(8,128)(2,1)S(1)} %pad_maximum_fusion.refs_0_), channel_id=1, source_target_pairs={{0,16},{8,72},{16,32},{24,88},{32,48},{40,104},{48,0},{56,120},{64... | collective-permute-start | bytes 1572872 | tf_op jit(solution)/shard_map/ppermute | solution.py:186
  104.3 14.1 %collective-permute-start.34 = (bf16[4,256,256]{2,1,0:T(8,128)(2,1)S(1)}, bf16[4,256,256]{2,1,0:T(8,128)(2,1)S(1)}, u32[]{:S(2)}, u32[]{:S(2)}) collective-permute-start(bf16[4,256,256]{2,1,0:T(8,128)(2,1)S(1)} %pad_maximum_fusion.refs_0_), channel_id=1, source_target_pairs={{0,32},{8,136},{16,48},{24,152},{32,0},{40,168},{48,16},{56,184},{... | collective-permute-start | bytes 1572872 | tf_op jit(solution)/shard_map/ppermute | solution.py:186
  106.0 17.0 %collective-permute-start.35 = (bf16[4,256,256]{2,1,0:T(8,128)(2,1)S(1)}, bf16[4,256,256]{2,1,0:T(8,128)(2,1)S(1)}, u32[]{:S(2)}, u32[]{:S(2)}) collective-permute-start(bf16[4,256,256]{2,1,0:T(8,128)(2,1)S(1)} %pad_maximum_fusion.refs_0_), channel_id=1, source_target_pairs={{0,48},{8,200},{16,0},{24,216},{32,16},{40,232},{48,32},{56,248},{... | collective-permute-start | bytes 1572872 | tf_op jit(solution)/shard_map/ppermute | solution.py:186
  107.9 15.0 %collective-permute-start.36 = (bf16[4,256,256]{2,1,0:T(8,128)(2,1)S(1)}, bf16[4,256,256]{2,1,0:T(8,128)(2,1)S(1)}, u32[]{:S(2)}, u32[]{:S(2)}) collective-permute-start(bf16[4,256,256]{2,1,0:T(8,128)(2,1)S(1)} %pad_maximum_fusion.refs_0_), channel_id=1, source_target_pairs={{0,8},{8,0},{16,24},{24,16},{32,40},{40,32},{48,56},{56,48},{64,72... | collective-permute-start | bytes 1572872 | tf_op jit(solution)/shard_map/ppermute | solution.py:188
  112.3 10.7 %collective-permute-start.37 = (bf16[4,256,256]{2,1,0:T(8,128)(2,1)S(1)}, bf16[4,256,256]{2,1,0:T(8,128)(2,1)S(1)}, u32[]{:S(2)}, u32[]{:S(2)}) collective-permute-start(bf16[4,256,256]{2,1,0:T(8,128)(2,1)S(1)} %collective-permute-done.33.refs_1_), channel_id=1, source_target_pairs={{0,8},{8,0},{16,24},{24,16},{32,40},{40,32},{48,56},{56,48},{64,72... | collective-permute-start | bytes 1572872 | tf_op jit(solution)/shard_map/ppermute | solution.py:188
  118.3 6.1 %collective-permute-start.38 = (bf16[4,256,256]{2,1,0:T(8,128)(2,1)S(1)}, bf16[4,256,256]{2,1,0:T(8,128)(2,1)S(1)}, u32[]{:S(2)}, u32[]{:S(2)}) collective-permute-start(bf16[4,256,256]{2,1,0:T(8,128)(2,1)S(1)} %collective-permute-done.34.refs_2_), channel_id=1, source_target_pairs={{0,8},{8,0},{16,24},{24,16},{32,40},{40,32},{48,56},{56,48},{64,72... | collective-permute-start | bytes 1572872 | tf_op jit(solution)/shard_map/ppermute | solution.py:188
  122.9 2.3 %collective-permute-start.39 = (bf16[4,256,256]{2,1,0:T(8,128)(2,1)S(1)}, bf16[4,256,256]{2,1,0:T(8,128)(2,1)S(1)}, u32[]{:S(2)}, u32[]{:S(2)}) collective-permute-start(bf16[4,256,256]{2,1,0:T(8,128)(2,1)S(1)} %collective-permute-done.35.refs_3_), channel_id=1, source_target_pairs={{0,8},{8,0},{16,24},{24,16},{32,40},{40,32},{48,56},{56,48},{64,72... | collective-permute-start | bytes 1572872 | tf_op jit(solution)/shard_map/ppermute | solution.py:188

commit v7 on v6

--- a/solution.py
+++ b/solution.py
@@ -125,11 +125,10 @@
     chunk = kept((tokens, wide), jnp.bfloat16)
     chunks = mover(functools.partial(blocks_kernel, rows), [chunk] * (2 * SIDE), 1)(activations)
     from_peer = [lax.ppermute(part, "dp", CORE_SWAP) for part in chunks[SIDE:]]
-    acts = [
-        part[i] if i == 0 else lax.ppermute(part[i], "dp", ring(i, 0))
-        for part in (chunks[:SIDE], from_peer)
-        for i in range(SIDE)
-    ]
+    acts = []
+    for part in (chunks[:SIDE], from_peer):
+        sent = {i: lax.ppermute(part[i], "dp", ring(i, 0)) for i in (2, 1, 3)}
+        acts += [part[0]] + [sent[i] for i in range(1, SIDE)]
 
     mine = lax.all_to_all(out_grads.reshape(panels, tokens, cols), "tensor", 0, 0)
     early = (2, 6, 1, 3)

time: 128 us -> 128 us (level)
  no operation moved by 1% of the time
where the time goes in v7:
time: 128 us
  starting transfers between devices  71.1 us (56%)
  waiting for transfers between devices  44.1 us (34%)
  Pallas kernels  8.2 us (6%)
  other arithmetic  1.78 us (1%)
  local copies, waits for them, and re-layouts  1.65 us (1%)
    ppermute x6, waiting for transfers between devices, per_device(): sent = {i: lax.ppermute(part[i], 'dp', ring(i, 0)) for i in (2, 1, 3)}  17.4 us
    ppermute x7, starting transfers between devices, along_tensor(): lax.ppermute(part, 'tensor', [(i, (i + step) % panels) for i in range(pan...  13.6 us
    ppermute x4, starting transfers between devices, per_device(): peer = [lax.ppermute(part, 'dp', CORE_SWAP) for part in own]  10.4 us
    all_to_all x1, starting transfers between devices, per_device(): lax.all_to_all(out_grads.reshape(panels, tokens, cols), 'tensor', 0, 0)  9.03 us
    ppermute x6, starting transfers between devices, per_device(): lax.ppermute(part, 'dp', ring(i, 1))  8.43 us
    ppermute x6, starting transfers between devices, per_device(): sent = {i: lax.ppermute(part[i], 'dp', ring(i, 0)) for i in (2, 1, 3)}  7.16 us
    ppermute x6, waiting for transfers between devices, per_device(): lax.ppermute(part, 'dp', ring(i, 1))  6.25 us
    pallas_call x5, Pallas kernels, product(): mover(functools.partial(product_kernel, which, rows), [kept((len(away), r...  5.41 us
  transfers between devices with their start and end apart: 41, of which 23 were waited for; matrix products, arithmetic and copies ran while one was open for 1% of the time, Pallas kernels for 4%

profile of v7, /device:TPU:1, one launch (start us, length us, event | category | flops | bytes accessed | tf_op | source)
XLA Modules:
  0.0 127.7 jit_solution(1672629259523708842)
XLA Ops:
  0.6 9.0 %all-to-all-start = ((bf16[8,128,256]{2,1,0:T(8,128)(2,1)}), bf16[8,128,256]{2,1,0:T(8,128)(2,1)S(1)}, u32[]{:S(2)}, u32[]{:S(2)}) async-start(bf16[8,128,256]{2,1,0:T(8,128)(2,1)} %bitcast.41), calls=%async_computation | async-start | bytes 1048576 | tf_op jit(solution)/shard_map/all_to_all | solution.py:133
  9.7 1.6 %copy-done = bf16[128,8192]{1,0:T(8,128)(2,1)S(1)} copy-done((bf16[128,8192]{1,0:T(8,128)(2,1)S(1)}, bf16[128,8192]{1,0:T(8,128)(2,1)}, u32[]{:S(2)}) %copy-start) | copy-done | bytes 2097176
  11.2 0.3 shard_map.84
  11.6 1.0 collective-permute-start.1
  12.6 2.9 %collective-permute-start = (bf16[128,1024]{1,0:T(8,128)(2,1)S(1)}, bf16[128,1024]{1,0:T(8,128)(2,1)S(1)}, u32[]{:S(2)}, u32[]{:S(2)}) collective-permute-start(bf16[128,1024]{1,0:T(8,128)(2,1)S(1)} %get-tuple-element.24), channel_id=1, source_target_pairs={{0,128},{8,40},{16,144},{24,56},{32,160},{40,8},{48,176},{56,24},{... | collective-permute-start | bytes 786440 | tf_op jit(solution)/shard_map/ppermute | solution.py:130
  15.5 0.4 collective-permute-start.3
  15.9 2.3 %collective-permute-start.4 = (bf16[128,1024]{1,0:T(8,128)(2,1)S(1)}, bf16[128,1024]{1,0:T(8,128)(2,1)S(1)}, u32[]{:S(2)}, u32[]{:S(2)}) collective-permute-start(bf16[128,1024]{1,0:T(8,128)(2,1)S(1)} %get-tuple-element.27), channel_id=1, source_target_pairs={{0,192},{8,56},{16,208},{24,8},{32,224},{40,24},{48,240},{56,40},{... | collective-permute-start | bytes 786440 | tf_op jit(solution)/shard_map/ppermute | solution.py:130
  18.2 1.4 %collective-permute-done.refs_2_ = bf16[128,1024]{1,0:T(8,128)(2,1)S(1)} collective-permute-done((bf16[128,1024]{1,0:T(8,128)(2,1)S(1)}, bf16[128,1024]{1,0:T(8,128)(2,1)S(1)}, u32[]{:S(2)}, u32[]{:S(2)}) %collective-permute-start) | collective-permute-done | bytes 262176 | tf_op jit(solution)/shard_map/ppermute | solution.py:130
  19.6 2.8 %collective-permute-done.3.refs_1_ = bf16[128,1024]{1,0:T(8,128)(2,1)S(1)} collective-permute-done((bf16[128,1024]{1,0:T(8,128)(2,1)S(1)}, bf16[128,1024]{1,0:T(8,128)(2,1)S(1)}, u32[]{:S(2)}, u32[]{:S(2)}) %collective-permute-start.3) | collective-permute-done | bytes 262176 | tf_op jit(solution)/shard_map/ppermute | solution.py:130
  22.4 0.3 collective-permute-done.4.refs_3_
  22.8 2.5 %collective-permute-done.2.refs_6_ = bf16[128,1024]{1,0:T(8,128)(2,1)S(1)} collective-permute-done((bf16[128,1024]{1,0:T(8,128)(2,1)S(1)}, bf16[128,1024]{1,0:T(8,128)(2,1)S(1)}, u32[]{:S(2)}, u32[]{:S(2)}) %collective-permute-start.2) | collective-permute-done | bytes 262176 | tf_op jit(solution)/shard_map/ppermute | solution.py:130
  25.2 2.4 %all-to-all-done.refs_8_ = bf16[8,128,256]{2,1,0:T(8,128)(2,1)S(1)} async-done(((bf16[8,128,256]{2,1,0:T(8,128)(2,1)}), bf16[8,128,256]{2,1,0:T(8,128)(2,1)S(1)}, u32[]{:S(2)}, u32[]{:S(2)}) %all-to-all-start) | async-done | bytes 524320 | tf_op jit(solution)/shard_map/all_to_all | solution.py:133
  27.6 0.5 collective-permute-start.13
  28.1 1.3 %collective-permute-start.10 = (bf16[8,128,256]{2,1,0:T(8,128)(2,1)S(1)}, bf16[8,128,256]{2,1,0:T(8,128)(2,1)S(1)}, u32[]{:S(2)}, u32[]{:S(2)}) collective-permute-start(bf16[8,128,256]{2,1,0:T(8,128)(2,1)S(1)} %all-to-all-done.refs_8_), channel_id=1, source_target_pairs={{0,64},{8,24},{16,80},{24,40},{32,96},{40,56},{48,112},{56,8},{64,... | collective-permute-start | bytes 1572872 | tf_op jit(solution)/shard_map/ppermute | solution.py:139
  29.4 0.2 collective-permute-done.13.refs_12_
  29.6 2.7 %collective-permute-start.15 = (bf16[8,128,256]{2,1,0:T(8,128)(2,1)S(1)}, bf16[8,128,256]{2,1,0:T(8,128)(2,1)S(1)}, u32[]{:S(2)}, u32[]{:S(2)}) collective-permute-start(bf16[8,128,256]{2,1,0:T(8,128)(2,1)S(1)} %collective-permute-done.13.refs_12_), channel_id=1, source_target_pairs={{0,192},{8,56},{16,208},{24,8},{32,224},{40,24},{48,240},{56,40},{... | collective-permute-start | bytes 1572872 | tf_op jit(solution)/shard_map/ppermute | solution.py:141
  32.4 0.4 collective-permute-start.6
  32.9 0.4 collective-permute-start.5
  33.3 0.7 collective-permute-done.6
  33.9 1.3 %collective-permute-start.7 = (bf16[128,1024]{1,0:T(8,128)(2,1)S(1)}, bf16[128,1024]{1,0:T(8,128)(2,1)S(1)}, u32[]{:S(2)}, u32[]{:S(2)}) collective-permute-start(bf16[128,1024]{1,0:T(8,128)(2,1)S(1)} %collective-permute-done.6), channel_id=1, source_target_pairs={{0,64},{8,24},{16,80},{24,40},{32,96},{40,56},{48,112},{56,8},{64,... | collective-permute-start | bytes 786440 | tf_op jit(solution)/shard_map/ppermute | solution.py:130
  35.2 1.8 %collective-permute-start.12 = (bf16[8,128,256]{2,1,0:T(8,128)(2,1)S(1)}, bf16[8,128,256]{2,1,0:T(8,128)(2,1)S(1)}, u32[]{:S(2)}, u32[]{:S(2)}) collective-permute-start(bf16[8,128,256]{2,1,0:T(8,128)(2,1)S(1)} %all-to-all-done.refs_8_), channel_id=1, source_target_pairs={{0,192},{8,56},{16,208},{24,8},{32,224},{40,24},{48,240},{56,40},{... | collective-permute-start | bytes 1572872 | tf_op jit(solution)/shard_map/ppermute | solution.py:139
  37.1 0.6 collective-permute-done.10.refs_9_
  37.7 0.3 collective-permute-start.11
  38.0 0.5 collective-permute-done.15.refs_15_
  38.5 3.4 %collective-permute-start.16 = (bf16[8,128,256]{2,1,0:T(8,128)(2,1)S(1)}, bf16[8,128,256]{2,1,0:T(8,128)(2,1)S(1)}, u32[]{:S(2)}, u32[]{:S(2)}) collective-permute-start(bf16[8,128,256]{2,1,0:T(8,128)(2,1)S(1)} %collective-permute-done.15.refs_15_), channel_id=1, source_target_pairs={{0,192},{8,56},{16,208},{24,8},{32,224},{40,24},{48,240},{56,40},{... | collective-permute-start | bytes 1572872 | tf_op jit(solution)/shard_map/ppermute | solution.py:142
  41.9 0.3 collective-permute-start.9
  42.2 10.4 %collective-permute-done.9.refs_7_ = bf16[128,1024]{1,0:T(8,128)(2,1)S(1)} collective-permute-done((bf16[128,1024]{1,0:T(8,128)(2,1)S(1)}, bf16[128,1024]{1,0:T(8,128)(2,1)S(1)}, u32[]{:S(2)}, u32[]{:S(2)}) %collective-permute-start.9) | collective-permute-done | bytes 262176 | tf_op jit(solution)/shard_map/ppermute | solution.py:130
  52.6 0.6 shard_map.88
  53.2 2.8 %collective-permute-start.20 = (bf16[3,256,256]{2,1,0:T(8,128)(2,1)S(1)}, bf16[3,256,256]{2,1,0:T(8,128)(2,1)S(1)}, u32[]{:S(2)}, u32[]{:S(2)}) collective-permute-start(bf16[3,256,256]{2,1,0:T(8,128)(2,1)S(1)} %shard_map.88), channel_id=1, source_target_pairs={{0,32},{8,136},{16,48},{24,152},{32,0},{40,168},{48,16},{56,184},{... | collective-permute-start | bytes 1179656 | tf_op jit(solution)/shard_map/ppermute | solution.py:155
  56.1 1.0 shard_map.89
  57.1 0.4 collective-permute-start.21
  57.5 2.4 %collective-permute-start.22 = (bf16[3,256,256]{2,1,0:T(8,128)(2,1)S(1)}, bf16[3,256,256]{2,1,0:T(8,128)(2,1)S(1)}, u32[]{:S(2)}, u32[]{:S(2)}) collective-permute-start(bf16[3,256,256]{2,1,0:T(8,128)(2,1)S(1)} %get-tuple-element.41), channel_id=1, source_target_pairs={{0,48},{8,200},{16,0},{24,216},{32,16},{40,232},{48,32},{56,248},{... | collective-permute-start | bytes 1179656 | tf_op jit(solution)/shard_map/ppermute | solution.py:155
  59.8 0.9 shard_map.86
  60.8 1.6 %shard_map.87 = (bf16[5,256,256]{2,1,0:T(8,128)(2,1)S(1)}, bf16[5,256,256]{2,1,0:T(8,128)(2,1)S(1)}) custom-call(bf16[128,1024]{1,0:T(8,128)(2,1)S(1)} %get-tuple-element.23.refs_0_, bf16[128,1024]{1,0:T(8,128)(2,1)S(1)} %collective-permute-done.3.refs_1_, bf16[128,1024]{1,0:T(8,128)(2,1)S(1)} %collective-permute-done.refs_2_, ...), custom_call_target="tpu_custom_call" | custom-call | tf_op jit(solution)/shard_map/pallas_call | solution.py:145
  62.4 0.6 collective-permute-start.18
  63.1 2.1 %collective-permute-start.19 = (bf16[5,256,256]{2,1,0:T(8,128)(2,1)S(1)}, bf16[5,256,256]{2,1,0:T(8,128)(2,1)S(1)}, u32[]{:S(2)}, u32[]{:S(2)}) collective-permute-start(bf16[5,256,256]{2,1,0:T(8,128)(2,1)S(1)} %get-tuple-element.38), channel_id=1, source_target_pairs={{0,48},{8,200},{16,0},{24,216},{32,16},{40,232},{48,32},{56,248},{... | collective-permute-start | bytes 1966088 | tf_op jit(solution)/shard_map/ppermute | solution.py:155
  65.2 1.3 %shard_map.85 = (bf16[3,256,256]{2,1,0:T(8,128)(2,1)S(1)}, bf16[5,256,256]{2,1,0:T(8,128)(2,1)S(1)}) custom-call(bf16[128,1024]{1,0:T(8,128)(2,1)S(1)} %get-tuple-element.23.refs_0_, bf16[128,1024]{1,0:T(8,128)(2,1)S(1)} %collective-permute-done.3.refs_1_, bf16[128,1024]{1,0:T(8,128)(2,1)S(1)} %collective-permute-done.refs_2_, ...), custom_call_target="tpu_custom_call" | custom-call | tf_op jit(solution)/shard_map/pallas_call | solution.py:145
  66.7 0.4 collective-permute-start.25
  67.1 2.4 %collective-permute-start.27 = (bf16[256,256]{1,0:T(8,128)(2,1)S(1)}, bf16[256,256]{1,0:T(8,128)(2,1)S(1)}, u32[]{:S(2)}, u32[]{:S(2)}) collective-permute-start(bf16[256,256]{1,0:T(8,128)(2,1)S(1)} %get-tuple-element.53), channel_id=1, source_target_pairs={{0,7},{1,0},{2,1},{3,2},{4,3},{5,4},{6,5},{7,6},{8,15},{9,8},{10,9... | collective-permute-start | bytes 393224 | tf_op jit(solution)/shard_map/ppermute | solution.py:164
  69.5 3.5 %collective-permute-done.17 = bf16[5,256,256]{2,1,0:T(8,128)(2,1)S(1)} collective-permute-done((bf16[5,256,256]{2,1,0:T(8,128)(2,1)S(1)}, bf16[5,256,256]{2,1,0:T(8,128)(2,1)S(1)}, u32[]{:S(2)}, u32[]{:S(2)}) %collective-permute-start.17) | collective-permute-done | bytes 655392 | tf_op jit(solution)/shard_map/ppermute | solution.py:155
  73.0 4.4 %collective-permute-start.23 = (bf16[256,256]{1,0:T(8,128)(2,1)S(1)}, bf16[256,256]{1,0:T(8,128)(2,1)S(1)}, u32[]{:S(2)}, u32[]{:S(2)}) collective-permute-start(bf16[256,256]{1,0:T(8,128)(2,1)S(1)} %get-tuple-element.52), channel_id=1, source_target_pairs={{0,4},{1,5},{2,6},{3,7},{4,0},{5,1},{6,2},{7,3},{8,12},{9,13},{10,... | collective-permute-start | bytes 393224 | tf_op jit(solution)/shard_map/ppermute | solution.py:164
  77.4 2.6 %collective-permute-done.18 = bf16[5,256,256]{2,1,0:T(8,128)(2,1)S(1)} collective-permute-done((bf16[5,256,256]{2,1,0:T(8,128)(2,1)S(1)}, bf16[5,256,256]{2,1,0:T(8,128)(2,1)S(1)}, u32[]{:S(2)}, u32[]{:S(2)}) %collective-permute-start.18) | collective-permute-done | bytes 655392 | tf_op jit(solution)/shard_map/ppermute | solution.py:155
  80.1 0.4 fusion.12
  80.6 1.3 %collective-permute-start.26 = (bf16[256,256]{1,0:T(8,128)(2,1)S(1)}, bf16[256,256]{1,0:T(8,128)(2,1)S(1)}, u32[]{:S(2)}, u32[]{:S(2)}) collective-permute-start(bf16[256,256]{1,0:T(8,128)(2,1)S(1)} %get-tuple-element.48), channel_id=1, source_target_pairs={{0,2},{1,3},{2,4},{3,5},{4,6},{5,7},{6,0},{7,1},{8,10},{9,11},{10,... | collective-permute-start | bytes 393224 | tf_op jit(solution)/shard_map/ppermute | solution.py:164
  82.0 2.3 %collective-permute-start.28 = (bf16[256,256]{1,0:T(8,128)(2,1)S(1)}, bf16[256,256]{1,0:T(8,128)(2,1)S(1)}, u32[]{:S(2)}, u32[]{:S(2)}) collective-permute-start(bf16[256,256]{1,0:T(8,128)(2,1)S(1)} %get-tuple-element.49), channel_id=1, source_target_pairs={{0,6},{1,7},{2,0},{3,1},{4,2},{5,3},{6,4},{7,5},{8,14},{9,15},{10,... | collective-permute-start | bytes 393224 | tf_op jit(solution)/shard_map/ppermute | solution.py:164
  84.3 0.4 collective-permute-start.24
  84.7 2.3 %collective-permute-start.29 = (bf16[256,256]{1,0:T(8,128)(2,1)S(1)}, bf16[256,256]{1,0:T(8,128)(2,1)S(1)}, u32[]{:S(2)}, u32[]{:S(2)}) collective-permute-start(bf16[256,256]{1,0:T(8,128)(2,1)S(1)} %get-tuple-element.51), channel_id=1, source_target_pairs={{0,7},{1,0},{2,1},{3,2},{4,3},{5,4},{6,5},{7,6},{8,15},{9,8},{10,9... | collective-permute-start | bytes 393224 | tf_op jit(solution)/shard_map/ppermute | solution.py:164
  87.2 3.8 %collective-permute-done.28 = bf16[256,256]{1,0:T(8,128)(2,1)S(1)} collective-permute-done((bf16[256,256]{1,0:T(8,128)(2,1)S(1)}, bf16[256,256]{1,0:T(8,128)(2,1)S(1)}, u32[]{:S(2)}, u32[]{:S(2)}) %collective-permute-start.28) | collective-permute-done | bytes 131104 | tf_op jit(solution)/shard_map/ppermute | solution.py:164
  90.9 1.2 collective-permute-done.24
  92.2 1.1 fusion.10
  93.3 5.2 %collective-permute-start.31 = (bf16[256,256]{1,0:T(8,128)(2,1)S(1)}, bf16[256,256]{1,0:T(8,128)(2,1)S(1)}, u32[]{:S(2)}, u32[]{:S(2)}) collective-permute-start(bf16[256,256]{1,0:T(8,128)(2,1)S(1)} %get-tuple-element.42), channel_id=1, source_target_pairs={{0,128},{8,40},{16,144},{24,56},{32,160},{40,8},{48,176},{56,24},{... | collective-permute-start | bytes 393224 | tf_op jit(solution)/shard_map/ppermute | solution.py:183
  98.5 1.2 collective-permute-done.30
  99.6 2.9 %collective-permute-done.31 = bf16[256,256]{1,0:T(8,128)(2,1)S(1)} collective-permute-done((bf16[256,256]{1,0:T(8,128)(2,1)S(1)}, bf16[256,256]{1,0:T(8,128)(2,1)S(1)}, u32[]{:S(2)}, u32[]{:S(2)}) %collective-permute-start.31) | collective-permute-done | bytes 131104 | tf_op jit(solution)/shard_map/ppermute | solution.py:183
  102.7 1.6 %collective-permute-start.33 = (bf16[4,256,256]{2,1,0:T(8,128)(2,1)S(1)}, bf16[4,256,256]{2,1,0:T(8,128)(2,1)S(1)}, u32[]{:S(2)}, u32[]{:S(2)}) collective-permute-start(bf16[4,256,256]{2,1,0:T(8,128)(2,1)S(1)} %pad_maximum_fusion.refs_0_), channel_id=1, source_target_pairs={{0,16},{8,72},{16,32},{24,88},{32,48},{40,104},{48,0},{56,120},{64... | collective-permute-start | bytes 1572872 | tf_op jit(solution)/shard_map/ppermute | solution.py:185
  104.3 1.7 %collective-permute-start.34 = (bf16[4,256,256]{2,1,0:T(8,128)(2,1)S(1)}, bf16[4,256,256]{2,1,0:T(8,128)(2,1)S(1)}, u32[]{:S(2)}, u32[]{:S(2)}) collective-permute-start(bf16[4,256,256]{2,1,0:T(8,128)(2,1)S(1)} %pad_maximum_fusion.refs_0_), channel_id=1, source_target_pairs={{0,32},{8,136},{16,48},{24,152},{32,0},{40,168},{48,16},{56,184},{... | collective-permute-start | bytes 1572872 | tf_op jit(solution)/shard_map/ppermute | solution.py:185
  106.0 2.0 %collective-permute-start.35 = (bf16[4,256,256]{2,1,0:T(8,128)(2,1)S(1)}, bf16[4,256,256]{2,1,0:T(8,128)(2,1)S(1)}, u32[]{:S(2)}, u32[]{:S(2)}) collective-permute-start(bf16[4,256,256]{2,1,0:T(8,128)(2,1)S(1)} %pad_maximum_fusion.refs_0_), channel_id=1, source_target_pairs={{0,48},{8,200},{16,0},{24,216},{32,16},{40,232},{48,32},{56,248},{... | collective-permute-start | bytes 1572872 | tf_op jit(solution)/shard_map/ppermute | solution.py:185
  107.9 2.2 %collective-permute-start.36 = (bf16[4,256,256]{2,1,0:T(8,128)(2,1)S(1)}, bf16[4,256,256]{2,1,0:T(8,128)(2,1)S(1)}, u32[]{:S(2)}, u32[]{:S(2)}) collective-permute-start(bf16[4,256,256]{2,1,0:T(8,128)(2,1)S(1)} %pad_maximum_fusion.refs_0_), channel_id=1, source_target_pairs={{0,8},{8,0},{16,24},{24,16},{32,40},{40,32},{48,56},{56,48},{64,72... | collective-permute-start | bytes 1572872 | tf_op jit(solution)/shard_map/ppermute | solution.py:187
  110.1 2.1 %collective-permute-done.33.refs_1_ = bf16[4,256,256]{2,1,0:T(8,128)(2,1)S(1)} collective-permute-done((bf16[4,256,256]{2,1,0:T(8,128)(2,1)S(1)}, bf16[4,256,256]{2,1,0:T(8,128)(2,1)S(1)}, u32[]{:S(2)}, u32[]{:S(2)}) %collective-permute-start.33) | collective-permute-done | bytes 524320 | tf_op jit(solution)/shard_map/ppermute | solution.py:185
  112.3 3.6 %collective-permute-start.37 = (bf16[4,256,256]{2,1,0:T(8,128)(2,1)S(1)}, bf16[4,256,256]{2,1,0:T(8,128)(2,1)S(1)}, u32[]{:S(2)}, u32[]{:S(2)}) collective-permute-start(bf16[4,256,256]{2,1,0:T(8,128)(2,1)S(1)} %collective-permute-done.33.refs_1_), channel_id=1, source_target_pairs={{0,8},{8,0},{16,24},{24,16},{32,40},{40,32},{48,56},{56,48},{64,72... | collective-permute-start | bytes 1572872 | tf_op jit(solution)/shard_map/ppermute | solution.py:187
  115.8 2.5 %collective-permute-done.34.refs_2_ = bf16[4,256,256]{2,1,0:T(8,128)(2,1)S(1)} collective-permute-done((bf16[4,256,256]{2,1,0:T(8,128)(2,1)S(1)}, bf16[4,256,256]{2,1,0:T(8,128)(2,1)S(1)}, u32[]{:S(2)}, u32[]{:S(2)}) %collective-permute-start.34) | collective-permute-done | bytes 524320 | tf_op jit(solution)/shard_map/ppermute | solution.py:185
  118.3 4.6 %collective-permute-start.38 = (bf16[4,256,256]{2,1,0:T(8,128)(2,1)S(1)}, bf16[4,256,256]{2,1,0:T(8,128)(2,1)S(1)}, u32[]{:S(2)}, u32[]{:S(2)}) collective-permute-start(bf16[4,256,256]{2,1,0:T(8,128)(2,1)S(1)} %collective-permute-done.34.refs_2_), channel_id=1, source_target_pairs={{0,8},{8,0},{16,24},{24,16},{32,40},{40,32},{48,56},{56,48},{64,72... | collective-permute-start | bytes 1572872 | tf_op jit(solution)/shard_map/ppermute | solution.py:187
  122.9 1.5 %collective-permute-done.38.refs_6_ = bf16[4,256,256]{2,1,0:T(8,128)(2,1)S(1)} collective-permute-done((bf16[4,256,256]{2,1,0:T(8,128)(2,1)S(1)}, bf16[4,256,256]{2,1,0:T(8,128)(2,1)S(1)}, u32[]{:S(2)}, u32[]{:S(2)}) %collective-permute-start.38) | collective-permute-done | bytes 524320 | tf_op jit(solution)/shard_map/ppermute | solution.py:187
  124.5 0.7 collective-permute-done.39.refs_7_
  125.2 2.5 %shard_map.90 = bf16[4,4,2,256,256]{4,3,2,1,0:T(8,128)(2,1)} custom-call(bf16[4,256,256]{2,1,0:T(8,128)(2,1)S(1)} %pad_maximum_fusion.refs_0_, bf16[4,256,256]{2,1,0:T(8,128)(2,1)S(1)} %collective-permute-done.33.refs_1_, bf16[4,256,256]{2,1,0:T(8,128)(2,1)S(1)} %collective-permute-done.34.refs_2_, bf16[4,256,256]{2,1,0:T(8,128)(2,1)S(1)} %collective-permute-done.35.refs_3_, ...), custom_call_target="tpu_custom_call" | custom-call | tf_op jit(solution)/shard_map/pallas_call | solution.py:188
  (40 shorter events, 1.0 us)
Async XLA Ops:
  0.6 27.0 %all-to-all-start = ((bf16[8,128,256]{2,1,0:T(8,128)(2,1)}), bf16[8,128,256]{2,1,0:T(8,128)(2,1)S(1)}, u32[]{:S(2)}, u32[]{:S(2)}) async-start(bf16[8,128,256]{2,1,0:T(8,128)(2,1)} %bitcast.41), calls=%async_computation | async-start | bytes 1048576 | tf_op jit(solution)/shard_map/all_to_all | solution.py:133
  9.7 1.6 %copy-start = (bf16[128,8192]{1,0:T(8,128)(2,1)S(1)}, bf16[128,8192]{1,0:T(8,128)(2,1)}, u32[]{:S(2)}) copy-start(bf16[128,8192]{1,0:T(8,128)(2,1)} %acts.1) | copy-start | bytes 6291460
  11.6 6.6 %collective-permute-start.1 = (bf16[128,1024]{1,0:T(8,128)(2,1)S(1)}, bf16[128,1024]{1,0:T(8,128)(2,1)S(1)}, u32[]{:S(2)}, u32[]{:S(2)}) collective-permute-start(bf16[128,1024]{1,0:T(8,128)(2,1)S(1)} %get-tuple-element.25), channel_id=1, source_target_pairs={{0,8},{8,0},{16,24},{24,16},{32,40},{40,32},{48,56},{56,48},{64,72... | collective-permute-start | bytes 786440 | tf_op jit(solution)/shard_map/ppermute | solution.py:127
  12.6 7.0 %collective-permute-start = (bf16[128,1024]{1,0:T(8,128)(2,1)S(1)}, bf16[128,1024]{1,0:T(8,128)(2,1)S(1)}, u32[]{:S(2)}, u32[]{:S(2)}) collective-permute-start(bf16[128,1024]{1,0:T(8,128)(2,1)S(1)} %get-tuple-element.24), channel_id=1, source_target_pairs={{0,128},{8,40},{16,144},{24,56},{32,160},{40,8},{48,176},{56,24},{... | collective-permute-start | bytes 786440 | tf_op jit(solution)/shard_map/ppermute | solution.py:130
  15.5 6.9 %collective-permute-start.3 = (bf16[128,1024]{1,0:T(8,128)(2,1)S(1)}, bf16[128,1024]{1,0:T(8,128)(2,1)S(1)}, u32[]{:S(2)}, u32[]{:S(2)}) collective-permute-start(bf16[128,1024]{1,0:T(8,128)(2,1)S(1)} %get-tuple-element.26), channel_id=1, source_target_pairs={{0,64},{8,24},{16,80},{24,40},{32,96},{40,56},{48,112},{56,8},{64,... | collective-permute-start | bytes 786440 | tf_op jit(solution)/shard_map/ppermute | solution.py:130
  15.9 6.9 %collective-permute-start.4 = (bf16[128,1024]{1,0:T(8,128)(2,1)S(1)}, bf16[128,1024]{1,0:T(8,128)(2,1)S(1)}, u32[]{:S(2)}, u32[]{:S(2)}) collective-permute-start(bf16[128,1024]{1,0:T(8,128)(2,1)S(1)} %get-tuple-element.27), channel_id=1, source_target_pairs={{0,192},{8,56},{16,208},{24,8},{32,224},{40,24},{48,240},{56,40},{... | collective-permute-start | bytes 786440 | tf_op jit(solution)/shard_map/ppermute | solution.py:130
  18.2 7.0 %collective-permute-start.2 = (bf16[128,1024]{1,0:T(8,128)(2,1)S(1)}, bf16[128,1024]{1,0:T(8,128)(2,1)S(1)}, u32[]{:S(2)}, u32[]{:S(2)}) collective-permute-start(bf16[128,1024]{1,0:T(8,128)(2,1)S(1)} %collective-permute-done.1), channel_id=1, source_target_pairs={{0,128},{8,40},{16,144},{24,56},{32,160},{40,8},{48,176},{56,24},{... | collective-permute-start | bytes 786440 | tf_op jit(solution)/shard_map/ppermute | solution.py:130
  27.6 2.0 %collective-permute-start.13 = (bf16[8,128,256]{2,1,0:T(8,128)(2,1)S(1)}, bf16[8,128,256]{2,1,0:T(8,128)(2,1)S(1)}, u32[]{:S(2)}, u32[]{:S(2)}) collective-permute-start(bf16[8,128,256]{2,1,0:T(8,128)(2,1)S(1)} %all-to-all-done.refs_8_), channel_id=1, source_target_pairs={{0,8},{8,0},{16,24},{24,16},{32,40},{40,32},{48,56},{56,48},{64,72... | collective-permute-start | bytes 1572872 | tf_op jit(solution)/shard_map/ppermute | solution.py:138
  28.1 9.6 %collective-permute-start.10 = (bf16[8,128,256]{2,1,0:T(8,128)(2,1)S(1)}, bf16[8,128,256]{2,1,0:T(8,128)(2,1)S(1)}, u32[]{:S(2)}, u32[]{:S(2)}) collective-permute-start(bf16[8,128,256]{2,1,0:T(8,128)(2,1)S(1)} %all-to-all-done.refs_8_), channel_id=1, source_target_pairs={{0,64},{8,24},{16,80},{24,40},{32,96},{40,56},{48,112},{56,8},{64,... | collective-permute-start | bytes 1572872 | tf_op jit(solution)/shard_map/ppermute | solution.py:139
  29.6 8.9 %collective-permute-start.15 = (bf16[8,128,256]{2,1,0:T(8,128)(2,1)S(1)}, bf16[8,128,256]{2,1,0:T(8,128)(2,1)S(1)}, u32[]{:S(2)}, u32[]{:S(2)}) collective-permute-start(bf16[8,128,256]{2,1,0:T(8,128)(2,1)S(1)} %collective-permute-done.13.refs_12_), channel_id=1, source_target_pairs={{0,192},{8,56},{16,208},{24,8},{32,224},{40,24},{48,240},{56,40},{... | collective-permute-start | bytes 1572872 | tf_op jit(solution)/shard_map/ppermute | solution.py:141
  32.4 1.6 %collective-permute-start.6 = (bf16[128,1024]{1,0:T(8,128)(2,1)S(1)}, bf16[128,1024]{1,0:T(8,128)(2,1)S(1)}, u32[]{:S(2)}, u32[]{:S(2)}) collective-permute-start(bf16[128,1024]{1,0:T(8,128)(2,1)S(1)} %get-tuple-element.32), channel_id=1, source_target_pairs={{0,8},{8,0},{16,24},{24,16},{32,40},{40,32},{48,56},{56,48},{64,72... | collective-permute-start | bytes 786440 | tf_op jit(solution)/shard_map/ppermute | solution.py:127
  32.8 2.5 %collective-permute-start.8 = (bf16[128,1024]{1,0:T(8,128)(2,1)S(1)}, bf16[128,1024]{1,0:T(8,128)(2,1)S(1)}, u32[]{:S(2)}, u32[]{:S(2)}) collective-permute-start(bf16[128,1024]{1,0:T(8,128)(2,1)S(1)} %get-tuple-element.34), channel_id=1, source_target_pairs={{0,8},{8,0},{16,24},{24,16},{32,40},{40,32},{48,56},{56,48},{64,72... | collective-permute-start | bytes 786440 | tf_op jit(solution)/shard_map/ppermute | solution.py:127
  32.9 4.2 %collective-permute-start.5 = (bf16[128,1024]{1,0:T(8,128)(2,1)S(1)}, bf16[128,1024]{1,0:T(8,128)(2,1)S(1)}, u32[]{:S(2)}, u32[]{:S(2)}) collective-permute-start(bf16[128,1024]{1,0:T(8,128)(2,1)S(1)} %get-tuple-element.31), channel_id=1, source_target_pairs={{0,8},{8,0},{16,24},{24,16},{32,40},{40,32},{48,56},{56,48},{64,72... | collective-permute-start | bytes 786440 | tf_op jit(solution)/shard_map/ppermute | solution.py:127
  33.9 8.0 %collective-permute-start.7 = (bf16[128,1024]{1,0:T(8,128)(2,1)S(1)}, bf16[128,1024]{1,0:T(8,128)(2,1)S(1)}, u32[]{:S(2)}, u32[]{:S(2)}) collective-permute-start(bf16[128,1024]{1,0:T(8,128)(2,1)S(1)} %collective-permute-done.6), channel_id=1, source_target_pairs={{0,64},{8,24},{16,80},{24,40},{32,96},{40,56},{48,112},{56,8},{64,... | collective-permute-start | bytes 786440 | tf_op jit(solution)/shard_map/ppermute | solution.py:130
  35.2 17.3 %collective-permute-start.12 = (bf16[8,128,256]{2,1,0:T(8,128)(2,1)S(1)}, bf16[8,128,256]{2,1,0:T(8,128)(2,1)S(1)}, u32[]{:S(2)}, u32[]{:S(2)}) collective-permute-start(bf16[8,128,256]{2,1,0:T(8,128)(2,1)S(1)} %all-to-all-done.refs_8_), channel_id=1, source_target_pairs={{0,192},{8,56},{16,208},{24,8},{32,224},{40,24},{48,240},{56,40},{... | collective-permute-start | bytes 1572872 | tf_op jit(solution)/shard_map/ppermute | solution.py:139
  37.1 15.5 %collective-permute-start.14 = (bf16[8,128,256]{2,1,0:T(8,128)(2,1)S(1)}, bf16[8,128,256]{2,1,0:T(8,128)(2,1)S(1)}, u32[]{:S(2)}, u32[]{:S(2)}) collective-permute-start(bf16[8,128,256]{2,1,0:T(8,128)(2,1)S(1)} %collective-permute-done.13.refs_12_), channel_id=1, source_target_pairs={{0,64},{8,24},{16,80},{24,40},{32,96},{40,56},{48,112},{56,8},{64,... | collective-permute-start | bytes 1572872 | tf_op jit(solution)/shard_map/ppermute | solution.py:141
  37.7 14.9 %collective-permute-start.11 = (bf16[8,128,256]{2,1,0:T(8,128)(2,1)S(1)}, bf16[8,128,256]{2,1,0:T(8,128)(2,1)S(1)}, u32[]{:S(2)}, u32[]{:S(2)}) collective-permute-start(bf16[8,128,256]{2,1,0:T(8,128)(2,1)S(1)} %collective-permute-done.10.refs_9_), channel_id=1, source_target_pairs={{0,64},{8,24},{16,80},{24,40},{32,96},{40,56},{48,112},{56,8},{64,... | collective-permute-start | bytes 1572872 | tf_op jit(solution)/shard_map/ppermute | solution.py:140
  38.5 14.1 %collective-permute-start.16 = (bf16[8,128,256]{2,1,0:T(8,128)(2,1)S(1)}, bf16[8,128,256]{2,1,0:T(8,128)(2,1)S(1)}, u32[]{:S(2)}, u32[]{:S(2)}) collective-permute-start(bf16[8,128,256]{2,1,0:T(8,128)(2,1)S(1)} %collective-permute-done.15.refs_15_), channel_id=1, source_target_pairs={{0,192},{8,56},{16,208},{24,8},{32,224},{40,24},{48,240},{56,40},{... | collective-permute-start | bytes 1572872 | tf_op jit(solution)/shard_map/ppermute | solution.py:142
  41.9 10.6 %collective-permute-start.9 = (bf16[128,1024]{1,0:T(8,128)(2,1)S(1)}, bf16[128,1024]{1,0:T(8,128)(2,1)S(1)}, u32[]{:S(2)}, u32[]{:S(2)}) collective-permute-start(bf16[128,1024]{1,0:T(8,128)(2,1)S(1)} %collective-permute-done.8), channel_id=1, source_target_pairs={{0,192},{8,56},{16,208},{24,8},{32,224},{40,24},{48,240},{56,40},{... | collective-permute-start | bytes 786440 | tf_op jit(solution)/shard_map/ppermute | solution.py:130
  53.2 9.8 %collective-permute-start.20 = (bf16[3,256,256]{2,1,0:T(8,128)(2,1)S(1)}, bf16[3,256,256]{2,1,0:T(8,128)(2,1)S(1)}, u32[]{:S(2)}, u32[]{:S(2)}) collective-permute-start(bf16[3,256,256]{2,1,0:T(8,128)(2,1)S(1)} %shard_map.88), channel_id=1, source_target_pairs={{0,32},{8,136},{16,48},{24,152},{32,0},{40,168},{48,16},{56,184},{... | collective-permute-start | bytes 1179656 | tf_op jit(solution)/shard_map/ppermute | solution.py:155
  57.1 9.4 %collective-permute-start.21 = (bf16[3,256,256]{2,1,0:T(8,128)(2,1)S(1)}, bf16[3,256,256]{2,1,0:T(8,128)(2,1)S(1)}, u32[]{:S(2)}, u32[]{:S(2)}) collective-permute-start(bf16[3,256,256]{2,1,0:T(8,128)(2,1)S(1)} %get-tuple-element.40), channel_id=1, source_target_pairs={{0,16},{8,72},{16,32},{24,88},{32,48},{40,104},{48,0},{56,120},{64... | collective-permute-start | bytes 1179656 | tf_op jit(solution)/shard_map/ppermute | solution.py:155
  57.5 9.0 %collective-permute-start.22 = (bf16[3,256,256]{2,1,0:T(8,128)(2,1)S(1)}, bf16[3,256,256]{2,1,0:T(8,128)(2,1)S(1)}, u32[]{:S(2)}, u32[]{:S(2)}) collective-permute-start(bf16[3,256,256]{2,1,0:T(8,128)(2,1)S(1)} %get-tuple-element.41), channel_id=1, source_target_pairs={{0,48},{8,200},{16,0},{24,216},{32,16},{40,232},{48,32},{56,248},{... | collective-permute-start | bytes 1179656 | tf_op jit(solution)/shard_map/ppermute | solution.py:155
  60.7 12.3 %collective-permute-start.17 = (bf16[5,256,256]{2,1,0:T(8,128)(2,1)S(1)}, bf16[5,256,256]{2,1,0:T(8,128)(2,1)S(1)}, u32[]{:S(2)}, u32[]{:S(2)}) collective-permute-start(bf16[5,256,256]{2,1,0:T(8,128)(2,1)S(1)} %shard_map.86), channel_id=1, source_target_pairs={{0,32},{8,136},{16,48},{24,152},{32,0},{40,168},{48,16},{56,184},{... | collective-permute-start | bytes 1966088 | tf_op jit(solution)/shard_map/ppermute | solution.py:155
  62.4 17.6 %collective-permute-start.18 = (bf16[5,256,256]{2,1,0:T(8,128)(2,1)S(1)}, bf16[5,256,256]{2,1,0:T(8,128)(2,1)S(1)}, u32[]{:S(2)}, u32[]{:S(2)}) collective-permute-start(bf16[5,256,256]{2,1,0:T(8,128)(2,1)S(1)} %get-tuple-element.37), channel_id=1, source_target_pairs={{0,16},{8,72},{16,32},{24,88},{32,48},{40,104},{48,0},{56,120},{64... | collective-permute-start | bytes 1966088 | tf_op jit(solution)/shard_map/ppermute | solution.py:155
  63.1 17.1 %collective-permute-start.19 = (bf16[5,256,256]{2,1,0:T(8,128)(2,1)S(1)}, bf16[5,256,256]{2,1,0:T(8,128)(2,1)S(1)}, u32[]{:S(2)}, u32[]{:S(2)}) collective-permute-start(bf16[5,256,256]{2,1,0:T(8,128)(2,1)S(1)} %get-tuple-element.38), channel_id=1, source_target_pairs={{0,48},{8,200},{16,0},{24,216},{32,16},{40,232},{48,32},{56,248},{... | collective-permute-start | bytes 1966088 | tf_op jit(solution)/shard_map/ppermute | solution.py:155
  66.7 13.8 %collective-permute-start.25 = (bf16[256,256]{1,0:T(8,128)(2,1)S(1)}, bf16[256,256]{1,0:T(8,128)(2,1)S(1)}, u32[]{:S(2)}, u32[]{:S(2)}) collective-permute-start(bf16[256,256]{1,0:T(8,128)(2,1)S(1)} %get-tuple-element.54), channel_id=1, source_target_pairs={{0,1},{1,2},{2,3},{3,4},{4,5},{5,6},{6,7},{7,0},{8,9},{9,10},{10,1... | collective-permute-start | bytes 393224 | tf_op jit(solution)/shard_map/ppermute | solution.py:164
  67.1 13.5 %collective-permute-start.27 = (bf16[256,256]{1,0:T(8,128)(2,1)S(1)}, bf16[256,256]{1,0:T(8,128)(2,1)S(1)}, u32[]{:S(2)}, u32[]{:S(2)}) collective-permute-start(bf16[256,256]{1,0:T(8,128)(2,1)S(1)} %get-tuple-element.53), channel_id=1, source_target_pairs={{0,7},{1,0},{2,1},{3,2},{4,3},{5,4},{6,5},{7,6},{8,15},{9,8},{10,9... | collective-permute-start | bytes 393224 | tf_op jit(solution)/shard_map/ppermute | solution.py:164
  73.0 14.0 %collective-permute-start.23 = (bf16[256,256]{1,0:T(8,128)(2,1)S(1)}, bf16[256,256]{1,0:T(8,128)(2,1)S(1)}, u32[]{:S(2)}, u32[]{:S(2)}) collective-permute-start(bf16[256,256]{1,0:T(8,128)(2,1)S(1)} %get-tuple-element.52), channel_id=1, source_target_pairs={{0,4},{1,5},{2,6},{3,7},{4,0},{5,1},{6,2},{7,3},{8,12},{9,13},{10,... | collective-permute-start | bytes 393224 | tf_op jit(solution)/shard_map/ppermute | solution.py:164
  80.5 11.7 %copy-start.1 = (f32[256,256]{1,0:T(8,128)S(1)}, f32[256,256]{1,0:T(8,128)}, u32[]{:S(2)}) copy-start(f32[256,256]{1,0:T(8,128)} %param.7) | copy-start | bytes 786436
  80.5 11.6 %copy-start.2 = (f32[256,256]{1,0:T(8,128)S(1)}, f32[256,256]{1,0:T(8,128)}, u32[]{:S(2)}) copy-start(f32[256,256]{1,0:T(8,128)} %param.8) | copy-start | bytes 786436
  80.5 11.6 %copy-start.3 = (f32[256,256]{1,0:T(8,128)S(1)}, f32[256,256]{1,0:T(8,128)}, u32[]{:S(2)}) copy-start(f32[256,256]{1,0:T(8,128)} %param.9) | copy-start | bytes 786436
  80.6 6.5 %collective-permute-start.26 = (bf16[256,256]{1,0:T(8,128)(2,1)S(1)}, bf16[256,256]{1,0:T(8,128)(2,1)S(1)}, u32[]{:S(2)}, u32[]{:S(2)}) collective-permute-start(bf16[256,256]{1,0:T(8,128)(2,1)S(1)} %get-tuple-element.48), channel_id=1, source_target_pairs={{0,2},{1,3},{2,4},{3,5},{4,6},{5,7},{6,0},{7,1},{8,10},{9,11},{10,... | collective-permute-start | bytes 393224 | tf_op jit(solution)/shard_map/ppermute | solution.py:164
  82.0 9.0 %collective-permute-start.28 = (bf16[256,256]{1,0:T(8,128)(2,1)S(1)}, bf16[256,256]{1,0:T(8,128)(2,1)S(1)}, u32[]{:S(2)}, u32[]{:S(2)}) collective-permute-start(bf16[256,256]{1,0:T(8,128)(2,1)S(1)} %get-tuple-element.49), channel_id=1, source_target_pairs={{0,6},{1,7},{2,0},{3,1},{4,2},{5,3},{6,4},{7,5},{8,14},{9,15},{10,... | collective-permute-start | bytes 393224 | tf_op jit(solution)/shard_map/ppermute | solution.py:164
  84.3 7.8 %collective-permute-start.24 = (bf16[256,256]{1,0:T(8,128)(2,1)S(1)}, bf16[256,256]{1,0:T(8,128)(2,1)S(1)}, u32[]{:S(2)}, u32[]{:S(2)}) collective-permute-start(bf16[256,256]{1,0:T(8,128)(2,1)S(1)} %get-tuple-element.50), channel_id=1, source_target_pairs={{0,1},{1,2},{2,3},{3,4},{4,5},{5,6},{6,7},{7,0},{8,9},{9,10},{10,1... | collective-permute-start | bytes 393224 | tf_op jit(solution)/shard_map/ppermute | solution.py:164
  84.7 7.4 %collective-permute-start.29 = (bf16[256,256]{1,0:T(8,128)(2,1)S(1)}, bf16[256,256]{1,0:T(8,128)(2,1)S(1)}, u32[]{:S(2)}, u32[]{:S(2)}) collective-permute-start(bf16[256,256]{1,0:T(8,128)(2,1)S(1)} %get-tuple-element.51), channel_id=1, source_target_pairs={{0,7},{1,0},{2,1},{3,2},{4,3},{5,4},{6,5},{7,6},{8,15},{9,8},{10,9... | collective-permute-start | bytes 393224 | tf_op jit(solution)/shard_map/ppermute | solution.py:164
  93.2 6.4 %collective-permute-start.30 = (bf16[256,256]{1,0:T(8,128)(2,1)S(1)}, bf16[256,256]{1,0:T(8,128)(2,1)S(1)}, u32[]{:S(2)}, u32[]{:S(2)}) collective-permute-start(bf16[256,256]{1,0:T(8,128)(2,1)S(1)} %get-tuple-element.42), channel_id=1, source_target_pairs={{0,64},{8,24},{16,80},{24,40},{32,96},{40,56},{48,112},{56,8},{64,... | collective-permute-start | bytes 393224 | tf_op jit(solution)/shard_map/ppermute | solution.py:183
  93.3 9.3 %collective-permute-start.31 = (bf16[256,256]{1,0:T(8,128)(2,1)S(1)}, bf16[256,256]{1,0:T(8,128)(2,1)S(1)}, u32[]{:S(2)}, u32[]{:S(2)}) collective-permute-start(bf16[256,256]{1,0:T(8,128)(2,1)S(1)} %get-tuple-element.42), channel_id=1, source_target_pairs={{0,128},{8,40},{16,144},{24,56},{32,160},{40,8},{48,176},{56,24},{... | collective-permute-start | bytes 393224 | tf_op jit(solution)/shard_map/ppermute | solution.py:183
  98.5 4.1 %collective-permute-start.32 = (bf16[256,256]{1,0:T(8,128)(2,1)S(1)}, bf16[256,256]{1,0:T(8,128)(2,1)S(1)}, u32[]{:S(2)}, u32[]{:S(2)}) collective-permute-start(bf16[256,256]{1,0:T(8,128)(2,1)S(1)} %get-tuple-element.42), channel_id=1, source_target_pairs={{0,192},{8,56},{16,208},{24,8},{32,224},{40,24},{48,240},{56,40},{... | collective-permute-start | bytes 393224 | tf_op jit(solution)/shard_map/ppermute | solution.py:183
  102.7 9.6 %collective-permute-start.33 = (bf16[4,256,256]{2,1,0:T(8,128)(2,1)S(1)}, bf16[4,256,256]{2,1,0:T(8,128)(2,1)S(1)}, u32[]{:S(2)}, u32[]{:S(2)}) collective-permute-start(bf16[4,256,256]{2,1,0:T(8,128)(2,1)S(1)} %pad_maximum_fusion.refs_0_), channel_id=1, source_target_pairs={{0,16},{8,72},{16,32},{24,88},{32,48},{40,104},{48,0},{56,120},{64... | collective-permute-start | bytes 1572872 | tf_op jit(solution)/shard_map/ppermute | solution.py:185
  104.3 14.1 %collective-permute-start.34 = (bf16[4,256,256]{2,1,0:T(8,128)(2,1)S(1)}, bf16[4,256,256]{2,1,0:T(8,128)(2,1)S(1)}, u32[]{:S(2)}, u32[]{:S(2)}) collective-permute-start(bf16[4,256,256]{2,1,0:T(8,128)(2,1)S(1)} %pad_maximum_fusion.refs_0_), channel_id=1, source_target_pairs={{0,32},{8,136},{16,48},{24,152},{32,0},{40,168},{48,16},{56,184},{... | collective-permute-start | bytes 1572872 | tf_op jit(solution)/shard_map/ppermute | solution.py:185
  106.0 17.0 %collective-permute-start.35 = (bf16[4,256,256]{2,1,0:T(8,128)(2,1)S(1)}, bf16[4,256,256]{2,1,0:T(8,128)(2,1)S(1)}, u32[]{:S(2)}, u32[]{:S(2)}) collective-permute-start(bf16[4,256,256]{2,1,0:T(8,128)(2,1)S(1)} %pad_maximum_fusion.refs_0_), channel_id=1, source_target_pairs={{0,48},{8,200},{16,0},{24,216},{32,16},{40,232},{48,32},{56,248},{... | collective-permute-start | bytes 1572872 | tf_op jit(solution)/shard_map/ppermute | solution.py:185
  107.9 15.0 %collective-permute-start.36 = (bf16[4,256,256]{2,1,0:T(8,128)(2,1)S(1)}, bf16[4,256,256]{2,1,0:T(8,128)(2,1)S(1)}, u32[]{:S(2)}, u32[]{:S(2)}) collective-permute-start(bf16[4,256,256]{2,1,0:T(8,128)(2,1)S(1)} %pad_maximum_fusion.refs_0_), channel_id=1, source_target_pairs={{0,8},{8,0},{16,24},{24,16},{32,40},{40,32},{48,56},{56,48},{64,72... | collective-permute-start | bytes 1572872 | tf_op jit(solution)/shard_map/ppermute | solution.py:187
  112.3 10.7 %collective-permute-start.37 = (bf16[4,256,256]{2,1,0:T(8,128)(2,1)S(1)}, bf16[4,256,256]{2,1,0:T(8,128)(2,1)S(1)}, u32[]{:S(2)}, u32[]{:S(2)}) collective-permute-start(bf16[4,256,256]{2,1,0:T(8,128)(2,1)S(1)} %collective-permute-done.33.refs_1_), channel_id=1, source_target_pairs={{0,8},{8,0},{16,24},{24,16},{32,40},{40,32},{48,56},{56,48},{64,72... | collective-permute-start | bytes 1572872 | tf_op jit(solution)/shard_map/ppermute | solution.py:187
  118.3 6.1 %collective-permute-start.38 = (bf16[4,256,256]{2,1,0:T(8,128)(2,1)S(1)}, bf16[4,256,256]{2,1,0:T(8,128)(2,1)S(1)}, u32[]{:S(2)}, u32[]{:S(2)}) collective-permute-start(bf16[4,256,256]{2,1,0:T(8,128)(2,1)S(1)} %collective-permute-done.34.refs_2_), channel_id=1, source_target_pairs={{0,8},{8,0},{16,24},{24,16},{32,40},{40,32},{48,56},{56,48},{64,72... | collective-permute-start | bytes 1572872 | tf_op jit(solution)/shard_map/ppermute | solution.py:187
  122.9 2.3 %collective-permute-start.39 = (bf16[4,256,256]{2,1,0:T(8,128)(2,1)S(1)}, bf16[4,256,256]{2,1,0:T(8,128)(2,1)S(1)}, u32[]{:S(2)}, u32[]{:S(2)}) collective-permute-start(bf16[4,256,256]{2,1,0:T(8,128)(2,1)S(1)} %collective-permute-done.35.refs_3_), channel_id=1, source_target_pairs={{0,8},{8,0},{16,24},{24,16},{32,40},{40,32},{48,56},{56,48},{64,72... | collective-permute-start | bytes 1572872 | tf_op jit(solution)/shard_map/ppermute | solution.py:187
